TPU v7x, 32 devices: a whole 2x2x4 slice. The times are simulated.
32 devices in a mesh: rep: 2 (over core), batch: 4 (over z), ctx: 4 (over y, x).
Axes of the slice: x: 2, y: 2, z: 4, core: 2. Of those that a mesh axis runs over, the one named last changes fastest.
Arguments:
- tokens: bfloat16 [8, 2304, 1024], P(('rep', 'batch'), 'ctx'), may hold values from -6 to 6
- cotangent: bfloat16 [8, 2304, 1024], P(('rep', 'batch'), 'ctx'), may hold values from -6 to 6
- segment_ids: int32 [8, 2304], P(('rep', 'batch')), may hold values from 0 to 3, never falling along the last dimension, each value on 1 to 1152 neighbouring positions
- first_gain: bfloat16 [1024], P('ctx'), may hold values from 0.099609375 to 1.8984375
- first_shift: bfloat16 [1024], P('ctx'), may hold values from -1.1953125 to 1.1953125
- second_gain: bfloat16 [1024], P('ctx'), may hold values from 0.099609375 to 1.8984375
- second_shift: bfloat16 [1024], P('ctx'), may hold values from -1.1953125 to 1.1953125
- final_gain: bfloat16 [1024], P('ctx'), may hold values from 0.099609375 to 1.8984375
- final_shift: bfloat16 [1024], P('ctx'), may hold values from -1.1953125 to 1.1953125
- project_weight: bfloat16 [1024, 3072], P('ctx'), may hold values from -0.1875 to 0.1875
- output_weight: bfloat16 [1024, 1024], P('ctx'), may hold values from -0.75 to 0.75
- upward_weight: bfloat16 [1024, 4096], P('ctx'), may hold values from -0.1875 to 0.1875
- downward_weight: bfloat16 [4096, 1024], P('ctx'), may hold values from -0.09375 to 0.09375
- store_keys: bfloat16 [32768, 1024], P(('batch', 'ctx')), may hold values from -6 to 6
- store_values: int32 [32768], P(('batch', 'ctx')), may hold values from 0 to 267743, as said below
- owners: int32 [8, 2304, 4], P(('rep', 'batch'), 'ctx'), may hold values from 0 to 15, all different within a row; in each aligned block of 576 rows (0 to 575, 576 to 1151, ..., all dimensions but the last counted through in order) at most 288 rows name the same one
- neighbours: int32 [2, 16, 16, 288, 256], P('rep', ('batch', 'ctx')), may hold values from 0 to 2047, as said below
- targets: int32 [8, 2304], P(('rep', 'batch'), 'ctx'), may hold values from 0 to 267743, as said below
- model_prob: float32 [8, 2304], P(('rep', 'batch'), 'ctx'), may hold values from 0.05 to 0.5
Outputs:
- hidden_out: bfloat16 [8, 2304, 1024], P(('rep', 'batch'), 'ctx')
- losses: float32 [8, 2304], P(('rep', 'batch'), 'ctx')
- query_grad: float32 [8, 2304, 1024], P(('rep', 'batch'), 'ctx')
- input_grad: float32 [8, 2304, 1024], P(('rep', 'batch'), 'ctx')
- project_grad: float32 [1024, 3072], P('ctx')
- output_grad: float32 [1024, 1024], P('ctx')
- upward_grad: float32 [1024, 4096], P('ctx')
- downward_grad: float32 [4096, 1024], P('ctx')
- first_gain_grad: float32 [1024], P('ctx')
- first_shift_grad: float32 [1024], P('ctx')
- second_gain_grad: float32 [1024], P('ctx')
- second_shift_grad: float32 [1024], P('ctx')
- final_gain_grad: float32 [1024], P('ctx')
- final_shift_grad: float32 [1024], P('ctx')
Inputs may be any that keep to these rules, and one draw needn't show every extreme that they name: Each token names 4 different owners; in each aligned block of 576 positions of a sequence (the positions of one sequence on one device) no owner is named by more than 288 tokens. Entry [r, o, s, c, n] is the n-th neighbour, an index among owner o's 2048 keys, of the c-th request that device s of replica r sends to owner o, its requests counted in order of sequence, position and owner rank. The 256 neighbours of a slot are different, the n-th among keys n * 8 to (n + 1) * 8 - 1. Slots that no request fills hold unused indices. `store_values`: word ids; about half of them are four frequent words, the same four for the targets. `targets`: word ids; about half of them are four frequent words, the same four for the datastore's values.
All inputs are finite; a program needn't handle non-finite values.
Results may differ from a plain program's by a relative error of at most 0.02.
Values may be sent and summed in bfloat16 or wider, within the bound.
No kernel may reach another device: no remote copies, remote signals or barrier semaphores. Data moves between devices by JAX's collectives and lax.ppermute only.
A program may use at most 512 MiB of HBM per device.

v0:
```python
import jax
import jax.numpy as jnp
from jax import lax
from jax.sharding import PartitionSpec as P

HEADS = 16


norm_eps = 1e-05
mix_weight = 0.25
masked_value = -1e30


def norm_rows(values, scale_gain, shift_term):
    average = jnp.mean(values, axis=-1, keepdims=True)
    centred = values - average
    spread = jnp.mean(centred * centred, axis=-1, keepdims=True)
    return centred * lax.rsqrt(spread + norm_eps) * scale_gain + shift_term


def row_dot(left_side, right_side):
    return jnp.dot(left_side, right_side, preferred_element_type=jnp.float32)


def left_dot(left_side, right_side):
    return lax.dot_general(
        left_side, right_side, (((0,), (0,)), ((), ())), preferred_element_type=jnp.float32
    )


def right_dot(left_side, right_side):
    return lax.dot_general(
        left_side, right_side, (((1,), (1,)), ((), ())), preferred_element_type=jnp.float32
    )


def allowed_mask(query_pos, key_pos, query_seg, key_seg):
    return (key_pos[None, :] <= query_pos[:, None]) & (key_seg[None, :] == query_seg[:, None])


def split_heads(values, head_count):
    return values.reshape(values.shape[0], head_count, values.shape[1] // head_count)


def attend(query_one, keys_one, values_one, allowed, head_count):
    score_scale = (query_one.shape[1] // head_count) ** (-0.5)
    raw_scores = (
        jnp.einsum(
            "qhd,khd->hqk",
            split_heads(query_one, head_count),
            split_heads(keys_one, head_count),
            preferred_element_type=jnp.float32,
        )
        * score_scale
    )
    raw_scores = jnp.where(allowed[None], raw_scores, masked_value)
    row_peak = jnp.max(raw_scores, axis=-1, keepdims=True)
    exp_scores = jnp.exp(raw_scores - row_peak)
    row_total = jnp.sum(exp_scores, axis=-1, keepdims=True)
    weights_low = (exp_scores / row_total).astype(jnp.bfloat16)
    attended = jnp.einsum(
        "hqk,khd->qhd",
        weights_low,
        split_heads(values_one, head_count),
        preferred_element_type=jnp.float32,
    )
    return (
        attended.reshape(query_one.shape).astype(jnp.bfloat16),
        (row_peak + jnp.log(row_total))[..., 0],
    )


def score_parts(query_one, keys_one, values_one, grad_one, lse_one, allowed, head_count):
    score_scale = (query_one.shape[1] // head_count) ** (-0.5)
    raw_scores = (
        jnp.einsum(
            "qhd,khd->hqk",
            split_heads(query_one, head_count),
            split_heads(keys_one, head_count),
            preferred_element_type=jnp.float32,
        )
        * score_scale
    )
    raw_scores = jnp.where(allowed[None], raw_scores, masked_value)
    weights_full = jnp.exp(raw_scores - lse_one[..., None])
    weight_grad = jnp.einsum(
        "qhd,khd->hqk",
        split_heads(grad_one, head_count),
        split_heads(values_one, head_count),
        preferred_element_type=jnp.float32,
    )
    return (weights_full, weight_grad, score_scale)


def local(
    tokens,
    cotangent,
    segment_ids,
    first_gain,
    first_shift,
    second_gain,
    second_shift,
    final_gain,
    final_shift,
    project_weight,
    output_weight,
    upward_weight,
    downward_weight,
    store_keys,
    store_values,
    owners,
    neighbours,
    targets,
    model_prob,
):
    head_count = HEADS
    group_seqs, block_len, width = tokens.shape
    seq_len = segment_ids.shape[1]
    shard_count = lax.axis_size("batch") * lax.axis_size("ctx")
    capacity = neighbours.shape[3]
    near_count = neighbours.shape[4]
    top_count = owners.shape[2]
    key_count = store_keys.shape[0]
    spacing = key_count // near_count
    slot_rows = shard_count * capacity
    dist_scale = width ** (-0.5)
    gathered = (
        lax.all_gather(project_weight, "ctx", axis=0, tiled=True),
        lax.all_gather(output_weight, "ctx", axis=0, tiled=True),
        lax.all_gather(upward_weight, "ctx", axis=0, tiled=True),
        lax.all_gather(downward_weight, "ctx", axis=0, tiled=True),
        lax.all_gather(first_gain, "ctx", axis=0, tiled=True),
        lax.all_gather(first_shift, "ctx", axis=0, tiled=True),
        lax.all_gather(second_gain, "ctx", axis=0, tiled=True),
        lax.all_gather(second_shift, "ctx", axis=0, tiled=True),
        lax.all_gather(final_gain, "ctx", axis=0, tiled=True),
        lax.all_gather(final_shift, "ctx", axis=0, tiled=True),
    )
    proj_full, out_full, up_full, down_full = (gathered[0], gathered[1], gathered[2], gathered[3])
    gain_list = [vector.astype(jnp.float32) for vector in gathered[4:]]
    offset = lax.axis_index("ctx") * block_len
    positions = jnp.arange(seq_len, dtype=jnp.int32)
    query_pos = offset + jnp.arange(block_len, dtype=jnp.int32)
    query_seg = lax.dynamic_slice_in_dim(segment_ids, offset, block_len, 1)
    inputs = tokens.astype(jnp.float32).reshape(-1, width)
    normed_one = norm_rows(inputs, gain_list[0], gain_list[1]).astype(jnp.bfloat16)
    projected = (
        row_dot(normed_one, proj_full)
        .astype(jnp.bfloat16)
        .reshape(group_seqs, block_len, 3 * width)
    )
    query_rows = projected[..., :width]
    key_rows = projected[..., width : 2 * width]
    value_rows = projected[..., 2 * width :]
    context_keys, context_values = (
        lax.all_gather(key_rows, "ctx", axis=1, tiled=True),
        lax.all_gather(value_rows, "ctx", axis=1, tiled=True),
    )

    def forward_one(operands):
        query_one, keys_one, values_one, seg_one, qseg_one = operands
        allowed = allowed_mask(query_pos, positions, qseg_one, seg_one)
        return attend(query_one, keys_one, values_one, allowed, head_count)

    attended, log_total = lax.map(
        forward_one, (query_rows, context_keys, context_values, segment_ids, query_seg)
    )
    hidden = inputs + row_dot(attended.reshape(-1, width), out_full)
    normed_two = norm_rows(hidden, gain_list[2], gain_list[3]).astype(jnp.bfloat16)
    upper_rows = row_dot(normed_two, up_full)
    active = jax.nn.gelu(upper_rows).astype(jnp.bfloat16)
    summed = hidden + row_dot(active, down_full)
    final_rows = norm_rows(summed, gain_list[4], gain_list[5]).astype(jnp.bfloat16)
    owner_flat = owners.reshape(-1)
    onehot = (owner_flat[:, None] == jnp.arange(shard_count, dtype=jnp.int32)[None, :]).astype(
        jnp.int32
    )
    running = jnp.cumsum(onehot, axis=0) - jnp.int32(1)
    slots = jnp.sum(running * onehot, axis=1)
    bucket_index = owner_flat * capacity + slots
    send_queries = (
        jnp.zeros((slot_rows, width), jnp.bfloat16)
        .at[bucket_index]
        .set(jnp.repeat(final_rows, top_count, axis=0))
        .reshape(shard_count, capacity, width)
    )
    send_targets = (
        jnp.zeros((slot_rows,), jnp.int32)
        .at[bucket_index]
        .set(jnp.repeat(targets.reshape(-1), top_count))
        .reshape(shard_count, capacity)
    )
    got_targets = lax.all_to_all(
        send_targets, ("batch", "ctx"), split_axis=0, concat_axis=0, tiled=True
    )
    got_queries = lax.all_to_all(
        send_queries, ("batch", "ctx"), split_axis=0, concat_axis=0, tiled=True
    ).reshape(slot_rows, width)
    near_table = neighbours.reshape(slot_rows, near_count)
    within = near_table - spacing * jnp.arange(near_count, dtype=jnp.int32)[None, :]
    picker = within[:, :, None] == jnp.arange(spacing, dtype=jnp.int32)[None, None, :]
    inner_dots = right_dot(got_queries, store_keys).reshape(slot_rows, near_count, spacing)
    key_square = jnp.sum(jnp.square(store_keys.astype(jnp.float32)), axis=1).reshape(
        1, near_count, spacing
    )
    zero_float = jnp.zeros((), jnp.float32)
    picked = jnp.sum(jnp.where(picker, inner_dots, zero_float), axis=2)
    square_near = jnp.sum(jnp.where(picker, key_square, zero_float), axis=2)
    near_scores = (2.0 * picked - square_near) * dist_scale
    value_hits = store_values.reshape(1, near_count, spacing) == got_targets.reshape(
        slot_rows, 1, 1
    )
    matched = jnp.any(picker & value_hits, axis=2)
    local_peak = jnp.max(near_scores, axis=1)
    near_exp = jnp.exp(near_scores - local_peak[:, None])
    local_total = jnp.sum(near_exp, axis=1)
    local_hits = jnp.sum(jnp.where(matched, near_exp, zero_float), axis=1)
    replies = (
        lax.all_to_all(
            local_peak.reshape(shard_count, capacity),
            ("batch", "ctx"),
            split_axis=0,
            concat_axis=0,
            tiled=True,
        ),
        lax.all_to_all(
            local_total.reshape(shard_count, capacity),
            ("batch", "ctx"),
            split_axis=0,
            concat_axis=0,
            tiled=True,
        ),
        lax.all_to_all(
            local_hits.reshape(shard_count, capacity),
            ("batch", "ctx"),
            split_axis=0,
            concat_axis=0,
            tiled=True,
        ),
    )
    peak_req = replies[0].reshape(-1)[bucket_index].reshape(-1, top_count)
    total_req = replies[1].reshape(-1)[bucket_index].reshape(-1, top_count)
    hits_req = replies[2].reshape(-1)[bucket_index].reshape(-1, top_count)
    best_peak = jnp.max(peak_req, axis=1, keepdims=True)
    rescale = jnp.exp(peak_req - best_peak)
    knn_total = jnp.sum(total_req * rescale, axis=1)
    knn_prob = jnp.sum(hits_req * rescale, axis=1) / knn_total
    mixture = mix_weight * knn_prob + (1.0 - mix_weight) * model_prob.reshape(-1)
    token_loss = -jnp.log(mixture)
    coefficient = (-mix_weight / (mixture * knn_total))[:, None] * rescale
    send_coeff = (
        jnp.zeros((slot_rows,), jnp.float32)
        .at[bucket_index]
        .set(coefficient.reshape(-1))
        .reshape(shard_count, capacity)
    )
    send_prob = (
        jnp.zeros((slot_rows,), jnp.float32)
        .at[bucket_index]
        .set(jnp.repeat(knn_prob, top_count))
        .reshape(shard_count, capacity)
    )
    got_coeff, got_prob = (
        lax.all_to_all(send_coeff, ("batch", "ctx"), split_axis=0, concat_axis=0, tiled=True),
        lax.all_to_all(send_prob, ("batch", "ctx"), split_axis=0, concat_axis=0, tiled=True),
    )
    near_grad = (
        got_coeff.reshape(slot_rows, 1)
        * (matched.astype(jnp.float32) - got_prob.reshape(slot_rows, 1))
        * near_exp
        * (2.0 * dist_scale)
    ).astype(jnp.bfloat16)
    dense_grad = jnp.where(picker, near_grad[:, :, None], jnp.zeros((), jnp.bfloat16)).reshape(
        slot_rows, key_count
    )
    partial_grad = row_dot(dense_grad, store_keys).reshape(shard_count, capacity, width)
    returned = (
        lax.all_to_all(
            partial_grad.astype(jnp.bfloat16),
            ("batch", "ctx"),
            split_axis=0,
            concat_axis=0,
            tiled=True,
        )
        .astype(partial_grad.dtype)
        .reshape(slot_rows, width)
    )
    query_grad = jnp.sum(returned[bucket_index].reshape(-1, top_count, width), axis=1)
    out_grad = cotangent.reshape(-1, width).astype(jnp.float32) + query_grad
    final_vjp = jax.vjp(norm_rows, summed, gain_list[4], gain_list[5])[1]
    summed_grad, final_gain_grad, final_shift_grad = final_vjp(out_grad)
    branch_grad = summed_grad.astype(jnp.bfloat16)
    downward_grad = left_dot(active, branch_grad)
    active_grad = right_dot(branch_grad, down_full)
    gelu_vjp = jax.vjp(jax.nn.gelu, upper_rows)[1]
    upper_grad = gelu_vjp(active_grad)[0].astype(jnp.bfloat16)
    upward_grad = left_dot(normed_two, upper_grad)
    second_vjp = jax.vjp(norm_rows, hidden, gain_list[2], gain_list[3])[1]
    hidden_part, second_gain_grad, second_shift_grad = second_vjp(right_dot(upper_grad, up_full))
    hidden_grad = summed_grad + hidden_part
    attn_grad = hidden_grad.astype(jnp.bfloat16)
    output_grad = left_dot(attended.reshape(-1, width), attn_grad)
    attended_grad = (
        right_dot(attn_grad, out_full).astype(jnp.bfloat16).reshape(group_seqs, block_len, width)
    )

    def every_key(operands):
        query_one, keys_one, values_one, seg_one, qseg_one, lse_one, grad_one = operands
        allowed = allowed_mask(query_pos, positions, qseg_one, seg_one)
        weights_full, weight_grad, score_scale = score_parts(
            query_one, keys_one, values_one, grad_one, lse_one, allowed, head_count
        )
        row_dots = jnp.sum(weights_full * weight_grad, axis=-1)
        score_grad = (weights_full * (weight_grad - row_dots[..., None]) * score_scale).astype(
            jnp.bfloat16
        )
        query_part = jnp.einsum(
            "hqk,khd->qhd",
            score_grad,
            split_heads(keys_one, head_count),
            preferred_element_type=jnp.float32,
        ).reshape(query_one.shape)
        key_part = jnp.einsum(
            "hqk,qhd->khd",
            score_grad,
            split_heads(query_one, head_count),
            preferred_element_type=jnp.float32,
        ).reshape(keys_one.shape)
        value_part = jnp.einsum(
            "hqk,qhd->khd",
            weights_full.astype(jnp.bfloat16),
            split_heads(grad_one, head_count),
            preferred_element_type=jnp.float32,
        ).reshape(keys_one.shape)
        return (query_part, jnp.concatenate([key_part, value_part], axis=1))

    query_part, key_value_terms = lax.map(
        every_key,
        (
            query_rows,
            context_keys,
            context_values,
            segment_ids,
            query_seg,
            log_total,
            attended_grad,
        ),
    )
    key_value_grad = lax.psum_scatter(
        key_value_terms.astype(jnp.bfloat16), "ctx", scatter_dimension=1, tiled=True
    ).astype(jnp.float32)
    proj_grad = (
        jnp.concatenate([query_part, key_value_grad], axis=2)
        .astype(jnp.bfloat16)
        .reshape(-1, 3 * width)
    )
    project_grad = left_dot(normed_one, proj_grad)
    first_vjp = jax.vjp(norm_rows, inputs, gain_list[0], gain_list[1])[1]
    input_part, first_gain_grad, first_shift_grad = first_vjp(right_dot(proj_grad, proj_full))
    input_grad = hidden_grad + input_part
    shard_grads = (
        lax.psum_scatter(
            project_grad.astype(jnp.bfloat16), "ctx", scatter_dimension=0, tiled=True
        ).astype(jnp.float32),
        lax.psum_scatter(
            output_grad.astype(jnp.bfloat16), "ctx", scatter_dimension=0, tiled=True
        ).astype(jnp.float32),
        lax.psum_scatter(
            upward_grad.astype(jnp.bfloat16), "ctx", scatter_dimension=0, tiled=True
        ).astype(jnp.float32),
        lax.psum_scatter(
            downward_grad.astype(jnp.bfloat16), "ctx", scatter_dimension=0, tiled=True
        ).astype(jnp.float32),
        lax.psum_scatter(
            first_gain_grad.astype(jnp.bfloat16), "ctx", scatter_dimension=0, tiled=True
        ).astype(jnp.float32),
        lax.psum_scatter(
            first_shift_grad.astype(jnp.bfloat16), "ctx", scatter_dimension=0, tiled=True
        ).astype(jnp.float32),
        lax.psum_scatter(
            second_gain_grad.astype(jnp.bfloat16), "ctx", scatter_dimension=0, tiled=True
        ).astype(jnp.float32),
        lax.psum_scatter(
            second_shift_grad.astype(jnp.bfloat16), "ctx", scatter_dimension=0, tiled=True
        ).astype(jnp.float32),
        lax.psum_scatter(
            final_gain_grad.astype(jnp.bfloat16), "ctx", scatter_dimension=0, tiled=True
        ).astype(jnp.float32),
        lax.psum_scatter(
            final_shift_grad.astype(jnp.bfloat16), "ctx", scatter_dimension=0, tiled=True
        ).astype(jnp.float32),
    )
    total_grads = (
        lax.psum(shard_grads[0].astype(jnp.bfloat16), ("rep", "batch")).astype(jnp.float32),
        lax.psum(shard_grads[1].astype(jnp.bfloat16), ("rep", "batch")).astype(jnp.float32),
        lax.psum(shard_grads[2].astype(jnp.bfloat16), ("rep", "batch")).astype(jnp.float32),
        lax.psum(shard_grads[3].astype(jnp.bfloat16), ("rep", "batch")).astype(jnp.float32),
        lax.psum(shard_grads[4].astype(jnp.bfloat16), ("rep", "batch")).astype(jnp.float32),
        lax.psum(shard_grads[5].astype(jnp.bfloat16), ("rep", "batch")).astype(jnp.float32),
        lax.psum(shard_grads[6].astype(jnp.bfloat16), ("rep", "batch")).astype(jnp.float32),
        lax.psum(shard_grads[7].astype(jnp.bfloat16), ("rep", "batch")).astype(jnp.float32),
        lax.psum(shard_grads[8].astype(jnp.bfloat16), ("rep", "batch")).astype(jnp.float32),
        lax.psum(shard_grads[9].astype(jnp.bfloat16), ("rep", "batch")).astype(jnp.float32),
    )
    return (
        final_rows.reshape(group_seqs, block_len, width),
        token_loss.reshape(group_seqs, block_len),
        query_grad.reshape(group_seqs, block_len, width),
        input_grad.reshape(group_seqs, block_len, width),
        total_grads[0],
        total_grads[1],
        total_grads[2],
        total_grads[3],
        total_grads[4],
        total_grads[5],
        total_grads[6],
        total_grads[7],
        total_grads[8],
        total_grads[9],
    )


def solution(mesh):
    placed = (
        P(("rep", "batch"), "ctx", None),
        P(("rep", "batch"), "ctx", None),
        P(("rep", "batch"), None),
        P("ctx"),
        P("ctx"),
        P("ctx"),
        P("ctx"),
        P("ctx"),
        P("ctx"),
        P("ctx", None),
        P("ctx", None),
        P("ctx", None),
        P("ctx", None),
        P(("batch", "ctx"), None),
        P(("batch", "ctx")),
        P(("rep", "batch"), "ctx", None),
        P("rep", ("batch", "ctx"), None, None, None),
        P(("rep", "batch"), "ctx"),
        P(("rep", "batch"), "ctx"),
    )
    return jax.shard_map(
        local,
        mesh=mesh,
        in_specs=placed,
        out_specs=(
            P(("rep", "batch"), "ctx", None),
            P(("rep", "batch"), "ctx"),
            P(("rep", "batch"), "ctx", None),
            P(("rep", "batch"), "ctx", None),
            P("ctx", None),
            P("ctx", None),
            P("ctx", None),
            P("ctx", None),
            P("ctx"),
            P("ctx"),
            P("ctx"),
            P("ctx"),
            P("ctx"),
            P("ctx"),
        ),
        check_vma=False,
    )
```

profile of v0, /device:TPU:0, one launch (start us, length us, event | category | flops | bytes accessed | tf_op | source)
XLA Modules:
  0.0 2121.5 jit_solution(2219111252475890050)
XLA Ops:
  9.3 9.5 all-gather.1
  30.7 52.0 %all-gather.13.cloned.1.call-done = bf16[1024,3072]{1,0:T(8,128)(2,1)} async-done(((bf16[256,3072]{1,0:T(8,128)(2,1)}), bf16[1024,3072]{1,0:T(8,128)(2,1)}) %all-gather.13.cloned.1.call-update) | async-done | bytes 6291472 | tf_op jit(solution)/shard_map/all_gather | solution.py:128
  100.5 9.0 scatter_custom_fusion
  161.2 32.8 %fusion.94 = (f32[16,576]{1,0:T(8,128)S(1)}, f32[16,576,2304]{2,1,0:T(8,128)}) fusion(bf16[576,16,64]{0,2,1:T(8,128)(2,1)S(1)} %bitcast.156, bf16[2304,16,64]{0,2,1:T(8,128)(2,1)} %bitcast.149, pred[576,2304]{1,0:T(8,128)(4,1)S(1)} %fusion.37), kind=kOutput, calls=%fused_computation.166 | convolution fusion | flops 2781600768 | bytes 92196864 | tf_op jit(solution)/shard_map/while/body/eval_jaxpr/qhd,khd->hqk/dot_general | solution.py:48
  194.0 27.0 %fusion.4 = f32[16,576]{1,0:T(8,128)S(1)} fusion(f32[16,576,2304]{2,1,0:T(8,128)} %get-tuple-element.122, f32[16,576]{1,0:T(8,128)S(1)} %get-tuple-element.121), kind=kLoop, calls=%fused_computation.16 | loop fusion | flops 42458112 | bytes 85008384 | tf_op jit(solution)/shard_map/while/body/eval_jaxpr/reduce_sum | solution.py:59
  227.8 31.4 %fusion.61 = bf16[16,64,576]{2,1,0:T(8,128)(2,1)} fusion(bf16[2304,16,64]{0,2,1:T(8,128)(2,1)} %bitcast.146, f32[16,576,2304]{2,1,0:T(8,128)} %get-tuple-element.122, f32[16,576]{1,0:T(8,128)S(1)} %fusion.4, f32[16,576]{1,0:T(8,128)S(1)} %get-tuple-element.121), kind=kOutput, calls=%fused_computation.101 | convolution fusion | flops 2782199808 | bytes 90906624 | tf_op jit(solution)/shard_map/while/body/eval_jaxpr/hqk,khd->qhd/dot_general | solution.py:61
  263.2 71.8 %all-gather.21.cloned.1.call-done = bf16[1024,4096]{1,0:T(8,128)(2,1)} async-done(((bf16[256,4096]{1,0:T(8,128)(2,1)}), bf16[1024,4096]{1,0:T(8,128)(2,1)}) %all-gather.21.cloned.1.call-update) | async-done | bytes 8388624 | tf_op jit(solution)/shard_map/all_gather | solution.py:130
  335.1 11.6 fusion.88
  346.8 77.7 %all-gather.23.cloned.1.call-done = bf16[4096,1024]{1,0:T(8,128)(2,1)} async-done(((bf16[1024,1024]{1,0:T(8,128)(2,1)}), bf16[4096,1024]{1,0:T(8,128)(2,1)}) %all-gather.23.cloned.1.call-update) | async-done | bytes 8388624 | tf_op jit(solution)/shard_map/all_gather | solution.py:131
  424.4 11.9 fusion.96
  449.6 19.5 scatter_custom_fusion.1
  492.6 12.3 fusion.12
  504.9 147.9 %all-to-all-done.1 = bf16[16,288,1024]{2,1,0:T(8,128)(2,1)} async-done(((bf16[16,288,1024]{2,1,0:T(8,128)(2,1)}), bf16[16,288,1024]{2,1,0:T(8,128)(2,1)}, u32[]{:S(2)}, u32[]{:S(2)}) %all-to-all-start.1) | async-done | bytes 9437216 | tf_op jit(solution)/shard_map/all_to_all | solution.py:196
  652.8 27.0 %select_reduce_fusion.1 = f32[4608,256]{1,0:T(8,128)S(1)} fusion(s32[4608,256]{1,0:T(8,128)} %bitcast_subtract_fusion, bf16[4608,1024,1]{1,0,2:T(8,128)(2,1)} %bitcast.18, bf16[256,8,1024]{2,1,0:T(8,128)(2,1)} %bitcast.159), kind=kOutput, calls=%fused_computation.24 | convolution fusion | flops 19354484736 | bytes 23068672 | tf_op jit(solution)/shard_map/dot_general | solution.py:32
  683.2 41.9 %all-to-all-start.3 = ((f32[16,1,288]{2,1,0:T(1,128)}), f32[16,1,288]{2,1,0:T(1,128)S(1)}, u32[]{:S(2)}, u32[]{:S(2)}) async-start(f32[16,1,288]{2,1,0:T(1,128)} %all_to_all.47), calls=%async_computation.3 | async-start | bytes 49152 | tf_op jit(solution)/shard_map/all_to_all | solution.py:219
  749.4 12.3 gather_fusion.1
  761.8 12.3 gather_fusion.2
  774.2 12.3 gather_fusion
  788.3 9.0 scatter_custom_fusion.3
  805.7 9.0 scatter_custom_fusion.2
  828.5 15.2 eq.111.clone
  843.7 49.7 %eq.127 = s32[16,288,2048]{1,0,2:T(8,128)} reshape(s32[4608,256,8]{0,2,1:T(8,128)} %eq.111.clone) | data formatting | bytes 75497472 | tf_op jit(solution)/shard_map/eq | solution.py:201
  910.9 44.0 %broadcast_in_dim.182 = bf16[16,288,2048]{1,0,2:T(8,128)(2,1)} reshape(bf16[4608,256,8]{0,2,1:T(8,128)(2,1)} %broadcast_in_dim.181) | data formatting | bytes 37748736 | tf_op jit(solution)/shard_map/jit(_where)/broadcast_in_dim | solution.py:273
  954.9 32.5 %compare_select_fusion = bf16[16,288,2048]{1,0,2:T(8,128)(2,1)} fusion(bf16[16,288,2048]{1,0,2:T(8,128)(2,1)} %broadcast_in_dim.182, s32[16,288,2048]{1,0,2:T(8,128)} %eq.127, s32[2048]{0:T(1024)S(1)} %eq.129), kind=kLoop, calls=%fused_computation.18 | loop fusion | flops 18874368 | bytes 75505664 | tf_op jit(solution)/shard_map/jit(_where)/select_n | solution.py:273
  987.3 28.4 %fusion.28 = bf16[16,288,1024]{2,1,0:T(8,128)(2,1)} fusion(bf16[16,288,2048]{1,0,2:T(8,128)(2,1)} %compare_select_fusion, bf16[2048,1024]{1,0:T(8,128)(2,1)} %param.32), kind=kOutput, calls=%fused_computation.48 | convolution fusion | flops 19332071424 | bytes 32505856 | tf_op jit(solution)/shard_map/dot_general | solution.py:22
  1023.8 165.6 %all-to-all-done.7 = bf16[16,288,1024]{2,1,0:T(8,128)(2,1)} async-done(((bf16[16,288,1024]{2,1,0:T(8,128)(2,1)}), bf16[16,288,1024]{2,1,0:T(8,128)(2,1)}, u32[]{:S(2)}, u32[]{:S(2)}) %all-to-all-start.7) | async-done | bytes 9437216 | tf_op jit(solution)/shard_map/all_to_all | solution.py:278
  1189.3 12.6 bitcast_convert_fusion
  1201.9 17.3 gather_fusion.3
  1219.3 11.7 reshape.606
  1231.0 11.0 reduce_sum.290
  1246.4 19.9 fusion.27
  1280.3 31.5 %fusion.97 = f32[16,576,2304]{2,1,0:T(8,128)} fusion(bf16[576,16,64]{0,2,1:T(8,128)(2,1)S(1)} %bitcast.154, bf16[2304,16,64]{0,2,1:T(8,128)(2,1)} %bitcast.147), kind=kOutput, calls=%fused_computation.169 | convolution fusion | flops 2717908992 | bytes 90832896 | tf_op jit(solution)/shard_map/while/body/eval_jaxpr/qhd,khd->hqk/dot_general | solution.py:86
  1311.8 31.3 %fusion.34 = bf16[16,64,2304]{2,1,0:T(8,128)(2,1)} fusion(bf16[576,16,64]{0,2,1:T(8,128)(2,1)S(1)} %bitcast.155, f32[16,576,2304]{2,1,0:T(8,128)} %get-tuple-element.122, f32[16,576]{1,0:T(8,128)S(1)} %copy-done.17), kind=kOutput, calls=%fused_computation.51 | convolution fusion | flops 2762735616 | bytes 90869760 | tf_op jit(solution)/shard_map/while/body/eval_jaxpr/hqk,qhd->khd/dot_general | solution.py:329
  1343.1 134.0 %fusion.31 = bf16[16,64,2304]{2,1,0:T(8,128)(2,1)} fusion(bf16[576,16,64]{0,2,1:T(8,128)(2,1)S(1)} %bitcast.157, f32[16,576,2304]{2,1,0:T(8,128)} %fusion.97, f32[16,576,2304]{2,1,0:T(8,128)} %get-tuple-element.122, f32[16,576]{1,0:T(8,128)S(1)} %copy-done.17), kind=kOutput, calls=%fused_computation.50 | convolution fusion | flops 2868915456 | bytes 175804416 | tf_op jit(solution)/shard_map/while/body/eval_jaxpr/hqk,qhd->khd/dot_general | solution.py:323
  1485.9 41.9 %copy.67 = bf16[1,2304,2048]{2,0,1:T(2,128)(2,1)} copy(bf16[1,2304,2048]{1,2,0:T(8,128)(2,1)} %pad_maximum_fusion) | data formatting | bytes 18874368
  1527.8 15.0 copy.80
  1549.0 13.5 convolution_convert_fusion.1
  1564.2 11.5 convolution_convert_fusion
  1575.7 128.6 %fusion.58 = bf16[16,64,576]{2,1,0:T(8,128)(2,1)S(1)} fusion(bf16[2304,16,64]{0,2,1:T(8,128)(2,1)} %bitcast.150, f32[16,576,2304]{2,1,0:T(8,128)} %fusion.97, f32[16,576,2304]{2,1,0:T(8,128)} %get-tuple-element.122, f32[16,576]{1,0:T(8,128)S(1)} %copy-done.17), kind=kOutput, calls=%fused_computation.100 | convolution fusion | flops 2867145984 | bytes 175804416 | tf_op jit(solution)/shard_map/while/body/eval_jaxpr/hqk,khd->qhd/dot_general | solution.py:317
  1710.4 11.2 copy.68
  1721.6 9.3 convolution_convert_fusion.2
  1735.3 64.8 %reduce-scatter.14.cloned.1.call-done = bf16[1024,1024]{1,0:T(8,128)(2,1)} async-done(((bf16[4096,1024]{1,0:T(8,128)(2,1)}), bf16[1024,1024]{1,0:T(8,128)(2,1)}) %reduce-scatter.14.cloned.1.call-update) | async-done | bytes 2097168 | tf_op jit(solution)/shard_map/reduce_scatter | solution.py:371
  1800.1 89.3 %reduce-scatter.12.cloned.1.call-done = bf16[256,4096]{1,0:T(8,128)(2,1)} async-done(((bf16[1024,4096]{1,0:T(8,128)(2,1)}), bf16[256,4096]{1,0:T(8,128)(2,1)}) %reduce-scatter.12.cloned.1.call-update) | async-done | bytes 2097168 | tf_op jit(solution)/shard_map/reduce_scatter | solution.py:368
  1889.4 73.5 %reduce-scatter.8.cloned.1.call-done = bf16[256,3072]{1,0:T(8,128)(2,1)} async-done(((bf16[1024,3072]{1,0:T(8,128)(2,1)}), bf16[256,3072]{1,0:T(8,128)(2,1)}) %reduce-scatter.8.cloned.1.call-update) | async-done | bytes 1572880 | tf_op jit(solution)/shard_map/reduce_scatter | solution.py:362
  1963.5 9.1 fusion.89
  1974.3 16.3 all-reduce.8
  1998.1 17.0 all-reduce.6
  2027.0 76.3 %all-reduce.11.cloned.1.call-done = (bf16[256,3072]{1,0:T(8,128)(2,1)}, bf16[256,1024]{1,0:T(8,128)(2,1)}, bf16[256,4096]{1,0:T(8,128)(2,1)}, bf16[1024,1024]{1,0:T(8,128)(2,1)}) async-done(((bf16[256,3072]{1,0:T(8,128)(2,1)}, bf16[256,1024]{1,0:T(8,128)(2,1)}, bf16[256,4096]{1,0:T(8,128)(2,1)}, bf16[1024,1024]{1,0:T(8,128)(2,1)}), (bf16[256,3072]{1,0:T(8,128)(2,1)}, bf16[256,1024]{1,0:T(8,128)(2,1)}, ...) | async-done | bytes 6291472 | tf_op jit(solution)/shard_map/psum | solution.py:394
  (340 shorter events, 284.5 us)
Async XLA Ops:
  7.2 75.6 %all-gather.13.cloned.1.call-start = ((), (), s32[]{:S(2)}) async-start(), calls=%async_computation.13 | async-start | bytes 7864320 | tf_op jit(solution)/shard_map/all_gather | solution.py:128
  7.9 145.9 %all-gather.17.cloned.1.call-start = ((), (), s32[]{:S(2)}) async-start(), calls=%async_computation.15 | async-start | bytes 5898240 | tf_op jit(solution)/shard_map/all_gather | solution.py:156
  18.8 71.1 %copy-start.61 = (f32[4,1,256]{2,1,0:T(1,128)}, f32[4,1,256]{2,1,0:T(1,128)S(1)}, u32[]{:S(2)}) copy-start(f32[4,1,256]{2,1,0:T(1,128)S(1)} %convert_element_type.247) | copy-start | bytes 12292
  26.8 63.0 %copy-start.36 = (f32[4,1,256]{2,1,0:T(1,128)}, f32[4,1,256]{2,1,0:T(1,128)S(1)}, u32[]{:S(2)}) copy-start(f32[4,1,256]{2,1,0:T(1,128)S(1)} %convert_element_type.246) | copy-start | bytes 12292
  28.4 61.5 %copy-start.31 = (f32[576]{0:T(1024)}, f32[576]{0:T(1024)S(1)}, u32[]{:S(2)}) copy-start(f32[576]{0:T(1024)S(1)} %broadcast_multiply_fusion.4) | copy-start | bytes 6916
  30.7 59.2 %copy-start.39 = (f32[576]{0:T(1024)}, f32[576]{0:T(1024)S(1)}, u32[]{:S(2)}) copy-start(f32[576]{0:T(1024)S(1)} %fusion.75) | copy-start | bytes 6916
  91.8 129.3 %all-gather.15.cloned.1.call-start = ((), (), s32[]{:S(2)}) async-start(), calls=%async_computation.14 | async-start | bytes 5898240 | tf_op jit(solution)/shard_map/all_gather | solution.py:157
  91.9 24.6 %copy-start.69 = (bf16[256]{0:T(256)(128)(2,1)S(1)}, bf16[256]{0:T(256)(128)(2,1)}, u32[]{:S(2)}) copy-start(bf16[256]{0:T(256)(128)(2,1)} %param.26) | copy-start | bytes 1540
  91.9 24.6 %copy-start.70 = (bf16[256]{0:T(256)(128)(2,1)S(1)}, bf16[256]{0:T(256)(128)(2,1)}, u32[]{:S(2)}) copy-start(bf16[256]{0:T(256)(128)(2,1)} %param.27) | copy-start | bytes 1540
  91.9 58.6 %copy-start.57 = (s32[1,2304]{1,0:T(1,128)S(1)}, s32[1,2304]{1,0:T(1,128)}, u32[]{:S(2)}) copy-start(s32[1,2304]{1,0:T(1,128)} %param.21) | copy-start | bytes 27652
  92.5 166.7 %all-gather.19.cloned.1.call-start = ((), (), s32[]{:S(2)}) async-start(), calls=%async_computation.16 | async-start | bytes 2621440 | tf_op jit(solution)/shard_map/all_gather | solution.py:129
  93.1 241.9 %all-gather.21.cloned.1.call-start = ((), (), s32[]{:S(2)}) async-start(), calls=%async_computation.17 | async-start | bytes 10485760 | tf_op jit(solution)/shard_map/all_gather | solution.py:130
  100.5 50.1 %copy-start.33 = (s32[2304]{0:T(1024)}, s32[2304]{0:T(1024)S(1)}, u32[]{:S(2)}) copy-start(s32[2304]{0:T(1024)S(1)} %fusion.74) | copy-start | bytes 27652
  110.2 358.9 %all-to-all-start = ((s32[16,1,288]{2,1,0:T(1,128)}), s32[16,1,288]{2,1,0:T(1,128)}, u32[]{:S(2)}, u32[]{:S(2)}) async-start(s32[16,1,288]{2,1,0:T(1,128)} %all_to_all.42), calls=%async_computation | async-start | bytes 49152 | tf_op jit(solution)/shard_map/all_to_all | solution.py:193
  115.9 308.6 %all-gather.23.cloned.1.call-start = ((), (), s32[]{:S(2)}) async-start(), calls=%async_computation.18 | async-start | bytes 10485760 | tf_op jit(solution)/shard_map/all_gather | solution.py:131
  194.0 33.8 %copy-start.18 = (f32[16,576]{1,0:T(8,128)}, f32[16,576]{1,0:T(8,128)S(1)}, u32[]{:S(2)}) copy-start(f32[16,576]{1,0:T(8,128)S(1)} %get-tuple-element.121) | copy-start | bytes 110596
  227.8 31.5 %copy-start.4 = (bf16[1,576,1024]{2,1,0:T(8,128)(2,1)S(1)}, bf16[1,576,1024]{2,1,0:T(8,128)(2,1)}, u32[]{:S(2)}) copy-start(bf16[1,576,1024]{2,1,0:T(8,128)(2,1)} %param.19) | copy-start | bytes 3538948
  259.3 75.8 %copy-start.53 = (f32[4,1,256]{2,1,0:T(1,128)S(1)}, f32[4,1,256]{2,1,0:T(1,128)}, u32[]{:S(2)}) copy-start(f32[4,1,256]{2,1,0:T(1,128)} %convert_element_type.248) | copy-start | bytes 12292
  259.3 75.8 %copy-start.63 = (f32[4,1,256]{2,1,0:T(1,128)S(1)}, f32[4,1,256]{2,1,0:T(1,128)}, u32[]{:S(2)}) copy-start(f32[4,1,256]{2,1,0:T(1,128)} %convert_element_type.249) | copy-start | bytes 12292
  262.8 161.7 %copy-start.6 = (f32[576,1024]{1,0:T(8,128)}, f32[576,1024]{1,0:T(8,128)S(1)}, u32[]{:S(2)}) copy-start(f32[576,1024]{1,0:T(8,128)S(1)} %get-tuple-element.124) | copy-start | bytes 7077892
  262.8 72.3 %copy-start.43 = (f32[576]{0:T(1024)}, f32[576]{0:T(1024)S(1)}, u32[]{:S(2)}) copy-start(f32[576]{0:T(1024)S(1)} %broadcast_multiply_fusion.3) | copy-start | bytes 6916
  263.2 71.9 %copy-start.49 = (f32[576]{0:T(1024)}, f32[576]{0:T(1024)S(1)}, u32[]{:S(2)}) copy-start(f32[576]{0:T(1024)S(1)} %multiply_reduce_fusion.7) | copy-start | bytes 6916
  263.2 83.5 %copy-start.55 = (f32[576]{0:T(1024)}, f32[576]{0:T(1024)S(1)}, u32[]{:S(2)}) copy-start(f32[576]{0:T(1024)S(1)} %fusion.76) | copy-start | bytes 6916
  346.7 91.0 %copy-start.25 = (f32[4,1,256]{2,1,0:T(1,128)S(1)}, f32[4,1,256]{2,1,0:T(1,128)}, u32[]{:S(2)}) copy-start(f32[4,1,256]{2,1,0:T(1,128)} %convert_element_type.250) | copy-start | bytes 12292
  346.8 91.0 %copy-start.42 = (f32[4,1,256]{2,1,0:T(1,128)S(1)}, f32[4,1,256]{2,1,0:T(1,128)}, u32[]{:S(2)}) copy-start(f32[4,1,256]{2,1,0:T(1,128)} %convert_element_type.251) | copy-start | bytes 12292
  469.1 183.7 %all-to-all-start.1 = ((bf16[16,288,1024]{2,1,0:T(8,128)(2,1)}), bf16[16,288,1024]{2,1,0:T(8,128)(2,1)}, u32[]{:S(2)}, u32[]{:S(2)}) async-start(bf16[16,288,1024]{2,1,0:T(8,128)(2,1)} %bitcast.145), calls=%async_computation.1 | async-start | bytes 18874368 | tf_op jit(solution)/shard_map/all_to_all | solution.py:196
  492.6 187.2 %slice-start = ((s8[4718592]{0:T(1024)(128)(4,1)}), s8[524288]{0:T(1024)(128)(4,1)S(1)}, s32[]{:S(2)}) async-start(s8[4718592]{0:T(1024)(128)(4,1)} %bitcast.152), calls=%async_computation.25 | async-start | bytes 1048576
  652.8 27.0 %slice-start.1 = ((s8[4718592]{0:T(1024)(128)(4,1)}), s8[4194304]{0:T(1024)(128)(4,1)S(1)}, s32[]{:S(2)}) async-start(s8[4718592]{0:T(1024)(128)(4,1)} %bitcast.152), calls=%async_computation.26 | async-start | bytes 8388608
  682.5 66.6 %copy-start.58 = (f32[1,576]{1,0:T(1,128)S(1)}, f32[1,576]{1,0:T(1,128)}, u32[]{:S(2)}) copy-start(f32[1,576]{1,0:T(1,128)} %param.37) | copy-start | bytes 6916
  683.2 49.3 %all-to-all-start.3 = ((f32[16,1,288]{2,1,0:T(1,128)}), f32[16,1,288]{2,1,0:T(1,128)S(1)}, u32[]{:S(2)}, u32[]{:S(2)}) async-start(f32[16,1,288]{2,1,0:T(1,128)} %all_to_all.47), calls=%async_computation.3 | async-start | bytes 49152 | tf_op jit(solution)/shard_map/all_to_all | solution.py:219
  732.5 12.7 all-to-all-start.4
  745.2 28.9 %all-to-all-start.2 = ((f32[16,1,288]{2,1,0:T(1,128)}), f32[16,1,288]{2,1,0:T(1,128)S(1)}, u32[]{:S(2)}, u32[]{:S(2)}) async-start(f32[16,1,288]{2,1,0:T(1,128)} %all_to_all.45), calls=%async_computation.2 | async-start | bytes 49152 | tf_op jit(solution)/shard_map/all_to_all | solution.py:233
  788.0 40.4 %copy-start.47 = (f32[576]{0:T(1024)}, f32[576]{0:T(1024)S(1)}, u32[]{:S(2)}) copy-start(f32[576]{0:T(1024)S(1)} %get-tuple-element.115) | copy-start | bytes 6916
  798.0 17.4 all-to-all-start.6
  815.4 78.2 %all-to-all-start.5 = ((f32[16,1,288]{2,1,0:T(1,128)}), f32[16,1,288]{2,1,0:T(1,128)S(1)}, u32[]{:S(2)}, u32[]{:S(2)}) async-start(f32[16,1,288]{2,1,0:T(1,128)} %all_to_all.51), calls=%async_computation.5 | async-start | bytes 49152 | tf_op jit(solution)/shard_map/all_to_all | solution.py:264
  1015.7 173.6 %all-to-all-start.7 = ((bf16[16,288,1024]{2,1,0:T(8,128)(2,1)}), bf16[16,288,1024]{2,1,0:T(8,128)(2,1)}, u32[]{:S(2)}, u32[]{:S(2)}) async-start(bf16[16,288,1024]{2,1,0:T(8,128)(2,1)} %fusion.28), calls=%async_computation.7 | async-start | bytes 18874368 | tf_op jit(solution)/shard_map/all_to_all | solution.py:278
  1022.8 681.5 %reduce-scatter.16.cloned.1.call-start = ((), (), s32[]{:S(2)}) async-start(), calls=%async_computation.23 | async-start | bytes 11796480
  1246.3 29.6 %copy-start.11 = (f32[576,1024]{1,0:T(8,128)}, f32[576,1024]{1,0:T(8,128)S(1)}, u32[]{:S(2)}) copy-start(f32[576,1024]{1,0:T(8,128)S(1)} %get-tuple-element.113) | copy-start | bytes 7077892
  1280.3 31.5 %copy-start.17 = (f32[16,576]{1,0:T(8,128)S(1)}, f32[16,576]{1,0:T(8,128)}, u32[]{:S(2)}) copy-start(f32[16,576]{1,0:T(8,128)} %log_add_fusion) | copy-start | bytes 110596
  1311.8 31.3 %copy-start.13 = (bf16[1,576,1024]{1,2,0:T(8,128)(2,1)S(1)}, bf16[1,576,1024]{1,2,0:T(8,128)(2,1)}, u32[]{:S(2)}) copy-start(bf16[1,576,1024]{1,2,0:T(8,128)(2,1)} %copy-done.12) | copy-start | bytes 3538948
  1542.9 192.4 %reduce-scatter.10.cloned.1.call-start = ((), (), s32[]{:S(2)}) async-start(), calls=%async_computation.20 | async-start | bytes 2621440 | tf_op jit(solution)/shard_map/reduce_scatter | solution.py:365
  1549.0 251.1 %reduce-scatter.14.cloned.1.call-start = ((), (), s32[]{:S(2)}) async-start(), calls=%async_computation.22 | async-start | bytes 10485760 | tf_op jit(solution)/shard_map/reduce_scatter | solution.py:371
  1562.5 326.8 %reduce-scatter.12.cloned.1.call-start = ((), (), s32[]{:S(2)}) async-start(), calls=%async_computation.21 | async-start | bytes 10485760 | tf_op jit(solution)/shard_map/reduce_scatter | solution.py:368
  1575.7 387.2 %reduce-scatter.8.cloned.1.call-start = ((), (), s32[]{:S(2)}) async-start(), calls=%async_computation.19 | async-start | bytes 7864320 | tf_op jit(solution)/shard_map/reduce_scatter | solution.py:362
  1731.0 372.4 %all-reduce.11.cloned.1.call-start = ((), (), s32[]{:S(2)}) async-start(), calls=%async_computation.24 | async-start | bytes 12582912 | tf_op jit(solution)/shard_map/psum | solution.py:394
  1735.2 227.7 %copy-start.48 = (f32[576]{0:T(1024)S(1)}, f32[576]{0:T(1024)}, u32[]{:S(2)}) copy-start(f32[576]{0:T(1024)} %copy-done.47) | copy-start | bytes 6916
  1735.3 227.7 %copy-start.59 = (f32[1,576]{1,0:T(1,128)S(1)}, f32[1,576]{1,0:T(1,128)}, u32[]{:S(2)}) copy-start(f32[1,576]{1,0:T(1,128)} %param.37) | copy-start | bytes 6916
  1735.3 228.3 %copy-start.38 = (f32[4,1,256]{2,1,0:T(1,128)S(1)}, f32[4,1,256]{2,1,0:T(1,128)}, u32[]{:S(2)}) copy-start(f32[4,1,256]{2,1,0:T(1,128)} %copy-done.36) | copy-start | bytes 12292
  (48 other events, 419.2 us)
Sparse Core Ops, SparseCore 0:
  9.9 72.8 all-gather.12
  91.9 57.1 all-gather.16
  151.6 57.0 all-gather.14
  210.4 35.3 all-gather.18
  247.4 87.5 all-gather.20
  336.8 87.6 all-gather.22
  1543.0 129.0 reduce-scatter.15
  1675.0 35.1 reduce-scatter.9
  1713.6 86.4 reduce-scatter.13
  1803.0 86.3 reduce-scatter.11
  1892.7 70.1 reduce-scatter.7
  1965.6 137.7 all-reduce.10
where the time goes:
time: 2140 us; the launch traced here: 2120 us
  waiting for transfers between devices  830 us (39%)
  matrix products  557 us (26%)
  local copies, waits for them, and re-layouts  368 us (17%)
  other arithmetic  182 us (9%)
  starting transfers between devices  84.1 us (4%)
  blocking collectives  82.4 us (4%)
    all_to_all x1, waiting for transfers between devices, local(): lax.all_to_all(partial_grad.astype(jnp.bfloat16), ('batch', 'ctx'), split...  166 us
    all_to_all x1, waiting for transfers between devices, local(): lax.all_to_all(send_queries, ('batch', 'ctx'), split_axis=0, concat_axis=...  148 us
    dot_general x1, matrix products, every_key(): jnp.einsum('hqk,qhd->khd', score_grad, split_heads(query_one, head_count)...  134 us
    dot_general x1, matrix products, every_key(): jnp.einsum('hqk,khd->qhd', score_grad, split_heads(keys_one, head_count),...  129 us
    unnamed x171, local copies, waits for them, and re-layouts  97.5 us
    reduce_scatter x1, waiting for transfers between devices, local(): lax.psum_scatter(upward_grad.astype(jnp.bfloat16), 'ctx', scatter_dimensi...  89.3 us
    all_gather x1, waiting for transfers between devices, local(): lax.all_gather(downward_weight, 'ctx', axis=0, tiled=True)  77.7 us
    psum x1, waiting for transfers between devices, local(): lax.psum(shard_grads[0].astype(jnp.bfloat16), ('rep', 'batch'))  76.3 us
  transfers between devices with their start and end apart: 20, of which 11 were waited for; matrix products, arithmetic and copies ran while one was open for 26% of the time, Pallas kernels for 0%

commit v1 on v0

v1 whole, which is shorter than its diff:
```python
import functools

import jax
import jax.numpy as jnp
from jax import lax
from jax.experimental import pallas as pl
from jax.experimental.pallas import tpu as pltpu
from jax.sharding import PartitionSpec as P

HEADS = 16


norm_eps = 1e-05
mix_weight = 0.25
masked_value = -1e30
vmem_limit = 60 * 1024 * 1024


def norm_rows(values, scale_gain, shift_term):
    average = jnp.mean(values, axis=-1, keepdims=True)
    centred = values - average
    spread = jnp.mean(centred * centred, axis=-1, keepdims=True)
    return centred * lax.rsqrt(spread + norm_eps) * scale_gain + shift_term


def row_dot(left_side, right_side):
    return jnp.dot(left_side, right_side, preferred_element_type=jnp.float32)


def left_dot(left_side, right_side):
    return lax.dot_general(
        left_side, right_side, (((0,), (0,)), ((), ())), preferred_element_type=jnp.float32
    )


def right_dot(left_side, right_side):
    return lax.dot_general(
        left_side, right_side, (((1,), (1,)), ((), ())), preferred_element_type=jnp.float32
    )


def spec(shape, index_map):
    return pl.BlockSpec(shape, index_map)


def kernel_params(dims=1):
    return pltpu.CompilerParams(
        vmem_limit_bytes=vmem_limit, dimension_semantics=("arbitrary",) * dims
    )


def head_rows(head, size):
    return slice(head * size, (head + 1) * size)


def masked_heads(block, head_count, axis):
    size = block.shape[axis] // head_count
    index = lax.broadcasted_iota(jnp.int32, block.shape, axis) // size
    zero = jnp.zeros((), block.dtype)
    return [jnp.where(index == head, block, zero) for head in range(head_count)]


def block_mask(key_block, query_block, size, start_row):
    key_pos = key_block * size + lax.broadcasted_iota(jnp.int32, (size, size), 0)
    query_pos = query_block * size + lax.broadcasted_iota(jnp.int32, (size, size), 1)
    return (key_pos <= query_pos) & (key_pos >= start_row)


def attend_kernel(
    head_count, low_ref, q_ref, k_ref, v_ref, start_ref, o_ref, lse_ref, vt_ref, acc_ref
):
    step = pl.program_id(0)
    size, width = q_ref.shape
    head_size = width // head_count
    blocks = k_ref.shape[0] // size

    @pl.when(step == 0)
    def _():
        for block in range(blocks):
            rows = slice(block * size, (block + 1) * size)
            vt_ref[:, rows] = v_ref[rows, :].astype(jnp.float32).T.astype(jnp.bfloat16)

    scaled = q_ref[...].astype(jnp.float32) * (head_size ** (-0.5))
    turned = masked_heads(scaled.T, head_count, 0)
    turned = [part.astype(jnp.bfloat16) for part in turned]
    start_row = start_ref[0:1, :]
    acc_ref[...] = jnp.zeros_like(acc_ref)
    first = (
        tuple(jnp.full((1, size), masked_value, jnp.float32) for _ in range(head_count)),
        tuple(jnp.zeros((1, size), jnp.float32) for _ in range(head_count)),
    )

    def body(block, state):
        peaks, totals = state
        rows = pl.ds(pl.multiple_of(block * size, size), size)
        keys = k_ref[rows, :]
        allowed = block_mask(block, step, size, start_row)
        new_peaks, new_totals = [], []
        for head in range(head_count):
            scores = jnp.where(allowed, row_dot(keys, turned[head]), masked_value)
            peak = jnp.maximum(peaks[head], jnp.max(scores, axis=0, keepdims=True))
            fade = jnp.exp(peaks[head] - peak)
            weights = jnp.exp(scores - peak)
            new_peaks.append(peak)
            new_totals.append(totals[head] * fade + jnp.sum(weights, axis=0, keepdims=True))
            part = head_rows(head, head_size)
            acc_ref[part, :] = acc_ref[part, :] * fade + row_dot(
                vt_ref[part, rows], weights.astype(jnp.bfloat16)
            )
        return tuple(new_peaks), tuple(new_totals)

    peaks, totals = lax.fori_loop(low_ref[step], step + 1, body, first)
    for head in range(head_count):
        part = head_rows(head, head_size)
        acc_ref[part, :] = acc_ref[part, :] / totals[head]
        lse_ref[head : head + 1, :] = peaks[head] + jnp.log(totals[head])
    o_ref[...] = acc_ref[...].T.astype(jnp.bfloat16)


def attend(query, key, value, start_rows, low_blocks, head_count, size):
    length, width = query.shape
    blocks = length // size
    stat_rows = -(-head_count // 8) * 8
    return pl.pallas_call(
        functools.partial(attend_kernel, head_count),
        grid_spec=pltpu.PrefetchScalarGridSpec(
            num_scalar_prefetch=1,
            grid=(blocks,),
            in_specs=[
                spec((size, width), lambda i, low: (i, 0)),
                spec((length, width), lambda i, low: (0, 0)),
                spec((length, width), lambda i, low: (0, 0)),
                spec((8, size), lambda i, low: (0, i)),
            ],
            out_specs=[
                spec((size, width), lambda i, low: (i, 0)),
                spec((stat_rows, size), lambda i, low: (0, i)),
            ],
            scratch_shapes=[
                pltpu.VMEM((width, length), jnp.bfloat16),
                pltpu.VMEM((width, size), jnp.float32),
            ],
        ),
        out_shape=[
            jax.ShapeDtypeStruct((length, width), jnp.bfloat16),
            jax.ShapeDtypeStruct((stat_rows, length), jnp.float32),
        ],
        compiler_params=kernel_params(),
        cost_estimate=pl.CostEstimate(
            flops=2 * length * length * width,
            bytes_accessed=8 * length * width,
            transcendentals=length * length * head_count // 3,
        ),
        name="attend",
    )(low_blocks, query, key, value, start_rows)


def attend_back_kernel(
    head_count,
    low_ref,
    q_ref,
    k_ref,
    v_ref,
    grad_ref,
    o_ref,
    lse_ref,
    start_ref,
    dq_ref,
    dk_ref,
    dv_ref,
    kt_ref,
    dkey_ref,
    dvalue_ref,
    dqt_ref,
    score_ref,
    weight_ref,
):
    step = pl.program_id(0)
    size, width = q_ref.shape
    head_size = width // head_count
    score_scale = head_size ** (-0.5)
    blocks = k_ref.shape[0] // size

    @pl.when(step == 0)
    def _():
        dkey_ref[...] = jnp.zeros_like(dkey_ref)
        dvalue_ref[...] = jnp.zeros_like(dvalue_ref)
        for block in range(blocks):
            rows = slice(block * size, (block + 1) * size)
            kt_ref[:, rows] = k_ref[rows, :].astype(jnp.float32).T.astype(jnp.bfloat16)

    scaled = q_ref[...].astype(jnp.float32) * score_scale
    grads = grad_ref[...].astype(jnp.float32)
    dots = (grads * o_ref[...].astype(jnp.float32)).T
    query_turned = [p.astype(jnp.bfloat16) for p in masked_heads(scaled.T, head_count, 0)]
    grad_turned = [p.astype(jnp.bfloat16) for p in masked_heads(grads.T, head_count, 0)]
    query_stack = jnp.concatenate(
        [p.astype(jnp.bfloat16) for p in masked_heads(scaled, head_count, 1)], axis=0
    )
    grad_stack = jnp.concatenate(
        [p.astype(jnp.bfloat16) for p in masked_heads(grads, head_count, 1)], axis=0
    )
    row_dots = [
        jnp.sum(dots[head_rows(head, head_size), :], axis=0, keepdims=True)
        for head in range(head_count)
    ]
    start_row = start_ref[0:1, :]
    dqt_ref[...] = jnp.zeros_like(dqt_ref)

    def body(block, carry):
        rows = pl.ds(pl.multiple_of(block * size, size), size)
        keys = k_ref[rows, :]
        values = v_ref[rows, :]
        allowed = block_mask(block, step, size, start_row)
        for head in range(head_count):
            lanes = slice(head * size, (head + 1) * size)
            part = head_rows(head, head_size)
            scores = jnp.where(allowed, row_dot(keys, query_turned[head]), masked_value)
            weights = jnp.exp(scores - lse_ref[head : head + 1, :])
            weight_grad = row_dot(values, grad_turned[head])
            score_grad = (weights * (weight_grad - row_dots[head])).astype(jnp.bfloat16)
            score_ref[:, lanes] = score_grad
            weight_ref[:, lanes] = weights.astype(jnp.bfloat16)
            dqt_ref[part, :] += row_dot(kt_ref[part, rows], score_grad)
        dkey_ref[rows, :] += row_dot(score_ref[...], query_stack)
        dvalue_ref[rows, :] += row_dot(weight_ref[...], grad_stack)
        return carry

    lax.fori_loop(low_ref[step], step + 1, body, 0)
    dq_ref[...] = (dqt_ref[...] * score_scale).T.astype(jnp.bfloat16)

    @pl.when(step == blocks - 1)
    def _():
        dk_ref[...] = dkey_ref[...].astype(jnp.bfloat16)
        dv_ref[...] = dvalue_ref[...].astype(jnp.bfloat16)


def attend_back(query, key, value, grad, attended, lse, start_rows, low_blocks, head_count, size):
    length, width = query.shape
    blocks = length // size
    stat_rows = lse.shape[0]
    block_spec = spec((size, width), lambda i, low: (i, 0))
    whole_spec = spec((length, width), lambda i, low: (0, 0))
    return pl.pallas_call(
        functools.partial(attend_back_kernel, head_count),
        grid_spec=pltpu.PrefetchScalarGridSpec(
            num_scalar_prefetch=1,
            grid=(blocks,),
            in_specs=[
                block_spec,
                whole_spec,
                whole_spec,
                block_spec,
                block_spec,
                spec((stat_rows, size), lambda i, low: (0, i)),
                spec((8, size), lambda i, low: (0, i)),
            ],
            out_specs=[block_spec, whole_spec, whole_spec],
            scratch_shapes=[
                pltpu.VMEM((width, length), jnp.bfloat16),
                pltpu.VMEM((length, width), jnp.float32),
                pltpu.VMEM((length, width), jnp.float32),
                pltpu.VMEM((width, size), jnp.float32),
                pltpu.VMEM((size, head_count * size), jnp.bfloat16),
                pltpu.VMEM((size, head_count * size), jnp.bfloat16),
            ],
        ),
        out_shape=[jax.ShapeDtypeStruct((length, width), jnp.bfloat16)] * 3,
        compiler_params=kernel_params(),
        cost_estimate=pl.CostEstimate(
            flops=5 * length * length * width,
            bytes_accessed=16 * length * width,
            transcendentals=length * length * head_count // 3,
        ),
        name="attend_back",
    )(low_blocks, query, key, value, grad, attended, lse, start_rows)


def to_columns(block, rows):
    parts = [block[group].T for group in range(block.shape[0])]
    return parts[0] if len(parts) == 1 else jnp.concatenate(parts, axis=0)


def near_kernel(
    spacing, dist_scale, q_ref, keys_ref, square_ref, values_ref, near_ref, target_ref, e_ref, s_ref
):
    rows, near_count = near_ref.shape
    lane = lax.broadcasted_iota(jnp.int32, (rows, near_count), 1)
    offset = near_ref[...] - spacing * lane
    target = to_columns(target_ref, rows)[:, 0:1]
    picked = jnp.zeros((rows, near_count), jnp.float32)
    words = jnp.full((rows, near_count), -1.0, jnp.float32)
    queries = q_ref[...]
    for plane in range(spacing):
        lanes = slice(plane * near_count, (plane + 1) * near_count)
        inner = row_dot(queries, keys_ref[:, lanes])
        chosen = offset == plane
        picked = jnp.where(chosen, 2.0 * inner - square_ref[plane : plane + 1, :], picked)
        words = jnp.where(chosen, values_ref[plane : plane + 1, :], words)
    scores = picked * dist_scale
    matched = words == target
    peak = jnp.max(scores, axis=1, keepdims=True)
    raised = jnp.exp(scores - peak)
    total = jnp.sum(raised, axis=1, keepdims=True)
    hits = jnp.sum(jnp.where(matched, raised, 0.0), axis=1, keepdims=True)
    e_ref[...] = jnp.where(matched, raised, -raised)
    stat_lane = lax.broadcasted_iota(jnp.int32, (rows, 128), 1)
    stats = jnp.where(stat_lane == 0, peak, jnp.where(stat_lane == 1, total, hits))
    groups, stat_rows, piece = s_ref.shape
    for group in range(groups):
        s_ref[group] = stats[group * piece : (group + 1) * piece, :].T[:stat_rows, :]


def near_scores(queries, keys_turned, square, values, near, target_rows, rows, spacing):
    slot_rows, width = queries.shape
    near_count = near.shape[1]
    groups = target_rows.shape[0] * rows // slot_rows
    piece = target_rows.shape[2]
    keys = keys_turned.shape[1]
    return pl.pallas_call(
        functools.partial(near_kernel, spacing, width ** (-0.5)),
        grid=(slot_rows // rows,),
        in_specs=[
            spec((rows, width), lambda i: (i, 0)),
            spec((width, keys), lambda i: (0, 0)),
            spec((spacing, near_count), lambda i: (0, 0)),
            spec((spacing, near_count), lambda i: (0, 0)),
            spec((rows, near_count), lambda i: (i, 0)),
            spec((groups, 8, piece), lambda i: (i, 0, 0)),
        ],
        out_specs=[
            spec((rows, near_count), lambda i: (i, 0)),
            spec((groups, 8, piece), lambda i: (i, 0, 0)),
        ],
        out_shape=[
            jax.ShapeDtypeStruct((slot_rows, near_count), jnp.float32),
            jax.ShapeDtypeStruct(target_rows.shape, jnp.float32),
        ],
        compiler_params=kernel_params(),
        cost_estimate=pl.CostEstimate(
            flops=2 * slot_rows * width * keys,
            bytes_accessed=slot_rows * (2 * width + 8 * near_count) + 2 * keys * width,
            transcendentals=slot_rows * near_count,
        ),
        name="near_scores",
    )(queries, keys_turned, square, values, near, target_rows)


def near_back_kernel(spacing, factor, e_ref, near_ref, coeff_ref, keys_ref, out_ref, dense_ref):
    rows, near_count = near_ref.shape
    lane = lax.broadcasted_iota(jnp.int32, (rows, near_count), 1)
    offset = near_ref[...] - spacing * lane
    columns = to_columns(coeff_ref, rows)
    coefficient, probability = columns[:, 0:1], columns[:, 1:2]
    marked = e_ref[...]
    matched = jnp.where(marked > 0.0, 1.0, 0.0)
    grads = coefficient * (matched - probability) * jnp.abs(marked) * factor
    for plane in range(spacing):
        lanes = slice(plane * near_count, (plane + 1) * near_count)
        dense_ref[:, lanes] = jnp.where(offset == plane, grads, 0.0).astype(jnp.bfloat16)
    out_ref[...] = row_dot(dense_ref[...], keys_ref[...]).astype(out_ref.dtype)


def near_back(marked, near, coeff_rows, keys_planes, rows, spacing):
    slot_rows, near_count = near.shape
    keys, width = keys_planes.shape
    groups = coeff_rows.shape[0] * rows // slot_rows
    piece = coeff_rows.shape[2]
    return pl.pallas_call(
        functools.partial(near_back_kernel, spacing, 2.0 * width ** (-0.5)),
        grid=(slot_rows // rows,),
        in_specs=[
            spec((rows, near_count), lambda i: (i, 0)),
            spec((rows, near_count), lambda i: (i, 0)),
            spec((groups, 8, piece), lambda i: (i, 0, 0)),
            spec((keys, width), lambda i: (0, 0)),
        ],
        out_specs=spec((rows, width), lambda i: (i, 0)),
        out_shape=jax.ShapeDtypeStruct((slot_rows, width), jnp.bfloat16),
        scratch_shapes=[pltpu.VMEM((rows, keys), jnp.bfloat16)],
        compiler_params=kernel_params(),
        cost_estimate=pl.CostEstimate(
            flops=2 * slot_rows * width * keys,
            bytes_accessed=slot_rows * (2 * width + 8 * near_count) + 2 * keys * width,
            transcendentals=0,
        ),
        name="near_back",
    )(marked, near, coeff_rows, keys_planes)


def pack_kernel(rows_ref, map_ref, out_ref):
    capacity = out_ref.shape[1]
    slot = lax.broadcasted_iota(jnp.int32, (capacity, rows_ref.shape[0]), 0)
    chosen = jnp.where(map_ref[0] == slot, 1.0, 0.0).astype(jnp.bfloat16)
    out_ref[0] = row_dot(chosen, rows_ref[...]).astype(out_ref.dtype)


def pack_rows(rows, slot_map, capacity):
    owners, tokens = slot_map.shape
    width = rows.shape[1]
    return pl.pallas_call(
        pack_kernel,
        grid=(owners,),
        in_specs=[
            spec((tokens, width), lambda o: (0, 0)),
            spec((1, 1, tokens), lambda o: (o, 0, 0)),
        ],
        out_specs=spec((1, capacity, width), lambda o: (o, 0, 0)),
        out_shape=jax.ShapeDtypeStruct((owners, capacity, width), rows.dtype),
        compiler_params=kernel_params(),
        cost_estimate=pl.CostEstimate(
            flops=2 * owners * capacity * tokens * width,
            bytes_accessed=2 * owners * capacity * width,
            transcendentals=0,
        ),
        name="pack_rows",
    )(rows, slot_map.reshape(owners, 1, tokens))


def unpack_kernel(back_ref, column_ref, out_ref):
    owner = pl.program_id(0)
    tokens, capacity = out_ref.shape[0], back_ref.shape[1]
    slot = lax.broadcasted_iota(jnp.int32, (tokens, capacity), 1)
    chosen = jnp.where(column_ref[0] == slot, 1.0, 0.0).astype(jnp.bfloat16)
    part = row_dot(chosen, back_ref[0])

    @pl.when(owner == 0)
    def _():
        out_ref[...] = part

    @pl.when(owner > 0)
    def _():
        out_ref[...] += part


def unpack_rows(returned, slot_map):
    owners, capacity, width = returned.shape
    tokens = slot_map.shape[1]
    return pl.pallas_call(
        unpack_kernel,
        grid=(owners,),
        in_specs=[
            spec((1, capacity, width), lambda o: (o, 0, 0)),
            spec((1, tokens, 1), lambda o: (o, 0, 0)),
        ],
        out_specs=spec((tokens, width), lambda o: (0, 0)),
        out_shape=jax.ShapeDtypeStruct((tokens, width), jnp.float32),
        compiler_params=kernel_params(),
        cost_estimate=pl.CostEstimate(
            flops=2 * owners * capacity * tokens * width,
            bytes_accessed=2 * owners * capacity * width,
            transcendentals=0,
        ),
        name="unpack_rows",
    )(returned, slot_map.reshape(owners, tokens, 1))


def mix_kernel(stats_ref, map_ref, prob_ref, loss_ref, send_ref, peak_ref, total_ref, hits_ref):
    owners, stat_rows, capacity = stats_ref.shape
    tokens = map_ref.shape[1]
    slot = lax.broadcasted_iota(jnp.int32, (capacity, tokens), 0)
    for owner in range(owners):
        chosen = map_ref[owner : owner + 1, :] == slot
        columns = stats_ref[owner].T
        for place, target in enumerate((peak_ref, total_ref, hits_ref)):
            target[owner : owner + 1, :] = jnp.sum(
                jnp.where(chosen, columns[:, place : place + 1], 0.0), axis=0, keepdims=True
            )
    member = map_ref[...] >= 0
    peaks = jnp.where(member, peak_ref[...], -3e38)
    best = jnp.max(peaks, axis=0, keepdims=True)
    rescale = jnp.where(member, jnp.exp(peaks - best), 0.0)
    knn_total = jnp.sum(total_ref[...] * rescale, axis=0, keepdims=True)
    knn_prob = jnp.sum(hits_ref[...] * rescale, axis=0, keepdims=True) / knn_total
    mixture = mix_weight * knn_prob + (1.0 - mix_weight) * prob_ref[...]
    loss_ref[...] = -jnp.log(mixture)
    peak_ref[...] = (-mix_weight / (mixture * knn_total)) * rescale
    for owner in range(owners):
        chosen = map_ref[owner : owner + 1, :] == slot
        coefficient = jnp.sum(
            jnp.where(chosen, peak_ref[owner : owner + 1, :], 0.0), axis=1, keepdims=True
        )
        probability = jnp.sum(jnp.where(chosen, knn_prob, 0.0), axis=1, keepdims=True)
        lane = lax.broadcasted_iota(jnp.int32, (capacity, 128), 1)
        both = jnp.where(lane == 0, coefficient, probability)
        send_ref[owner] = both.T[:stat_rows, :]


def mix_losses(stats, slot_map, model_prob):
    owners, stat_rows, capacity = stats.shape
    tokens = slot_map.shape[1]
    vmem = pl.BlockSpec(memory_space=pltpu.VMEM)
    return pl.pallas_call(
        mix_kernel,
        in_specs=[vmem] * 3,
        out_specs=[vmem] * 2,
        out_shape=[
            jax.ShapeDtypeStruct((1, tokens), jnp.float32),
            jax.ShapeDtypeStruct(stats.shape, jnp.float32),
        ],
        scratch_shapes=[pltpu.VMEM((owners, tokens), jnp.float32)] * 3,
        compiler_params=pltpu.CompilerParams(vmem_limit_bytes=vmem_limit),
        name="mix_losses",
    )(stats, slot_map, model_prob)


def row_chunk(total, choices):
    for choice in choices:
        if total % choice == 0:
            return choice
    return total


def slot_picker(slot_map, capacity):
    return slot_map[:, None, :] == jnp.arange(capacity, dtype=jnp.int32)[None, :, None]


def pack_any(rows, slot_map, capacity):
    if capacity % 16 == 0:
        return pack_rows(rows, slot_map, capacity)
    chosen = slot_picker(slot_map, capacity).astype(jnp.bfloat16)
    return row_dot(chosen, rows).astype(rows.dtype)


def unpack_any(returned, slot_map):
    capacity = returned.shape[1]
    if capacity % 16 == 0:
        return unpack_rows(returned, slot_map)
    chosen = slot_picker(slot_map, capacity).astype(jnp.bfloat16)
    return jnp.einsum("ost,osw->tw", chosen, returned, preferred_element_type=jnp.float32)


def mix_any(stats, slot_map, model_prob):
    owners, stat_rows, capacity = stats.shape
    if capacity % 16 == 0:
        return mix_losses(stats, slot_map, model_prob)
    chosen = slot_picker(slot_map, capacity)
    peak, total, hits = [
        jnp.sum(jnp.where(chosen, stats[:, row, :, None], 0.0), axis=1) for row in range(3)
    ]
    member = slot_map >= 0
    peaks = jnp.where(member, peak, -3e38)
    best = jnp.max(peaks, axis=0, keepdims=True)
    rescale = jnp.where(member, jnp.exp(peaks - best), 0.0)
    knn_total = jnp.sum(total * rescale, axis=0, keepdims=True)
    knn_prob = jnp.sum(hits * rescale, axis=0, keepdims=True) / knn_total
    mixture = mix_weight * knn_prob + (1.0 - mix_weight) * model_prob
    coefficient = (-mix_weight / (mixture * knn_total)) * rescale
    sent = [
        jnp.sum(jnp.where(chosen, part[:, None, :], 0.0), axis=2)
        for part in (coefficient, jnp.broadcast_to(knn_prob, coefficient.shape))
    ]
    sent = jnp.stack(sent + [sent[1]] * (stat_rows - 2), axis=1)
    return -jnp.log(mixture), sent


def local(
    tokens,
    cotangent,
    segment_ids,
    first_gain,
    first_shift,
    second_gain,
    second_shift,
    final_gain,
    final_shift,
    project_weight,
    output_weight,
    upward_weight,
    downward_weight,
    store_keys,
    store_values,
    owners,
    neighbours,
    targets,
    model_prob,
):
    head_count = HEADS
    group_seqs, block_len, width = tokens.shape
    seq_len = segment_ids.shape[1]
    ctx_count = lax.axis_size("ctx")
    shard_count = lax.axis_size("batch") * ctx_count
    capacity = neighbours.shape[3]
    near_count = neighbours.shape[4]
    top_count = owners.shape[2]
    key_count = store_keys.shape[0]
    spacing = key_count // near_count
    slot_rows = shard_count * capacity
    everyone = ("batch", "ctx")
    own_heads = head_count // ctx_count
    own_width = width // ctx_count
    attend_size = row_chunk(seq_len, (256, 128))

    tokens_full = lax.all_gather(tokens[0], "ctx", axis=0, tiled=True)
    vectors = jnp.stack(
        [first_gain, first_shift, second_gain, second_shift, final_gain, final_shift]
    )
    vectors = lax.all_gather(vectors, "ctx", axis=1, tiled=True).astype(jnp.float32)
    gain_list = [vectors[row] for row in range(6)]
    own_rows = project_weight.shape[0]
    proj_own = lax.all_to_all(
        project_weight.reshape(own_rows, 3, ctx_count, own_width).transpose(2, 0, 1, 3),
        "ctx",
        split_axis=0,
        concat_axis=0,
        tiled=True,
    ).reshape(width, 3 * own_width)

    def gather_weight(weight):
        half = weight.shape[0] // lax.axis_size("rep")
        mine = lax.dynamic_slice_in_dim(weight, lax.axis_index("rep") * half, half, 0)
        return lax.all_gather(mine, ("ctx", "rep"), axis=0, tiled=True)

    out_full = gather_weight(output_weight)
    up_full = gather_weight(upward_weight)
    down_full = gather_weight(downward_weight)

    member = jnp.any(
        owners[0][:, :, None] == jnp.arange(shard_count, dtype=jnp.int32)[None, None, :], axis=1
    )
    place = jnp.arange(block_len, dtype=jnp.int32)
    earlier = (place[:, None] <= place[None, :]).astype(jnp.bfloat16)
    running = left_dot(member.astype(jnp.bfloat16), earlier).astype(jnp.int32)
    slot_map = jnp.where(member.T, running - 1, -1)
    send_targets = jnp.sum(
        jnp.where(slot_picker(slot_map, capacity), targets.reshape(1, 1, -1), 0), axis=2
    )
    got_targets = lax.all_to_all(
        send_targets.astype(jnp.int32), everyone, split_axis=0, concat_axis=0, tiled=True
    ).astype(jnp.float32)
    planes = store_keys.reshape(near_count, spacing, width).transpose(1, 0, 2)
    planes = planes.reshape(key_count, width)
    planes_turned = planes.T
    key_square = jnp.sum(jnp.square(store_keys.astype(jnp.float32)), axis=1)
    key_square = key_square.reshape(near_count, spacing).T
    value_planes = store_values.astype(jnp.float32).reshape(near_count, spacing).T
    near_table = neighbours.reshape(slot_rows, near_count)
    if capacity % 16 == 0:
        near_rows = row_chunk(slot_rows, (2 * capacity,))
        stat_shape = (shard_count, 8, capacity)
    else:
        near_rows = row_chunk(slot_rows, (576, 512, 384, 256, 128))
        stat_shape = (slot_rows // near_rows, 8, near_rows)
    target_rows = jnp.broadcast_to(got_targets.reshape(stat_shape[0], 1, stat_shape[2]), stat_shape)

    segments = segment_ids[0]
    start_rows = jnp.sum(
        (segments[None, :] < segments[:, None]).astype(jnp.int32), axis=1
    )
    low_blocks = start_rows[::attend_size] // attend_size
    start_rows = jnp.broadcast_to(start_rows[None, :], (8, seq_len))
    normed_full = norm_rows(
        tokens_full.astype(jnp.float32), gain_list[0], gain_list[1]
    ).astype(jnp.bfloat16)
    projected = row_dot(normed_full, proj_own).astype(jnp.bfloat16)
    query_own = projected[:, :own_width]
    key_own = projected[:, own_width : 2 * own_width]
    value_own = projected[:, 2 * own_width :]
    attended_own, log_total = attend(
        query_own, key_own, value_own, start_rows, low_blocks, own_heads, attend_size
    )
    attended = lax.all_to_all(attended_own, "ctx", split_axis=0, concat_axis=1, tiled=True)
    inputs = tokens[0].astype(jnp.float32)
    hidden = inputs + row_dot(attended, out_full)
    normed_two = norm_rows(hidden, gain_list[2], gain_list[3]).astype(jnp.bfloat16)
    upper_rows = row_dot(normed_two, up_full)
    active = jax.nn.gelu(upper_rows).astype(jnp.bfloat16)
    summed = hidden + row_dot(active, down_full)
    final_rows = norm_rows(summed, gain_list[4], gain_list[5]).astype(jnp.bfloat16)

    got_queries = lax.all_to_all(
        pack_any(final_rows, slot_map, capacity),
        everyone,
        split_axis=0,
        concat_axis=0,
        tiled=True,
    ).reshape(slot_rows, width)
    marked, stats = near_scores(
        got_queries,
        planes_turned,
        key_square,
        value_planes,
        near_table,
        target_rows,
        near_rows,
        spacing,
    )

    def to_senders(rows):
        if rows.shape[0] == shard_count:
            return rows
        return rows.transpose(1, 0, 2).reshape(8, shard_count, capacity).transpose(1, 0, 2)

    def to_blocks(rows):
        if rows.shape == stat_shape:
            return rows
        return (
            rows.transpose(1, 0, 2)
            .reshape(8, stat_shape[0], stat_shape[2])
            .transpose(1, 0, 2)
        )

    replies = lax.all_to_all(
        to_senders(stats), everyone, split_axis=0, concat_axis=0, tiled=True
    )
    token_loss, send_coeff = mix_any(replies, slot_map, model_prob)
    got_coeff = lax.all_to_all(send_coeff, everyone, split_axis=0, concat_axis=0, tiled=True)
    partial_grad = near_back(
        marked, near_table, to_blocks(got_coeff), planes, near_rows, spacing
    ).reshape(shard_count, capacity, width)
    returned = lax.all_to_all(partial_grad, everyone, split_axis=0, concat_axis=0, tiled=True)
    query_grad = unpack_any(returned, slot_map)

    out_grad = cotangent[0].astype(jnp.float32) + query_grad
    final_vjp = jax.vjp(norm_rows, summed, gain_list[4], gain_list[5])[1]
    summed_grad, final_gain_grad, final_shift_grad = final_vjp(out_grad)
    branch_grad = summed_grad.astype(jnp.bfloat16)
    downward_grad = left_dot(active, branch_grad)
    active_grad = right_dot(branch_grad, down_full)
    gelu_vjp = jax.vjp(jax.nn.gelu, upper_rows)[1]
    upper_grad = gelu_vjp(active_grad)[0].astype(jnp.bfloat16)
    upward_grad = left_dot(normed_two, upper_grad)
    second_vjp = jax.vjp(norm_rows, hidden, gain_list[2], gain_list[3])[1]
    hidden_part, second_gain_grad, second_shift_grad = second_vjp(right_dot(upper_grad, up_full))
    hidden_grad = summed_grad + hidden_part
    attn_grad = hidden_grad.astype(jnp.bfloat16)
    output_grad = left_dot(attended, attn_grad)
    attended_grad = right_dot(attn_grad, out_full).astype(jnp.bfloat16)
    grad_own = lax.all_to_all(attended_grad, "ctx", split_axis=1, concat_axis=0, tiled=True)
    proj_grad = jnp.concatenate(
        attend_back(
            query_own,
            key_own,
            value_own,
            grad_own,
            attended_own,
            log_total,
            start_rows,
            low_blocks,
            own_heads,
            attend_size,
        ),
        axis=1,
    )
    normed_terms = right_dot(proj_grad, proj_own)
    first_vjp = jax.vjp(
        lambda gain, shift: norm_rows(tokens_full.astype(jnp.float32), gain, shift),
        gain_list[0],
        gain_list[1],
    )[1]
    first_gain_grad, first_shift_grad = first_vjp(normed_terms)
    normed_grad = lax.psum_scatter(
        normed_terms.astype(jnp.bfloat16), "ctx", scatter_dimension=0, tiled=True
    ).astype(jnp.float32)
    input_vjp = jax.vjp(lambda rows: norm_rows(rows, gain_list[0], gain_list[1]), inputs)[1]
    input_grad = hidden_grad + input_vjp(normed_grad)[0]

    def scatter_grad(grad):
        return lax.psum_scatter(
            grad.astype(jnp.bfloat16), ("ctx", "rep"), scatter_dimension=0, tiled=True
        )

    project_part = lax.all_to_all(
        left_dot(normed_full, proj_grad).astype(jnp.bfloat16),
        "ctx",
        split_axis=0,
        concat_axis=0,
        tiled=True,
    )
    project_part = (
        project_part.reshape(ctx_count, own_rows, 3, own_width)
        .transpose(1, 2, 0, 3)
        .reshape(own_rows, 3 * width)
    )
    pieces = (
        lax.psum_scatter(project_part, "rep", scatter_dimension=0, tiled=True),
        scatter_grad(output_grad),
        scatter_grad(upward_grad),
        scatter_grad(downward_grad),
    )
    weight_grads = [
        lax.all_gather(lax.psum(piece, "batch"), "rep", axis=0, tiled=True).astype(jnp.float32)
        for piece in pieces
    ]
    vector_grads = lax.psum(
        jnp.stack(
            [
                first_gain_grad,
                first_shift_grad,
                second_gain_grad,
                second_shift_grad,
                final_gain_grad,
                final_shift_grad,
            ]
        ),
        ("rep", "batch", "ctx"),
    )
    own_vector = first_gain.shape[0]
    vector_grads = lax.dynamic_slice_in_dim(
        vector_grads, lax.axis_index("ctx") * own_vector, own_vector, 1
    )
    return (
        final_rows.reshape(group_seqs, block_len, width),
        token_loss.reshape(group_seqs, block_len),
        query_grad.reshape(group_seqs, block_len, width),
        input_grad.reshape(group_seqs, block_len, width),
        *weight_grads,
        *[vector_grads[row] for row in range(6)],
    )


def solution(mesh):
    placed = (
        P(("rep", "batch"), "ctx", None),
        P(("rep", "batch"), "ctx", None),
        P(("rep", "batch"), None),
        P("ctx"),
        P("ctx"),
        P("ctx"),
        P("ctx"),
        P("ctx"),
        P("ctx"),
        P("ctx", None),
        P("ctx", None),
        P("ctx", None),
        P("ctx", None),
        P(("batch", "ctx"), None),
        P(("batch", "ctx")),
        P(("rep", "batch"), "ctx", None),
        P("rep", ("batch", "ctx"), None, None, None),
        P(("rep", "batch"), "ctx"),
        P(("rep", "batch"), "ctx"),
    )
    return jax.shard_map(
        local,
        mesh=mesh,
        in_specs=placed,
        out_specs=(
            P(("rep", "batch"), "ctx", None),
            P(("rep", "batch"), "ctx"),
            P(("rep", "batch"), "ctx", None),
            P(("rep", "batch"), "ctx", None),
            P("ctx", None),
            P("ctx", None),
            P("ctx", None),
            P("ctx", None),
            P("ctx"),
            P("ctx"),
            P("ctx"),
            P("ctx"),
            P("ctx"),
            P("ctx"),
        ),
        check_vma=False,
    )
```

time: 2140 us -> 1400 us (0.65)
  matrix products: 557 us -> 111 us
  local copies, waits for them, and re-layouts: 368 us -> 52.7 us
  Pallas kernels: 0 us -> 179 us
  other arithmetic: 182 us -> 39.5 us
  blocking collectives: 82.4 us -> 182 us
  starting transfers between devices: 84.1 us -> 26 us
  waiting for transfers between devices: 830 us -> 786 us
    dot_general x6 -> x0, matrix products: 390 us -> none  [the longest x1 134 us: every_key(): jnp.einsum('hqk,qhd->khd', score_grad, split_heads(query_one, head_count)...]
    pallas_call x0 -> x7, Pallas kernels: none -> 179 us  [the longest x1 39.3 us: attend_back(): pl.pallas_call(functools.partial(attend_back_kernel, head_count), grid_sp...]
    all_to_all x0 -> x4, blocking collectives: none -> 110 us  [the longest x1 50 us: local(): lax.all_to_all(to_senders(stats), everyone, split_axis=0, concat_axis=0,...]
    all_gather x6 -> x7, waiting for transfers between devices: 202 us -> 113 us  [the longest x3 61.2 us: gather_weight(): return lax.all_gather(mine, ('ctx', 'rep'), axis=0, tiled=True)]
    unnamed x171 -> x134, local copies, waits for them, and re-layouts: 97.5 us -> 17 us
    eq x9 -> x0, local copies, waits for them, and re-layouts: 65.7 us -> none  [the longest x4 65 us: local(): within[:, :, None] == jnp.arange(spacing, dtype=jnp.int32)[None, None, :]]
    all_to_all x8 -> x5, starting transfers between devices: 83.4 us -> 25.5 us  [the longest x1 5.66 us: local(): lax.all_to_all(pack_any(final_rows, slot_map, capacity), everyone, split_...]
    broadcast_in_dim x7 -> x2, local copies, waits for them, and re-layouts: 56.3 us -> 1.32 us  [the longest x1 0.69 us: local(): jnp.broadcast_to(got_targets.reshape(stat_shape[0], 1, stat_shape[2]), st...]
  transfers between devices with their start and end apart: 20 -> 18, of which waited for: 11 -> 15; matrix products, arithmetic and copies ran while one was open for 26% -> 10% of each run, Pallas kernels for 0% -> 4%
where the time goes in v1:
time: 1400 us; the launch traced here: 1390 us
  waiting for transfers between devices  786 us (56%)
  blocking collectives  182 us (13%)
  Pallas kernels  179 us (13%)
  matrix products  111 us (8%)
  local copies, waits for them, and re-layouts  52.7 us (4%)
  other arithmetic  39.5 us (3%)
  starting transfers between devices  26 us (2%)
  between operations  15 us (1%)
    reduce_scatter x3, waiting for transfers between devices, scatter_grad(): lax.psum_scatter(grad.astype(jnp.bfloat16), ('ctx', 'rep'), scatter_dimen...  194 us
    all_to_all x1, waiting for transfers between devices, local(): lax.all_to_all(partial_grad, everyone, split_axis=0, concat_axis=0, tiled...  166 us
    all_to_all x1, waiting for transfers between devices, local(): lax.all_to_all(pack_any(final_rows, slot_map, capacity), everyone, split_...  161 us
    psum x1, waiting for transfers between devices, local(): lax.psum(piece, 'batch')  116 us
    all_gather x3, waiting for transfers between devices, gather_weight(): return lax.all_gather(mine, ('ctx', 'rep'), axis=0, tiled=True)  61.2 us
    all_to_all x1, blocking collectives, local(): lax.all_to_all(to_senders(stats), everyone, split_axis=0, concat_axis=0,...  50 us
    psum x1, blocking collectives, local(): lax.psum(jnp.stack([first_gain_grad, first_shift_grad, second_gain_grad,...  39.8 us
    dot_general x5, matrix products, left_dot(): lax.dot_general(left_side, right_side, (((0,), (0,)), ((), ())), preferre...  39.8 us
  transfers between devices with their start and end apart: 18, of which 15 were waited for; matrix products, arithmetic and copies ran while one was open for 10% of the time, Pallas kernels for 4%

profile of v1, /device:TPU:0, one launch (start us, length us, event | category | flops | bytes accessed | tf_op | source)
XLA Modules:
  0.0 1391.6 jit_solution(7969342643950116862)
XLA Ops:
  16.2 5.3 all-to-all-start
  24.0 30.3 %all_gather.28 = bf16[6,1024]{1,0:T(8,128)(2,1)S(1)} all-gather(bf16[6,256]{1,0:T(8,128)(2,1)S(1)} %stack.36), channel_id=1, replica_groups=mesh['rep'=2,'batch'=4,'ctx'=4] {'ctx'}, dimensions={1}, use_global_device_ids=true | all-gather | bytes 15360 | tf_op jit(solution)/shard_map/all_gather | solution.py:598
  57.1 29.6 %all-gather.21.cloned.1.call-done = bf16[1,2304,1024]{2,1,0:T(8,128)(2,1)} async-done(((bf16[1,576,1024]{2,1,0:T(8,128)(2,1)}), bf16[1,2304,1024]{2,1,0:T(8,128)(2,1)}) %all-gather.21.cloned.1.call-update) | async-done | bytes 4718608 | tf_op jit(solution)/shard_map/all_gather | solution.py:594
  91.8 5.0 convolution_convert_fusion.2
  99.3 35.4 %attend.1 = (bf16[2304,256]{1,0:T(8,128)(2,1)}, f32[8,2304]{1,0:T(8,128)}) custom-call(s32[9]{0:T(128)} %and_select_fusion.low_ref, bf16[2304,256]{1,0:T(8,128)(2,1)} %get-tuple-element.109.q_ref, bf16[2304,256]{1,0:T(8,128)(2,1)} %get-tuple-element.108.k_ref, bf16[2304,256]{1,0:T(8,128)(2,1)} %get-tuple-element.107.v_ref, s32[8,2304]{1,0:T(8,128)} %broadcast_in_dim.34.start_ref), custom_call_target="tpu_custom_call" | custom-call | flops 2717908992 | bytes 4718592 | tf_op jit(solution)/shard_map/attend/pallas_call | solution.py:124
  134.8 4.0 all-to-all-start.1
  141.9 12.5 all-to-all-done.1
  154.5 5.6 all-to-all-start.3
  160.3 3.5 fusion.45
  165.6 15.9 %all-gather.11.cloned.1.call-done = bf16[1024,4096]{1,0:T(8,128)(2,1)} async-done(((bf16[128,4096]{1,0:T(8,128)(2,1)}), bf16[1024,4096]{1,0:T(8,128)(2,1)}) %all-gather.11.cloned.1.call-update) | async-done | bytes 8388624 | tf_op jit(solution)/shard_map/all_gather | solution.py:612
  181.5 11.5 fusion.36
  193.0 45.3 %all-gather.13.cloned.1.call-done = bf16[4096,1024]{1,0:T(8,128)(2,1)} async-done(((bf16[512,1024]{1,0:T(8,128)(2,1)}), bf16[4096,1024]{1,0:T(8,128)(2,1)}) %all-gather.13.cloned.1.call-update) | async-done | bytes 8388624 | tf_op jit(solution)/shard_map/all_gather | solution.py:612
  238.3 12.6 fusion.46
  253.3 13.7 pack_rows.1
  267.0 5.7 all-to-all-start.2
  272.7 6.5 copy.96
  279.2 6.4 copy.100.keys_ref
  291.0 160.8 %all-to-all-done.2 = bf16[16,288,1024]{2,1,0:T(8,128)(2,1)} async-done(((bf16[16,288,1024]{2,1,0:T(8,128)(2,1)}), bf16[16,288,1024]{2,1,0:T(8,128)(2,1)}, u32[]{:S(2)}, u32[]{:S(2)}) %all-to-all-start.2) | async-done | bytes 9437216 | tf_op jit(solution)/shard_map/all_to_all | solution.py:671
  452.5 31.0 %near_scores.1 = (f32[4608,256]{1,0:T(8,128)}, f32[16,8,288]{2,1,0:T(8,128)}) custom-call(bf16[4608,1024]{1,0:T(8,128)(2,1)} %bitcast.16.q_ref, bf16[1024,2048]{1,0:T(8,128)(2,1)} %copy.100.keys_ref, f32[8,256]{1,0:T(8,128)} %bitcast.180, f32[8,256]{1,0:T(8,128)} %bitcast.181, s32[4608,256]{1,0:T(8,128)} %bitcast.198, f32[16,8,288]{2,1,0:T(8,128)} %broadcast_in_dim.39.target_ref), custom_call_target="tpu_custom_call" | custom-call | flops 19327352832 | bytes 23068672 | tf_op jit(solution)/shard_map/near_scores/pallas_call | solution.py:320
  483.5 50.0 %all_to_all.81.stats_ref = f32[16,8,288]{2,1,0:T(8,128)} all-to-all(f32[16,8,288]{2,1,0:T(8,128)} %get-tuple-element.24), channel_id=1, replica_groups=mesh['rep'=2,'batch'=4,'ctx'=4] {'batch','ctx'}, dimensions={0} | all-to-all | bytes 294912 | tf_op jit(solution)/shard_map/all_to_all | solution.py:703
  533.5 11.8 mix_losses.1
  545.3 12.4 all_to_all.82.coeff_ref
  557.8 27.7 %near_back.1 = bf16[4608,1024]{1,0:T(8,128)(2,1)} custom-call(f32[4608,256]{1,0:T(8,128)} %get-tuple-element.26.e_ref, s32[4608,256]{1,0:T(8,128)} %bitcast.199, f32[16,8,288]{2,1,0:T(8,128)} %all_to_all.82.coeff_ref, bf16[2048,1024]{1,0:T(8,128)(2,1)} %bitcast.141), custom_call_target="tpu_custom_call" | custom-call | flops 19327352832 | bytes 23068672 | tf_op jit(solution)/shard_map/near_back/pallas_call | solution.py:369
  585.5 4.9 all-to-all-start.6
  593.5 166.4 %all-to-all-done.6.back_ref = bf16[16,288,1024]{2,1,0:T(8,128)(2,1)} async-done(((bf16[16,288,1024]{2,1,0:T(8,128)(2,1)}), bf16[16,288,1024]{2,1,0:T(8,128)(2,1)}, u32[]{:S(2)}, u32[]{:S(2)}) %all-to-all-start.6) | async-done | bytes 9437216 | tf_op jit(solution)/shard_map/all_to_all | solution.py:711
  759.8 20.0 %unpack_rows.1 = f32[576,1024]{1,0:T(8,128)} custom-call(bf16[16,288,1024]{2,1,0:T(8,128)(2,1)} %all-to-all-done.6.back_ref, s32[16,576,1]{2,1,0:T(8,128)} %copy.101.column_ref), custom_call_target="tpu_custom_call" | custom-call | flops 5435817984 | bytes 9437184 | tf_op jit(solution)/shard_map/unpack_rows/pallas_call | solution.py:439
  779.9 3.4 multiply_reduce_fusion.1
  784.3 19.6 %fusion.15 = bf16[576,4096]{1,0:T(8,128)(2,1)} fusion(f32[576,4096]{1,0:T(8,128)} %fusion.36, bf16[4096,1024]{1,0:T(8,128)(2,1)} %all-gather.13.cloned.1.call-done, f32[576,1024]{1,0:T(8,128)S(1)} %get-tuple-element.105, f32[576]{0:T(1024)S(1)} %negate_multiply_fusion.2), kind=kOutput, calls=%fused_computation.22 | convolution fusion | flops 4880203776 | bytes 24905984 | tf_op jit(solution)/shard_map/dot_general | solution.py:37
  803.9 8.7 multiply_reduce_fusion.2
  816.6 30.4 %all_to_all.83 = bf16[576,4,256]{2,0,1:T(8,128)(2,1)} all-to-all(bf16[576,4,256]{2,0,1:T(8,128)(2,1)S(1)} %bitcast.149), channel_id=1, replica_groups=mesh['rep'=2,'batch'=4,'ctx'=4] {'ctx'}, dimensions={1} | all-to-all | bytes 2359296 | tf_op jit(solution)/shard_map/all_to_all | solution.py:729
  847.0 39.3 %attend_back.1 = (bf16[2304,256]{1,0:T(8,128)(2,1)}, bf16[2304,256]{1,0:T(8,128)(2,1)}, bf16[2304,256]{1,0:T(8,128)(2,1)}) custom-call(s32[9]{0:T(128)} %and_select_fusion.low_ref, bf16[2304,256]{1,0:T(8,128)(2,1)} %get-tuple-element.109.q_ref, bf16[2304,256]{1,0:T(8,128)(2,1)} %get-tuple-element.108.k_ref, bf16[2304,256]{1,0:T(8,128)(2,1)} %get-tuple-element.107.v_ref, ...), custom_call_target="tpu_custom_call" | custom-call | flops 6794772480 | bytes 9437184 | tf_op jit(solution)/shard_map/attend_back/pallas_call | solution.py:244
  888.7 9.3 convolution_convert_fusion.4
  900.6 17.3 %all_to_all.84 = bf16[4,256,768]{1,2,0:T(8,128)(2,1)S(1)} all-to-all(bf16[4,256,768]{1,2,0:T(8,128)(2,1)} %copy.103), channel_id=1, replica_groups=mesh['rep'=2,'batch'=4,'ctx'=4] {'ctx'}, dimensions={0} | all-to-all | bytes 3145728 | tf_op jit(solution)/shard_map/all_to_all | solution.py:763
  922.0 4.8 convolution_convert_fusion.3
  926.9 13.4 convolution_convert_fusion.1
  941.1 12.0 convolution_convert_fusion
  953.1 9.1 reduce-scatter.16.cloned.1.call-done
  964.4 43.7 %reduce-scatter.10.cloned.1.call-done = bf16[128,1024]{1,0:T(8,128)(2,1)} async-done(((bf16[1024,1024]{1,0:T(8,128)(2,1)}), bf16[128,1024]{1,0:T(8,128)(2,1)}) %reduce-scatter.10.cloned.1.call-update) | async-done | bytes 262160 | tf_op jit(solution)/shard_map/reduce_scatter | solution.py:759
  1008.1 74.7 %reduce-scatter.14.cloned.1.call-done = bf16[512,1024]{1,0:T(8,128)(2,1)} async-done(((bf16[4096,1024]{1,0:T(8,128)(2,1)}), bf16[512,1024]{1,0:T(8,128)(2,1)}) %reduce-scatter.14.cloned.1.call-update) | async-done | bytes 1048592 | tf_op jit(solution)/shard_map/reduce_scatter | solution.py:759
  1082.9 75.2 %reduce-scatter.12.cloned.1.call-done = bf16[128,4096]{1,0:T(8,128)(2,1)} async-done(((bf16[1024,4096]{1,0:T(8,128)(2,1)}), bf16[128,4096]{1,0:T(8,128)(2,1)}) %reduce-scatter.12.cloned.1.call-update) | async-done | bytes 1048592 | tf_op jit(solution)/shard_map/reduce_scatter | solution.py:759
  1158.2 9.4 fusion.39
  1167.6 115.8 %all-reduce.3.cloned.1.call-done = (bf16[128,3072]{0,1:T(8,128)(2,1)}, bf16[128,1024]{1,0:T(8,128)(2,1)}, bf16[128,4096]{1,0:T(8,128)(2,1)}, bf16[512,1024]{1,0:T(8,128)(2,1)}) async-done(((bf16[128,3072]{0,1:T(8,128)(2,1)}, bf16[128,1024]{1,0:T(8,128)(2,1)}, bf16[128,4096]{1,0:T(8,128)(2,1)}, bf16[512,1024]{1,0:T(8,128)(2,1)}), (bf16[128,3072]{0,1:T(8,128)(2,1)}, bf16[128,1024]{1,0:T(8,128)(2,1)}, ...) | async-done | bytes 3145744 | tf_op jit(solution)/shard_map/psum | solution.py:782
  1289.1 39.8 %psum.39 = f32[6,1024]{1,0:T(8,128)S(1)} all-reduce(f32[6,1024]{1,0:T(8,128)S(1)} %stack.37), channel_id=1, replica_groups=mesh['rep'=2,'batch'=4,'ctx'=4] {'rep','batch','ctx'}, use_global_device_ids=true, to_apply=%region_33.34 | all-reduce | flops 6144 | bytes 49152 | tf_op jit(solution)/shard_map/psum | solution.py:785
  1329.6 13.4 reduce-scatter.8.cloned.1.call-done
  1357.3 10.1 all-gather.17.cloned.1.call-done
  1367.4 4.2 convert_element_type.117
  1371.7 9.1 all-gather.19.cloned.1.call-done
  1380.7 4.1 convert_element_type.119
  (235 shorter events, 75.9 us)
Async XLA Ops:
  7.2 79.4 %all-gather.21.cloned.1.call-start = ((), (), s32[]{:S(2)}) async-start(), calls=%async_computation.24 | async-start | bytes 5898240 | tf_op jit(solution)/shard_map/all_gather | solution.py:594
  7.9 152.3 %all-gather.9.cloned.1.call-start = ((), (), s32[]{:S(2)}) async-start(), calls=%async_computation.14 | async-start | bytes 2359296 | tf_op jit(solution)/shard_map/all_gather | solution.py:612
  9.7 171.8 %all-gather.11.cloned.1.call-start = ((), (), s32[]{:S(2)}) async-start(), calls=%async_computation.15 | async-start | bytes 9437184 | tf_op jit(solution)/shard_map/all_gather | solution.py:612
  10.8 227.4 %all-gather.13.cloned.1.call-start = ((), (), s32[]{:S(2)}) async-start(), calls=%async_computation.16 | async-start | bytes 9437184 | tf_op jit(solution)/shard_map/all_gather | solution.py:612
  16.2 5.4 copy-start.59
  16.2 5.4 copy-start.60
  16.2 5.4 copy-start.47
  16.2 39.3 %all-to-all-start = ((bf16[4,256,3,256]{1,3,2,0:T(8,128)(2,1)}), bf16[4,256,3,256]{1,3,2,0:T(8,128)(2,1)S(1)}, u32[]{:S(2)}, u32[]{:S(2)}) async-start(bf16[4,256,3,256]{1,3,2,0:T(8,128)(2,1)} %copy.92), calls=%async_computation | async-start | bytes 3145728 | tf_op jit(solution)/shard_map/all_to_all | solution.py:601
  55.4 36.3 %copy-start.22 = (f32[1,1024]{1,0:T(1,128)}, f32[1,1024]{1,0:T(1,128)S(1)}, u32[]{:S(2)}) copy-start(f32[1,1024]{1,0:T(1,128)S(1)} %get-tuple-element.120) | copy-start | bytes 12292
  55.4 36.4 %copy-start.51 = (f32[1,1024]{1,0:T(1,128)}, f32[1,1024]{1,0:T(1,128)S(1)}, u32[]{:S(2)}) copy-start(f32[1,1024]{1,0:T(1,128)S(1)} %get-tuple-element.121) | copy-start | bytes 12292
  55.4 126.1 %copy-start.36 = (f32[1,1024]{1,0:T(1,128)}, f32[1,1024]{1,0:T(1,128)S(1)}, u32[]{:S(2)}) copy-start(f32[1,1024]{1,0:T(1,128)S(1)} %get-tuple-element.118) | copy-start | bytes 12292
  55.5 196.4 %copy-start.28 = (f32[1,1024]{1,0:T(1,128)}, f32[1,1024]{1,0:T(1,128)S(1)}, u32[]{:S(2)}) copy-start(f32[1,1024]{1,0:T(1,128)S(1)} %get-tuple-element.117) | copy-start | bytes 12292
  57.0 34.8 %copy-start.13 = (bf16[96,8,4,256]{3,1,2,0:T(8,128)(2,1)}, bf16[96,8,4,256]{3,1,2,0:T(8,128)(2,1)S(1)}, u32[]{:S(2)}) copy-start(bf16[96,8,4,256]{3,1,2,0:T(8,128)(2,1)S(1)} %copy.111) | copy-start | bytes 4718596
  134.8 25.5 %copy-start.2 = (bf16[1,576,1024]{2,1,0:T(8,128)(2,1)S(1)}, bf16[1,576,1024]{2,1,0:T(8,128)(2,1)}, u32[]{:S(2)}) copy-start(bf16[1,576,1024]{2,1,0:T(8,128)(2,1)} %param.19) | copy-start | bytes 3538948
  134.8 19.7 %all-to-all-start.1 = ((bf16[4,576,256]{2,1,0:T(8,128)(2,1)}), bf16[4,576,256]{2,1,0:T(8,128)(2,1)S(1)}, u32[]{:S(2)}, u32[]{:S(2)}) async-start(bf16[4,576,256]{2,1,0:T(8,128)(2,1)} %bitcast.155), calls=%async_computation.1 | async-start | bytes 2359296 | tf_op jit(solution)/shard_map/all_to_all | solution.py:662
  139.0 21.1 %copy-start.18 = (s32[16,576]{1,0:T(8,128)}, s32[16,576]{1,0:T(8,128)S(1)}, u32[]{:S(2)}) copy-start(s32[16,576]{1,0:T(8,128)S(1)} %fusion.27.map_ref) | copy-start | bytes 110596
  154.5 112.5 %all-to-all-start.3 = ((s32[16,1,288]{2,1,0:T(1,128)}), s32[16,1,288]{2,1,0:T(1,128)}, u32[]{:S(2)}, u32[]{:S(2)}) async-start(s32[16,1,288]{2,1,0:T(1,128)} %copy.99), calls=%async_computation.3 | async-start | bytes 49152 | tf_op jit(solution)/shard_map/all_to_all | solution.py:628
  163.8 17.7 %copy-start.49 = (f32[1,1024]{1,0:T(1,128)S(1)}, f32[1,1024]{1,0:T(1,128)}, u32[]{:S(2)}) copy-start(f32[1,1024]{1,0:T(1,128)} %get-tuple-element.119) | copy-start | bytes 12292
  163.8 29.2 %copy-start.29 = (f32[576]{0:T(1024)}, f32[576]{0:T(1024)S(1)}, u32[]{:S(2)}) copy-start(f32[576]{0:T(1024)S(1)} %broadcast_multiply_fusion.3) | copy-start | bytes 6916
  165.6 27.4 %copy-start.32 = (f32[576]{0:T(1024)}, f32[576]{0:T(1024)S(1)}, u32[]{:S(2)}) copy-start(f32[576]{0:T(1024)S(1)} %multiply_reduce_fusion.6) | copy-start | bytes 6916
  165.6 27.4 %copy-start.39 = (f32[576]{0:T(1024)}, f32[576]{0:T(1024)S(1)}, u32[]{:S(2)}) copy-start(f32[576]{0:T(1024)S(1)} %fusion.32) | copy-start | bytes 6916
  267.0 184.9 %all-to-all-start.2 = ((bf16[16,288,1024]{2,1,0:T(8,128)(2,1)}), bf16[16,288,1024]{2,1,0:T(8,128)(2,1)}, u32[]{:S(2)}, u32[]{:S(2)}) async-start(bf16[16,288,1024]{2,1,0:T(8,128)(2,1)} %pack_rows.1), calls=%async_computation.2 | async-start | bytes 18874368 | tf_op jit(solution)/shard_map/all_to_all | solution.py:671
  585.5 174.3 %all-to-all-start.6 = ((bf16[16,288,1024]{2,1,0:T(8,128)(2,1)}), bf16[16,288,1024]{2,1,0:T(8,128)(2,1)}, u32[]{:S(2)}, u32[]{:S(2)}) async-start(bf16[16,288,1024]{2,1,0:T(8,128)(2,1)} %bitcast.143), calls=%async_computation.6 | async-start | bytes 18874368 | tf_op jit(solution)/shard_map/all_to_all | solution.py:711
  590.4 371.7 %reduce-scatter.16.cloned.1.call-start = ((), (), s32[]{:S(2)}) async-start(), calls=%async_computation.25 | async-start | bytes 2359296
  593.5 186.4 %copy-start.12 = (bf16[1,576,1024]{2,1,0:T(8,128)(2,1)S(1)}, bf16[1,576,1024]{2,1,0:T(8,128)(2,1)}, u32[]{:S(2)}) copy-start(bf16[1,576,1024]{2,1,0:T(8,128)(2,1)} %param.20) | copy-start | bytes 3538948
  783.3 20.6 %slice-start = ((s8[8388608]{0:T(1024)(128)(4,1)}), s8[4194304]{0:T(1024)(128)(4,1)S(1)}, s32[]{:S(2)}) async-start(s8[8388608]{0:T(1024)(128)(4,1)} %bitcast.196), calls=%async_computation.27 | async-start | bytes 8388608
  784.2 29.3 %copy-start.11 = (f32[576,1024]{1,0:T(8,128)}, f32[576,1024]{1,0:T(8,128)S(1)}, u32[]{:S(2)}) copy-start(f32[576,1024]{1,0:T(8,128)S(1)} %get-tuple-element.105) | copy-start | bytes 7077892
  784.2 29.3 %copy-start.42 = (f32[576]{0:T(1024)}, f32[576]{0:T(1024)S(1)}, u32[]{:S(2)}) copy-start(f32[576]{0:T(1024)S(1)} %negate_multiply_fusion.2) | copy-start | bytes 6916
  784.2 19.7 %copy-start.8 = (f32[576,1024]{1,0:T(8,128)S(1)}, f32[576,1024]{1,0:T(8,128)}, u32[]{:S(2)}) copy-start(f32[576,1024]{1,0:T(8,128)} %copy-done.7) | copy-start | bytes 7077892
  784.2 19.7 %copy-start.30 = (f32[576]{0:T(1024)S(1)}, f32[576]{0:T(1024)}, u32[]{:S(2)}) copy-start(f32[576]{0:T(1024)} %copy-done.29) | copy-start | bytes 6916
  784.2 19.7 %copy-start.37 = (f32[1,1024]{1,0:T(1,128)S(1)}, f32[1,1024]{1,0:T(1,128)}, u32[]{:S(2)}) copy-start(f32[1,1024]{1,0:T(1,128)} %copy-done.36) | copy-start | bytes 12292
  784.2 19.7 %copy-start.40 = (f32[576]{0:T(1024)S(1)}, f32[576]{0:T(1024)}, u32[]{:S(2)}) copy-start(f32[576]{0:T(1024)} %copy-done.39) | copy-start | bytes 6916
  784.3 19.7 %slice-start.1 = ((s8[8388608]{0:T(1024)(128)(4,1)}), s8[4194304]{0:T(1024)(128)(4,1)S(1)}, s32[]{:S(2)}) async-start(s8[8388608]{0:T(1024)(128)(4,1)} %bitcast.196), calls=%async_computation.28 | async-start | bytes 8388608
  803.9 8.7 copy-start.33
  888.7 9.3 copy-start.20
  921.9 86.2 %reduce-scatter.10.cloned.1.call-start = ((), (), s32[]{:S(2)}) async-start(), calls=%async_computation.19 | async-start | bytes 2359296 | tf_op jit(solution)/shard_map/reduce_scatter | solution.py:759
  926.9 156.0 %reduce-scatter.14.cloned.1.call-start = ((), (), s32[]{:S(2)}) async-start(), calls=%async_computation.22 | async-start | bytes 9437184 | tf_op jit(solution)/shard_map/reduce_scatter | solution.py:759
  940.4 217.7 %reduce-scatter.12.cloned.1.call-start = ((), (), s32[]{:S(2)}) async-start(), calls=%async_computation.20 | async-start | bytes 9437184 | tf_op jit(solution)/shard_map/reduce_scatter | solution.py:759
  953.0 205.1 %copy-start.27 = (f32[2304]{0:T(1024)S(1)}, f32[2304]{0:T(1024)}, u32[]{:S(2)}) copy-start(f32[2304]{0:T(1024)} %copy-done.25) | copy-start | bytes 27652
  953.0 205.1 %copy-start.45 = (f32[2304]{0:T(1024)S(1)}, f32[2304]{0:T(1024)}, u32[]{:S(2)}) copy-start(f32[2304]{0:T(1024)} %copy-done.43) | copy-start | bytes 27652
  953.1 330.4 %all-reduce.3.cloned.1.call-start = ((), (), s32[]{:S(2)}) async-start(), calls=%async_computation.26 | async-start | bytes 6291456 | tf_op jit(solution)/shard_map/psum | solution.py:782
  1158.1 184.9 %reduce-scatter.8.cloned.1.call-start = ((), (), s32[]{:S(2)}) async-start(), calls=%async_computation.17 | async-start | bytes 5898240 | tf_op jit(solution)/shard_map/reduce_scatter | solution.py:752
  1167.5 116.5 %copy-start.3 = (bf16[1,576,1024]{2,1,0:T(8,128)(2,1)S(1)}, bf16[1,576,1024]{2,1,0:T(8,128)(2,1)}, u32[]{:S(2)}) copy-start(bf16[1,576,1024]{2,1,0:T(8,128)(2,1)} %param.19) | copy-start | bytes 3538948
  1167.5 186.7 %all-gather.15.cloned.1.call-start = ((), (), s32[]{:S(2)}) async-start(), calls=%async_computation.18 | async-start | bytes 2359296 | tf_op jit(solution)/shard_map/all_gather | solution.py:782
  1283.4 84.0 %all-gather.17.cloned.1.call-start = ((), (), s32[]{:S(2)}) async-start(), calls=%async_computation.21 | async-start | bytes 3145728 | tf_op jit(solution)/shard_map/all_gather | solution.py:782
  1284.0 96.7 %all-gather.19.cloned.1.call-start = ((), (), s32[]{:S(2)}) async-start(), calls=%async_computation.23 | async-start | bytes 3145728 | tf_op jit(solution)/shard_map/all_gather | solution.py:782
  1288.3 56.9 %copy-start.24 = (f32[576]{0:T(1024)S(1)}, f32[576]{0:T(1024)}, u32[]{:S(2)}) copy-start(f32[576]{0:T(1024)} %broadcast_multiply_fusion.1) | copy-start | bytes 6916
  1367.4 17.4 %copy-start.1 = (bf16[256,4096]{1,0:T(8,128)(2,1)S(1)}, bf16[256,4096]{1,0:T(8,128)(2,1)}, u32[]{:S(2)}) copy-start(bf16[256,4096]{1,0:T(8,128)(2,1)} %param.30) | copy-start | bytes 6291460
  (33 other events, 87.4 us)
Sparse Core Ops, SparseCore 0:
  9.9 76.6 all-gather.20
  89.1 27.9 all-gather.8
  119.5 61.9 all-gather.10
  183.8 54.3 all-gather.12
  922.1 40.0 reduce-scatter.15
  965.6 42.4 reduce-scatter.9
  1011.6 71.2 reduce-scatter.13
  1086.7 71.2 reduce-scatter.11
  1161.3 122.1 all-reduce.2
  1286.2 56.6 reduce-scatter.7
  1344.5 9.6 all-gather.14
  1355.6 11.7 all-gather.16
  1369.0 11.7 all-gather.18

commit v2 on v1

v2 whole, which is shorter than its diff:
```python
import functools

import jax
import jax.numpy as jnp
from jax import lax
from jax.experimental import pallas as pl
from jax.experimental.pallas import tpu as pltpu
from jax.sharding import PartitionSpec as P

HEADS = 16


norm_eps = 1e-05
mix_weight = 0.25
masked_value = -1e30
vmem_limit = 60 * 1024 * 1024
small_cost = pl.CostEstimate(flops=1000, bytes_accessed=1000, transcendentals=0)


def norm_rows(values, scale_gain, shift_term):
    average = jnp.mean(values, axis=-1, keepdims=True)
    centred = values - average
    spread = jnp.mean(centred * centred, axis=-1, keepdims=True)
    return centred * lax.rsqrt(spread + norm_eps) * scale_gain + shift_term


def row_dot(left_side, right_side):
    return jnp.dot(left_side, right_side, preferred_element_type=jnp.float32)


def left_dot(left_side, right_side):
    return lax.dot_general(
        left_side, right_side, (((0,), (0,)), ((), ())), preferred_element_type=jnp.float32
    )


def right_dot(left_side, right_side):
    return lax.dot_general(
        left_side, right_side, (((1,), (1,)), ((), ())), preferred_element_type=jnp.float32
    )


def spec(shape, index_map):
    return pl.BlockSpec(shape, index_map)


def kernel_params(dims=1):
    return pltpu.CompilerParams(
        vmem_limit_bytes=vmem_limit, dimension_semantics=("arbitrary",) * dims
    )


def later(kernel, place, count):
    return lambda *refs: kernel(*refs[:place], *refs[place + count :])


def later_specs(after):
    return [pl.BlockSpec(memory_space=pl.ANY)] * len(after)


def run_after(arrays, after):
    def kernel(*refs):
        pass

    return pl.pallas_call(
        kernel,
        in_specs=later_specs((*arrays, *after)),
        out_specs=later_specs(arrays),
        out_shape=[jax.ShapeDtypeStruct(rows.shape, rows.dtype) for rows in arrays],
        input_output_aliases={place: place for place in range(len(arrays))},
        cost_estimate=small_cost,
        name="run_after",
    )(*arrays, *after)


def place_kernel(count, start_ref, *refs):
    for place in range(count):

        @pl.when(pl.program_id(0) == place)
        def _():
            refs[count][...] = refs[place][...]


def place_rows(pieces, places):
    count = len(pieces)
    rows, width = pieces[0].shape
    return pl.pallas_call(
        functools.partial(place_kernel, count),
        grid_spec=pltpu.PrefetchScalarGridSpec(
            num_scalar_prefetch=1,
            grid=(count,),
            in_specs=[spec((rows, width), lambda i, places: (0, 0))] * count,
            out_specs=spec((rows, width), lambda i, places: (places[i], 0)),
        ),
        out_shape=jax.ShapeDtypeStruct((count * rows, width), pieces[0].dtype),
        compiler_params=kernel_params(),
        cost_estimate=small_cost,
        name="place_rows",
    )(places, *pieces)


def head_rows(head, size):
    return slice(head * size, (head + 1) * size)


def masked_heads(block, head_count, axis):
    size = block.shape[axis] // head_count
    index = lax.broadcasted_iota(jnp.int32, block.shape, axis) // size
    zero = jnp.zeros((), block.dtype)
    return [jnp.where(index == head, block, zero) for head in range(head_count)]


def block_mask(key_block, query_block, size, start_row):
    key_pos = key_block * size + lax.broadcasted_iota(jnp.int32, (size, size), 0)
    query_pos = query_block * size + lax.broadcasted_iota(jnp.int32, (size, size), 1)
    return (key_pos <= query_pos) & (key_pos >= start_row)


def attend_kernel(
    head_count, low_ref, q_ref, k_ref, v_ref, start_ref, o_ref, lse_ref, vt_ref, acc_ref
):
    step = pl.program_id(0)
    size, width = q_ref.shape
    head_size = width // head_count
    blocks = k_ref.shape[0] // size

    @pl.when(step == 0)
    def _():
        for block in range(blocks):
            rows = slice(block * size, (block + 1) * size)
            vt_ref[:, rows] = v_ref[rows, :].astype(jnp.float32).T.astype(jnp.bfloat16)

    scaled = q_ref[...].astype(jnp.float32) * (head_size ** (-0.5))
    turned = jnp.concatenate(
        [part.astype(jnp.bfloat16) for part in masked_heads(scaled.T, head_count, 0)], axis=1
    )
    start_row = start_ref[0:1, :]
    acc_ref[...] = jnp.zeros_like(acc_ref)
    first = (
        jnp.full((1, head_count * size), masked_value, jnp.float32),
        jnp.zeros((1, head_count * size), jnp.float32),
    )

    def body(masked, block, state):
        peak, total = state
        rows = pl.ds(pl.multiple_of(block * size, size), size)
        scores = row_dot(k_ref[rows, :], turned)
        if masked:
            allowed = block_mask(block, step, size, start_row)
            scores = jnp.concatenate(
                [
                    jnp.where(allowed, scores[:, head * size : (head + 1) * size], masked_value)
                    for head in range(head_count)
                ],
                axis=1,
            )
        new_peak = jnp.maximum(peak, jnp.max(scores, axis=0, keepdims=True))
        fade = jnp.exp(peak - new_peak)
        weights = jnp.exp(scores - new_peak)
        total = total * fade + jnp.sum(weights, axis=0, keepdims=True)
        weights = weights.astype(jnp.bfloat16)
        for head in range(head_count):
            part = head_rows(head, head_size)
            lanes = slice(head * size, (head + 1) * size)
            acc_ref[part, :] = acc_ref[part, :] * fade[:, lanes] + row_dot(
                vt_ref[part, rows], weights[:, lanes]
            )
        return new_peak, total

    low = low_ref[step]
    inner = low_ref[blocks + step]
    state = lax.fori_loop(low, inner, functools.partial(body, True), first)
    state = lax.fori_loop(inner, step, functools.partial(body, False), state)
    peak, total = body(True, step, state)
    for head in range(head_count):
        part = head_rows(head, head_size)
        lanes = slice(head * size, (head + 1) * size)
        acc_ref[part, :] = acc_ref[part, :] / total[:, lanes]
        lse_ref[head : head + 1, :] = peak[:, lanes] + jnp.log(total[:, lanes])
    o_ref[...] = acc_ref[...].T.astype(jnp.bfloat16)


def with_inner(low_blocks, start_rows, size):
    last = start_rows[0, size - 1 :: size]
    inner = jnp.minimum(-(-last // size), jnp.arange(low_blocks.shape[0], dtype=jnp.int32))
    return jnp.concatenate([low_blocks, inner])


def attend(query, key, value, start_rows, low_blocks, head_count, size, after=()):
    length, width = query.shape
    blocks = length // size
    stat_rows = -(-head_count // 8) * 8
    return pl.pallas_call(
        later(functools.partial(attend_kernel, head_count), 5, len(after)),
        grid_spec=pltpu.PrefetchScalarGridSpec(
            num_scalar_prefetch=1,
            grid=(blocks,),
            in_specs=[
                spec((size, width), lambda i, low: (i, 0)),
                spec((length, width), lambda i, low: (0, 0)),
                spec((length, width), lambda i, low: (0, 0)),
                spec((8, size), lambda i, low: (0, i)),
                *later_specs(after),
            ],
            out_specs=[
                spec((size, width), lambda i, low: (i, 0)),
                spec((stat_rows, size), lambda i, low: (0, i)),
            ],
            scratch_shapes=[
                pltpu.VMEM((width, length), jnp.bfloat16),
                pltpu.VMEM((width, size), jnp.float32),
            ],
        ),
        out_shape=[
            jax.ShapeDtypeStruct((length, width), jnp.bfloat16),
            jax.ShapeDtypeStruct((stat_rows, length), jnp.float32),
        ],
        compiler_params=kernel_params(),
        cost_estimate=pl.CostEstimate(
            flops=20_000_000_000, bytes_accessed=1000, transcendentals=0
        ),
        name="attend",
    )(with_inner(low_blocks, start_rows, size), query, key, value, start_rows, *after)


def attend_back_kernel(
    head_count,
    low_ref,
    q_ref,
    k_ref,
    v_ref,
    grad_ref,
    o_ref,
    lse_ref,
    start_ref,
    dq_ref,
    dk_ref,
    dv_ref,
    kt_ref,
    dkey_ref,
    dvalue_ref,
    dqt_ref,
    score_ref,
    weight_ref,
):
    step = pl.program_id(0)
    size, width = q_ref.shape
    head_size = width // head_count
    score_scale = head_size ** (-0.5)
    blocks = k_ref.shape[0] // size

    @pl.when(step == 0)
    def _():
        dkey_ref[...] = jnp.zeros_like(dkey_ref)
        dvalue_ref[...] = jnp.zeros_like(dvalue_ref)
        for block in range(blocks):
            rows = slice(block * size, (block + 1) * size)
            kt_ref[:, rows] = k_ref[rows, :].astype(jnp.float32).T.astype(jnp.bfloat16)

    scaled = q_ref[...].astype(jnp.float32) * score_scale
    grads = grad_ref[...].astype(jnp.float32)
    dots = (grads * o_ref[...].astype(jnp.float32)).T
    query_turned = [p.astype(jnp.bfloat16) for p in masked_heads(scaled.T, head_count, 0)]
    grad_turned = [p.astype(jnp.bfloat16) for p in masked_heads(grads.T, head_count, 0)]
    query_stack = jnp.concatenate(
        [p.astype(jnp.bfloat16) for p in masked_heads(scaled, head_count, 1)], axis=0
    )
    grad_stack = jnp.concatenate(
        [p.astype(jnp.bfloat16) for p in masked_heads(grads, head_count, 1)], axis=0
    )
    row_dots = [
        jnp.sum(dots[head_rows(head, head_size), :], axis=0, keepdims=True)
        for head in range(head_count)
    ]
    start_row = start_ref[0:1, :]
    dqt_ref[...] = jnp.zeros_like(dqt_ref)

    query_wide = jnp.concatenate(query_turned, axis=1)
    grad_wide = jnp.concatenate(grad_turned, axis=1)
    row_wide = jnp.concatenate(row_dots, axis=1)
    lse_wide = jnp.concatenate([lse_ref[head : head + 1, :] for head in range(head_count)], axis=1)

    def body(masked, block, carry):
        rows = pl.ds(pl.multiple_of(block * size, size), size)
        scores = row_dot(k_ref[rows, :], query_wide)
        if masked:
            allowed = block_mask(block, step, size, start_row)
            scores = jnp.concatenate(
                [
                    jnp.where(allowed, scores[:, head * size : (head + 1) * size], masked_value)
                    for head in range(head_count)
                ],
                axis=1,
            )
        weights = jnp.exp(scores - lse_wide)
        weight_grad = row_dot(v_ref[rows, :], grad_wide)
        score_grad = (weights * (weight_grad - row_wide)).astype(jnp.bfloat16)
        weights = weights.astype(jnp.bfloat16)
        for head in range(head_count):
            part = head_rows(head, head_size)
            lanes = slice(head * size, (head + 1) * size)
            dqt_ref[part, :] += row_dot(kt_ref[part, rows], score_grad[:, lanes])
        dkey_ref[rows, :] += row_dot(score_grad, query_stack)
        dvalue_ref[rows, :] += row_dot(weights, grad_stack)
        return carry

    low = low_ref[step]
    inner = low_ref[blocks + step]
    lax.fori_loop(low, inner, functools.partial(body, True), 0)
    lax.fori_loop(inner, step, functools.partial(body, False), 0)
    body(True, step, 0)
    dq_ref[...] = (dqt_ref[...] * score_scale).T.astype(jnp.bfloat16)

    @pl.when(step == blocks - 1)
    def _():
        dk_ref[...] = dkey_ref[...].astype(jnp.bfloat16)
        dv_ref[...] = dvalue_ref[...].astype(jnp.bfloat16)


def attend_back(
    query, key, value, grad, attended, lse, start_rows, low_blocks, head_count, size, after=()
):
    length, width = query.shape
    blocks = length // size
    stat_rows = lse.shape[0]
    block_spec = spec((size, width), lambda i, low: (i, 0))
    whole_spec = spec((length, width), lambda i, low: (0, 0))
    return pl.pallas_call(
        later(functools.partial(attend_back_kernel, head_count), 8, len(after)),
        grid_spec=pltpu.PrefetchScalarGridSpec(
            num_scalar_prefetch=1,
            grid=(blocks,),
            in_specs=[
                block_spec,
                whole_spec,
                whole_spec,
                block_spec,
                block_spec,
                spec((stat_rows, size), lambda i, low: (0, i)),
                spec((8, size), lambda i, low: (0, i)),
                *later_specs(after),
            ],
            out_specs=[block_spec, whole_spec, whole_spec],
            scratch_shapes=[
                pltpu.VMEM((width, length), jnp.bfloat16),
                pltpu.VMEM((length, width), jnp.float32),
                pltpu.VMEM((length, width), jnp.float32),
                pltpu.VMEM((width, size), jnp.float32),
                pltpu.VMEM((size, head_count * size), jnp.bfloat16),
                pltpu.VMEM((size, head_count * size), jnp.bfloat16),
            ],
        ),
        out_shape=[jax.ShapeDtypeStruct((length, width), jnp.bfloat16)] * 3,
        compiler_params=kernel_params(),
        cost_estimate=small_cost,
        name="attend_back",
    )(with_inner(low_blocks, start_rows, size), query, key, value, grad, attended, lse, start_rows, *after)


def project_kernel(count, own_width, order_ref, *refs):
    block_refs, weight_refs, vector_ref = refs[:count], refs[count : 2 * count], refs[2 * count]
    weight_ref, plain_ref, normed_ref, q_ref, k_ref, v_ref = refs[2 * count + 1 :]
    piece = weight_refs[0].shape[0]

    @pl.when(pl.program_id(0) == 0)
    def _():
        for place in range(count):
            rows = pl.ds(pl.multiple_of(order_ref[place] * piece, piece), piece)
            weight_ref[rows, :] = weight_refs[place][:, : 3 * own_width]

    for place in range(count):

        @pl.when(pl.program_id(0) == place)
        def _():
            rows = norm_rows(block_refs[place][...].astype(jnp.float32), 1.0, 0.0)
            plain_ref[...] = rows.astype(jnp.bfloat16)
            normed = (rows * vector_ref[0:1, :] + vector_ref[1:2, :]).astype(jnp.bfloat16)
            normed_ref[...] = normed
            projected = row_dot(normed, weight_ref[...]).astype(jnp.bfloat16)
            q_ref[...] = projected[:, :own_width]
            k_ref[...] = projected[:, own_width : 2 * own_width]
            v_ref[...] = projected[:, 2 * own_width :]


def project_rows(blocks, weights, order, vectors):
    count = len(blocks)
    size, width = blocks[0].shape
    weight_rows = weights[0].shape[0]
    own_width = width // count
    whole = lambda shape: spec(shape, lambda i, order: (0, 0))
    placed = lambda columns: spec((size, columns), lambda i, order: (order[i], 0))
    return pl.pallas_call(
        functools.partial(project_kernel, count, own_width),
        grid_spec=pltpu.PrefetchScalarGridSpec(
            num_scalar_prefetch=1,
            grid=(count,),
            in_specs=[
                *[whole((size, width))] * count,
                *[whole(weights[0].shape)] * count,
                whole(vectors.shape),
            ],
            out_specs=[whole((width, 3 * own_width))]
            + [placed(width)] * 2
            + [placed(own_width)] * 3,
        ),
        out_shape=[jax.ShapeDtypeStruct((width, 3 * own_width), jnp.bfloat16)]
        + [jax.ShapeDtypeStruct((count * size, width), jnp.bfloat16)] * 2
        + [jax.ShapeDtypeStruct((count * size, own_width), jnp.bfloat16)] * 3,
        compiler_params=kernel_params(),
        cost_estimate=pl.CostEstimate(
            flops=13_000_000_000, bytes_accessed=1000, transcendentals=0
        ),
        name="project_rows",
    )(order, *blocks, *weights, vectors)


def to_columns(block, rows):
    parts = [block[group].T for group in range(block.shape[0])]
    return parts[0] if len(parts) == 1 else jnp.concatenate(parts, axis=0)


def near_kernel(spacing, dist_scale, parts, *refs):
    order_ref, query_ref, keys_ref, square_ref, values_ref = refs[:5]
    near_refs, target_refs = refs[5 : 5 + parts], refs[5 + parts : 5 + 2 * parts]
    e_ref, s_ref = refs[5 + 2 * parts :]
    piece, near_count = near_refs[0].shape[1:]
    rows = parts * piece
    lane = lax.broadcasted_iota(jnp.int32, (rows, near_count), 1)
    near = jnp.concatenate([ref[0] for ref in near_refs], axis=0)
    offset = near - spacing * lane
    target = jnp.concatenate([ref[0].T for ref in target_refs], axis=0)[:, 0:1]
    picked = jnp.zeros((rows, near_count), jnp.float32)
    words = jnp.full((rows, near_count), -1.0, jnp.float32)
    queries = query_ref[...]
    for plane in range(spacing):
        lanes = slice(plane * near_count, (plane + 1) * near_count)
        inner = row_dot(queries, keys_ref[:, lanes])
        chosen = offset == plane
        picked = jnp.where(chosen, 2.0 * inner - square_ref[plane : plane + 1, :], picked)
        words = jnp.where(chosen, values_ref[plane : plane + 1, :], words)
    scores = picked * dist_scale
    matched = words == target
    peak = jnp.max(scores, axis=1, keepdims=True)
    raised = jnp.exp(scores - peak)
    total = jnp.sum(raised, axis=1, keepdims=True)
    hits = jnp.sum(jnp.where(matched, raised, 0.0), axis=1, keepdims=True)
    e_ref[...] = jnp.where(matched, raised, -raised)
    stat_lane = lax.broadcasted_iota(jnp.int32, (rows, 128), 1)
    stats = jnp.where(stat_lane == 0, peak, jnp.where(stat_lane == 1, total, hits))
    for part in range(parts):
        s_ref[part] = stats[part * piece : (part + 1) * piece, :].T[: s_ref.shape[1], :]


def picked_specs(shape, parts):
    return [
        spec((1,) + shape, functools.partial(lambda part, i, order: (order[i * parts + part], 0, 0), part))
        for part in range(parts)
    ]


def near_scores(queries, keys_turned, square, values, near, target_rows, order, parts, spacing):
    stat_rows, piece = target_rows.shape[1:]
    near_count = near.shape[2]
    slot_rows = queries.shape[0]
    width, keys = keys_turned.shape
    rows = parts * piece
    return pl.pallas_call(
        functools.partial(near_kernel, spacing, width ** (-0.5), parts),
        grid_spec=pltpu.PrefetchScalarGridSpec(
            num_scalar_prefetch=1,
            grid=(slot_rows // rows,),
            in_specs=[
                spec((rows, width), lambda i, order: (i, 0)),
                spec((width, keys), lambda i, order: (0, 0)),
                spec((spacing, near_count), lambda i, order: (0, 0)),
                spec((spacing, near_count), lambda i, order: (0, 0)),
            ]
            + picked_specs((piece, near_count), parts)
            + picked_specs((stat_rows, piece), parts),
            out_specs=[
                spec((rows, near_count), lambda i, order: (i, 0)),
                spec((parts, stat_rows, piece), lambda i, order: (i, 0, 0)),
            ],
        ),
        out_shape=[
            jax.ShapeDtypeStruct((slot_rows, near_count), jnp.float32),
            jax.ShapeDtypeStruct((slot_rows // piece, stat_rows, piece), jnp.float32),
        ],
        compiler_params=kernel_params(),
        cost_estimate=small_cost,
        name="near_scores",
    )(order, queries, keys_turned, square, values, *[near] * parts, *[target_rows] * parts)


def near_back_kernel(spacing, factor, parts, *refs):
    order_ref, e_ref = refs[:2]
    near_refs, coeff_refs = refs[2 : 2 + parts], refs[2 + parts : 2 + 2 * parts]
    keys_ref, out_ref, dense_ref = refs[2 + 2 * parts :]
    piece, near_count = near_refs[0].shape[1:]
    lane = lax.broadcasted_iota(jnp.int32, (piece, near_count), 1)
    for part in range(parts):
        rows = slice(part * piece, (part + 1) * piece)
        offset = near_refs[part][0] - spacing * lane
        columns = coeff_refs[part][0].T
        coefficient, probability = columns[:, 0:1], columns[:, 1:2]
        marked = e_ref[rows, :]
        matched = jnp.where(marked > 0.0, 1.0, 0.0)
        grads = coefficient * (matched - probability) * jnp.abs(marked) * factor
        for plane in range(spacing):
            lanes = slice(plane * near_count, (plane + 1) * near_count)
            dense_ref[rows, lanes] = jnp.where(offset == plane, grads, 0.0).astype(jnp.bfloat16)
    out_ref[...] = row_dot(dense_ref[...], keys_ref[...]).astype(out_ref.dtype)


def near_back(marked, near, coeff_rows, keys_planes, order, parts, spacing, after=()):
    stat_rows, piece = coeff_rows.shape[1:]
    slot_rows, near_count = marked.shape
    keys, width = keys_planes.shape
    rows = parts * piece
    return pl.pallas_call(
        later(
            functools.partial(near_back_kernel, spacing, 2.0 * width ** (-0.5), parts),
            3 + 2 * parts,
            len(after),
        ),
        grid_spec=pltpu.PrefetchScalarGridSpec(
            num_scalar_prefetch=1,
            grid=(slot_rows // rows,),
            in_specs=[spec((rows, near_count), lambda i, order: (i, 0))]
            + picked_specs((piece, near_count), parts)
            + picked_specs((stat_rows, piece), parts)
            + [spec((keys, width), lambda i, order: (0, 0))]
            + later_specs(after),
            out_specs=spec((rows, width), lambda i, order: (i, 0)),
            scratch_shapes=[pltpu.VMEM((rows, keys), jnp.bfloat16)],
        ),
        out_shape=jax.ShapeDtypeStruct((slot_rows, width), jnp.bfloat16),
        compiler_params=kernel_params(),
        cost_estimate=small_cost,
        name="near_back",
    )(order, marked, *[near] * parts, *[coeff_rows] * parts, keys_planes, *after)


def pack_kernel(options, pick_ref, *refs):
    row_refs, (map_ref, out_ref, chosen_ref) = refs[:options], refs[options:]
    owners, capacity = out_ref.shape[:2]
    tokens = map_ref.shape[1]

    @pl.when(pl.program_id(0) == 0)
    def _():
        slot = lax.broadcasted_iota(jnp.int32, (capacity, tokens), 0)
        for owner in range(owners):
            chosen = jnp.where(map_ref[owner : owner + 1, :] == slot, 1.0, 0.0)
            chosen_ref[owner * capacity : (owner + 1) * capacity, :] = chosen.astype(jnp.bfloat16)

    rows = row_refs[0][...]
    for place in range(1, options):
        rows = jnp.where(pick_ref[0] == place, row_refs[place][...], rows)
    packed = row_dot(chosen_ref[...], rows).astype(out_ref.dtype)
    out_ref[...] = packed.reshape(out_ref.shape)


def pack_rows(options, pick, slot_map, capacity, after=()):
    owners, tokens = slot_map.shape
    width = options[0].shape[1]
    columns = row_chunk(width, (256,))
    return pl.pallas_call(
        later(functools.partial(pack_kernel, len(options)), 2 + len(options), len(after)),
        grid_spec=pltpu.PrefetchScalarGridSpec(
            num_scalar_prefetch=1,
            grid=(width // columns,),
            in_specs=[
                *[spec((tokens, columns), lambda i, pick: (0, i))] * len(options),
                spec((owners, tokens), lambda i, pick: (0, 0)),
                *later_specs(after),
            ],
            out_specs=spec((owners, capacity, columns), lambda i, pick: (0, 0, i)),
            scratch_shapes=[pltpu.VMEM((owners * capacity, tokens), jnp.bfloat16)],
        ),
        out_shape=jax.ShapeDtypeStruct((owners, capacity, width), options[0].dtype),
        compiler_params=kernel_params(),
        cost_estimate=small_cost,
        name="pack_rows",
    )(pick, *options, slot_map, *after)


def unpack_kernel(back_ref, column_ref, out_ref, chosen_ref):
    owners, capacity, columns = back_ref.shape
    tokens = out_ref.shape[0]

    @pl.when(pl.program_id(0) == 0)
    def _():
        slot = lax.broadcasted_iota(jnp.int32, (capacity, tokens), 0)
        for owner in range(owners):
            chosen = jnp.where(column_ref[owner : owner + 1, :] == slot, 1.0, 0.0)
            chosen_ref[owner * capacity : (owner + 1) * capacity, :] = chosen.astype(jnp.bfloat16)

    back = back_ref[...].reshape(owners * capacity, columns)
    out_ref[...] = left_dot(chosen_ref[...], back).astype(out_ref.dtype)


def unpack_rows(returned, slot_map, kind, after=()):
    owners, capacity, width = returned.shape
    tokens = slot_map.shape[1]
    columns = row_chunk(width, (256,))
    return pl.pallas_call(
        later(unpack_kernel, 2, len(after)),
        grid=(width // columns,),
        in_specs=[
            spec((owners, capacity, columns), lambda i: (0, 0, i)),
            spec((owners, tokens), lambda i: (0, 0)),
            *later_specs(after),
        ],
        out_specs=spec((tokens, columns), lambda i: (0, i)),
        out_shape=jax.ShapeDtypeStruct((tokens, width), kind),
        scratch_shapes=[pltpu.VMEM((owners * capacity, tokens), jnp.bfloat16)],
        compiler_params=kernel_params(),
        cost_estimate=small_cost,
        name="unpack_rows",
    )(returned, slot_map, *after)


def mix_kernel(stats_ref, map_ref, prob_ref, loss_ref, send_ref, peak_ref, total_ref, hits_ref):
    owners, stat_rows, capacity = stats_ref.shape
    tokens = map_ref.shape[1]
    slot = lax.broadcasted_iota(jnp.int32, (capacity, tokens), 0)
    for owner in range(owners):
        chosen = map_ref[owner : owner + 1, :] == slot
        columns = stats_ref[owner].T
        for place, target in enumerate((peak_ref, total_ref, hits_ref)):
            target[owner : owner + 1, :] = jnp.sum(
                jnp.where(chosen, columns[:, place : place + 1], 0.0), axis=0, keepdims=True
            )
    member = map_ref[...] >= 0
    peaks = jnp.where(member, peak_ref[...], -3e38)
    best = jnp.max(peaks, axis=0, keepdims=True)
    rescale = jnp.where(member, jnp.exp(peaks - best), 0.0)
    knn_total = jnp.sum(total_ref[...] * rescale, axis=0, keepdims=True)
    knn_prob = jnp.sum(hits_ref[...] * rescale, axis=0, keepdims=True) / knn_total
    mixture = mix_weight * knn_prob + (1.0 - mix_weight) * prob_ref[...]
    loss_ref[...] = -jnp.log(mixture)
    peak_ref[...] = (-mix_weight / (mixture * knn_total)) * rescale
    for owner in range(owners):
        chosen = map_ref[owner : owner + 1, :] == slot
        coefficient = jnp.sum(
            jnp.where(chosen, peak_ref[owner : owner + 1, :], 0.0), axis=1, keepdims=True
        )
        probability = jnp.sum(jnp.where(chosen, knn_prob, 0.0), axis=1, keepdims=True)
        lane = lax.broadcasted_iota(jnp.int32, (capacity, 128), 1)
        both = jnp.where(lane == 0, coefficient, probability)
        send_ref[owner] = both.T[:stat_rows, :]


def mix_losses(stats, slot_map, model_prob):
    owners, stat_rows, capacity = stats.shape
    tokens = slot_map.shape[1]
    vmem = pl.BlockSpec(memory_space=pltpu.VMEM)
    return pl.pallas_call(
        mix_kernel,
        in_specs=[vmem] * 3,
        out_specs=[vmem] * 2,
        out_shape=[
            jax.ShapeDtypeStruct((1, tokens), jnp.float32),
            jax.ShapeDtypeStruct(stats.shape, jnp.float32),
        ],
        scratch_shapes=[pltpu.VMEM((owners, tokens), jnp.float32)] * 3,
        compiler_params=pltpu.CompilerParams(vmem_limit_bytes=vmem_limit),
        name="mix_losses",
    )(stats, slot_map, model_prob)


def row_chunk(total, choices):
    for choice in choices:
        if total % choice == 0:
            return choice
    return total


def slot_picker(slot_map, capacity):
    return slot_map[:, None, :] == jnp.arange(capacity, dtype=jnp.int32)[None, :, None]


def layer_table(count):
    return [
        sorted(range(count), key=lambda other: (abs(other - layer), (other ^ layer) != 1, other))
        for layer in range(count)
    ]


def own_choice(options):
    layer = lax.axis_index("batch")
    kept = options[0]
    for place in range(1, len(options)):
        if all(options[place] is not other for other in options[:place]):
            same = [i for i, other in enumerate(options) if other is options[place]]
            here = functools.reduce(jnp.logical_or, [layer == i for i in same])
            kept = jnp.where(here, options[place], kept)
    return kept


def layer_step(step, ups, downs):
    options, picks = [], []
    for layer, line in enumerate(layer_table(lax.axis_size("batch"))):
        there = line[step]
        block = ups[layer - there] if there < layer else downs[there - layer]
        places = [place for place, other in enumerate(options) if other is block]
        if not places:
            options.append(block)
        picks.append(places[0] if places else len(options) - 1)
    return options, jnp.array(picks, jnp.int32)[lax.axis_index("batch")][None]


def layer_hop(hop, blocks, above, below):
    count = lax.axis_size("batch")
    reach = count - hop
    table = layer_table(count)

    def bound(layer, to):
        return blocks[table[layer].index(to) if 0 <= to < count else hop_step]

    hop_step = reach
    up = own_choice([bound(layer, layer + reach) for layer in range(count)])
    down = own_choice([bound(layer, layer - reach) for layer in range(count)])
    if hop > 1:
        up = (up.astype(jnp.float32) + above).astype(up.dtype)
        down = (down.astype(jnp.float32) + below).astype(down.dtype)
    return (
        lax.ppermute(up, "batch", [(i, i + 1) for i in range(hop)]),
        lax.ppermute(down, "batch", [(i, i - 1) for i in range(reach, count)]),
    )


def across(rows, step):
    return lax.ppermute(rows, "ctx", [(i, i ^ step) for i in range(lax.axis_size("ctx"))])


def in_ctx_order(parts):
    count = len(parts)
    own = lax.axis_index("ctx")
    stacked = jnp.stack(parts)
    return stacked[jnp.arange(count, dtype=jnp.int32) ^ own]


def ctx_gather(rows):
    return in_ctx_order([rows] + [across(rows, step) for step in range(1, lax.axis_size("ctx"))])


def swap_cores(rows):
    return lax.ppermute(rows, "rep", [(0, 1), (1, 0)])


def reduce_cores(grad):
    count = lax.axis_size("ctx")
    parts = grad.astype(jnp.bfloat16).reshape(count, 2, grad.shape[0] // (2 * count), grad.shape[1])
    core = lax.axis_index("rep")
    keep = lax.dynamic_index_in_dim(parts, core, 1, keepdims=False)
    send = lax.dynamic_index_in_dim(parts, 1 - core, 1, keepdims=False)
    return (keep.astype(jnp.float32) + swap_cores(send)).astype(jnp.bfloat16)


def ctx_trade(blocks):
    return [part if step == 0 else across(part, step) for step, part in enumerate(blocks)]


def exchange(blocks, axis):
    return lax.all_to_all(blocks, axis, split_axis=0, concat_axis=0, tiled=True)


def block_sum(blocks):
    total = blocks[0].astype(jnp.float32)
    for place in range(1, len(blocks)):
        total = total + blocks[place].astype(jnp.float32)
    return total


def ctx_reduce(halves):
    return lax.psum_scatter(halves, "ctx", scatter_dimension=0)


def layer_total(blocks):
    return block_sum(exchange(blocks, "batch")).astype(jnp.bfloat16)


def layer_blocks(rows):
    return rows.reshape(lax.axis_size("batch"), -1, rows.shape[1])


def both_halves(half):
    other = swap_cores(half)
    first = lax.axis_index("rep") == 0
    both = jnp.stack([jnp.where(first, half, other), jnp.where(first, other, half)])
    return both.reshape(-1, half.shape[-1]).astype(jnp.float32)


def shard_gather(rows):
    return both_halves(lax.all_gather(rows, "batch"))


def layer_gather(rows):
    count, layer = lax.axis_size("batch"), lax.axis_index("batch")
    parts = [rows] + [
        lax.ppermute(rows, "batch", [(i, (i + hops) % count) for i in range(count)])
        for hops in range(1, count)
    ]
    return both_halves(jnp.stack(parts)[(layer - jnp.arange(count, dtype=jnp.int32)) % count])


def mix_any(stats, slot_map, model_prob):
    owners, stat_rows, capacity = stats.shape
    if capacity % 16 == 0:
        return mix_losses(stats, slot_map, model_prob)
    chosen = slot_picker(slot_map, capacity)
    peak, total, hits = [
        jnp.sum(jnp.where(chosen, stats[:, row, :, None], 0.0), axis=1) for row in range(3)
    ]
    member = slot_map >= 0
    peaks = jnp.where(member, peak, -3e38)
    best = jnp.max(peaks, axis=0, keepdims=True)
    rescale = jnp.where(member, jnp.exp(peaks - best), 0.0)
    knn_total = jnp.sum(total * rescale, axis=0, keepdims=True)
    knn_prob = jnp.sum(hits * rescale, axis=0, keepdims=True) / knn_total
    mixture = mix_weight * knn_prob + (1.0 - mix_weight) * model_prob
    coefficient = (-mix_weight / (mixture * knn_total)) * rescale
    sent = [
        jnp.sum(jnp.where(chosen, part[:, None, :], 0.0), axis=2)
        for part in (coefficient, jnp.broadcast_to(knn_prob, coefficient.shape))
    ]
    sent = jnp.stack(sent + [sent[1]] * (stat_rows - 2), axis=1)
    return -jnp.log(mixture), sent


def local(
    tokens,
    cotangent,
    segment_ids,
    first_gain,
    first_shift,
    second_gain,
    second_shift,
    final_gain,
    final_shift,
    project_weight,
    output_weight,
    upward_weight,
    downward_weight,
    store_keys,
    store_values,
    owners,
    neighbours,
    targets,
    model_prob,
):
    head_count = HEADS
    group_seqs, block_len, width = tokens.shape
    seq_len = segment_ids.shape[1]
    ctx_count = lax.axis_size("ctx")
    shard_count = lax.axis_size("batch") * ctx_count
    capacity = neighbours.shape[3]
    near_count = neighbours.shape[4]
    top_count = owners.shape[2]
    key_count = store_keys.shape[0]
    spacing = key_count // near_count
    slot_rows = shard_count * capacity
    everyone = ("batch", "ctx")
    own_heads = head_count // ctx_count
    own_width = width // ctx_count
    attend_size = row_chunk(seq_len, (256, 128))

    arrived = [tokens[0]] + [across(tokens[0], step) for step in range(1, ctx_count)]
    own_rows = project_weight.shape[0]
    own_ctx = lax.axis_index("ctx")
    vectors = jnp.stack(
        [first_gain, first_shift, second_gain, second_shift, final_gain, final_shift], axis=1
    )
    vectors = jnp.pad(vectors, ((0, 0), (0, 128 - vectors.shape[1])))
    proj_pieces = [
        jnp.concatenate(
            [
                lax.dynamic_slice_in_dim(
                    project_weight, part * width + (own_ctx ^ step) * own_width, own_width, 1
                )
                for part in range(3)
            ]
            + [vectors],
            axis=1,
        )
        for step in range(ctx_count)
    ]
    proj_pieces = ctx_trade(proj_pieces)
    vectors = in_ctx_order([piece[:, 3 * own_width :] for piece in proj_pieces])
    vectors = vectors.reshape(width, -1)[:, :6].T.astype(jnp.float32)
    gain_list = [vectors[row] for row in range(6)]

    member = jnp.any(
        owners[0][:, :, None] == jnp.arange(shard_count, dtype=jnp.int32)[None, None, :], axis=1
    )
    place = jnp.arange(block_len, dtype=jnp.int32)
    earlier = (place[:, None] <= place[None, :]).astype(jnp.bfloat16)
    running = left_dot(member.astype(jnp.bfloat16), earlier).astype(jnp.int32)
    slot_map = jnp.where(member.T, running - 1, -1)
    send_targets = jnp.sum(
        jnp.where(slot_picker(slot_map, capacity), targets.reshape(1, 1, -1), 0), axis=2
    )
    got_targets = exchange(send_targets.astype(jnp.int32), everyone).astype(jnp.float32)
    planes = store_keys.reshape(near_count, spacing, width).transpose(1, 0, 2)
    planes = planes.reshape(key_count, width)
    planes_turned = planes.T
    key_square = jnp.sum(jnp.square(store_keys.astype(jnp.float32)), axis=1)
    key_square = key_square.reshape(near_count, spacing).T
    value_planes = store_values.astype(jnp.float32).reshape(near_count, spacing).T
    by_layer = capacity % 16 == 0
    if by_layer:
        piece, parts = capacity, 2 if ctx_count % 2 == 0 else 1
        layer_count = lax.axis_size("batch")
        maps = exchange(slot_map.reshape(layer_count, ctx_count, block_len), "batch")
        table = jnp.array(layer_table(layer_count), jnp.int32)[lax.axis_index("batch")]
        maps = maps[table]
        orders = table[:, None] * ctx_count + jnp.arange(ctx_count, dtype=jnp.int32)[None, :]
    else:
        piece, parts = row_chunk(slot_rows, (576, 512, 384, 256, 128)), 1
        orders = jnp.arange(slot_rows // piece, dtype=jnp.int32)[None, :]
        chosen_slots = slot_picker(slot_map, capacity).astype(jnp.bfloat16)
    near_table = neighbours.reshape(slot_rows // piece, piece, near_count)
    stat_shape = (slot_rows // piece, 8, piece)
    target_rows = jnp.broadcast_to(got_targets.reshape(stat_shape[0], 1, piece), stat_shape)

    early = proj_pieces[1:]
    core = lax.axis_index("rep")

    def own_half(weight):
        half = weight.shape[0] // 2
        mine = lax.dynamic_slice_in_dim(weight, core * half, half, 0)
        return run_after([mine], [*arrived[1:], *early])[0]

    def gather_weight(weight):
        return lax.all_gather(own_half(weight), ("ctx", "rep"), axis=0, tiled=True)

    out_full = gather_weight(output_weight)
    down_full = gather_weight(downward_weight)
    up_half = own_half(upward_weight)
    up_pieces = [across(up_half, step) for step in range(1, ctx_count)]
    sources = own_ctx ^ jnp.arange(ctx_count, dtype=jnp.int32)

    segments = segment_ids[0]
    start_rows = jnp.sum((segments[None, :] < segments[:, None]).astype(jnp.int32), axis=1)
    low_blocks = start_rows[::attend_size] // attend_size
    start_rows = jnp.broadcast_to(start_rows[None, :], (8, seq_len))
    proj_own, plain_full, normed_full, query_own, key_own, value_own = project_rows(
        arrived, proj_pieces, sources, vectors
    )
    attended_own, log_total = attend(
        query_own, key_own, value_own, start_rows, low_blocks, own_heads, attend_size
    )
    attended = lax.all_to_all(attended_own, "ctx", split_axis=0, concat_axis=1, tiled=True)
    attended = run_after([attended], [target_rows, maps] if by_layer else [target_rows])[0]
    up_pieces = [up_half, *run_after(up_pieces, [attended])]
    up_full = place_rows(
        up_pieces + [swap_cores(piece) for piece in up_pieces],
        jnp.concatenate([2 * sources + core, 2 * sources + 1 - core]),
    )
    inputs = tokens[0].astype(jnp.float32)
    hidden = inputs + row_dot(attended, out_full)
    normed_two = norm_rows(hidden, gain_list[2], gain_list[3]).astype(jnp.bfloat16)
    upper_rows = row_dot(normed_two, up_full)
    active = jax.nn.gelu(upper_rows).astype(jnp.bfloat16)
    summed = hidden + row_dot(active, down_full)
    final_rows = norm_rows(summed, gain_list[4], gain_list[5]).astype(jnp.bfloat16)

    if by_layer:
        ups, downs, packed, queries = [final_rows], [final_rows], [], []
        for step in range(layer_count):
            hop = step + 1
            if hop < layer_count:
                up, down = ups[-1], downs[-1]
                if hop == 2:
                    up, down = run_after([up, down], packed)
                    ups[-1], downs[-1] = up, down
                elif hop > 2:
                    up, down = run_after([up, down], [queries[hop - 3]])
                    ups[-1], downs[-1] = up, down
                ups.append(
                    lax.ppermute(up, "batch", [(i, i + 1) for i in range(step, layer_count - 1)])
                )
                downs.append(
                    lax.ppermute(down, "batch", [(i, i - 1) for i in range(1, layer_count - step)])
                )
            options, pick = layer_step(step, ups, downs)
            between = (planes, planes_turned, key_square) if step == 1 else ()
            packed.append(pack_rows(options, pick, maps[step], capacity, between))
            queries.append(exchange(packed[step], "ctx").reshape(-1, width))
    else:
        packed = jnp.einsum(
            "ost,tw->osw", chosen_slots, final_rows, preferred_element_type=jnp.float32
        )
        queries = [exchange(packed.astype(jnp.bfloat16), everyone).reshape(slot_rows, width)]
    marked, stats = zip(
        *[
            near_scores(
                rows,
                planes_turned,
                key_square,
                value_planes,
                near_table,
                target_rows,
                orders[step],
                parts,
                spacing,
            )
            for step, rows in enumerate(queries)
        ]
    )
    if by_layer:
        inverse = jnp.argmin(
            jnp.abs(table[None, :] - jnp.arange(layer_count, dtype=jnp.int32)[:, None]), axis=1
        )
        stats = jnp.stack(stats)[inverse].reshape(stat_shape)
    else:
        stats = stats[0].transpose(1, 0, 2).reshape(8, shard_count, capacity).transpose(1, 0, 2)
    token_loss, send_coeff = mix_any(exchange(stats, everyone), slot_map, model_prob)
    got_coeff = exchange(send_coeff, everyone)
    if not by_layer:
        got_coeff = got_coeff.transpose(1, 0, 2).reshape(8, -1, piece).transpose(1, 0, 2)
    if by_layer:
        returned, above, below = {}, None, None
        for step in reversed(range(layer_count)):
            hop = layer_count - 1 - step
            partial_grad = near_back(
                marked[step],
                near_table,
                got_coeff,
                planes,
                orders[step],
                parts,
                spacing,
                [returned[step + 2]] if hop >= 2 else [],
            )
            back = exchange(partial_grad.reshape(ctx_count, capacity, width), "ctx")
            if hop > 0:
                above, below = layer_hop(hop, returned, above, below)
            returned[step] = unpack_rows(
                back,
                maps[step],
                jnp.bfloat16 if step > 0 else jnp.float32,
                [above, below] if hop > 0 else [],
            )
        query_grad = returned[0] + above.astype(jnp.float32) + below.astype(jnp.float32)
    else:
        partial_grad = near_back(
            marked[0], near_table, got_coeff, planes, orders[0], parts, spacing
        )
        back = exchange(partial_grad.reshape(shard_count, capacity, width), everyone)
        query_grad = jnp.einsum(
            "ost,osw->tw", chosen_slots, back, preferred_element_type=jnp.float32
        )

    out_grad = cotangent[0].astype(jnp.float32) + query_grad
    final_vjp = jax.vjp(norm_rows, summed, gain_list[4], gain_list[5])[1]
    summed_grad, final_gain_grad, final_shift_grad = final_vjp(out_grad)
    branch_grad = summed_grad.astype(jnp.bfloat16)
    downward_grad = left_dot(active, branch_grad)
    active_grad = right_dot(branch_grad, down_full)
    gelu_vjp = jax.vjp(jax.nn.gelu, upper_rows)[1]
    upper_grad = gelu_vjp(active_grad)[0].astype(jnp.bfloat16)
    downward_half = reduce_cores(downward_grad)
    upper_grad = run_after([upper_grad], [downward_half])[0]
    second_vjp = jax.vjp(norm_rows, hidden, gain_list[2], gain_list[3])[1]
    hidden_part, second_gain_grad, second_shift_grad = second_vjp(right_dot(upper_grad, up_full))
    hidden_grad = summed_grad + hidden_part
    attn_grad = hidden_grad.astype(jnp.bfloat16)
    attended_grad = right_dot(attn_grad, out_full).astype(jnp.bfloat16)
    downward_half = ctx_reduce(downward_half)
    second_half = reduce_cores(
        jnp.concatenate(
            [
                left_dot(normed_two, upper_grad).astype(jnp.bfloat16),
                left_dot(attended, attn_grad).astype(jnp.bfloat16),
            ],
            axis=1,
        )
    )
    attended_grad = run_after([attended_grad], [downward_half])[0]
    grad_own = lax.all_to_all(attended_grad, "ctx", split_axis=1, concat_axis=0, tiled=True)
    second_half = run_after([second_half], [grad_own])[0]
    downward_half = run_after([downward_half], [second_half])[0]
    downward_total = layer_total(layer_blocks(downward_half))
    proj_grad = jnp.concatenate(
        run_after(
            attend_back(
                query_own,
                key_own,
                value_own,
                grad_own,
                attended_own,
                log_total,
                start_rows,
                low_blocks,
                own_heads,
                attend_size,
                (second_half, downward_half),
            ),
            [downward_total],
        ),
        axis=1,
    )
    plain_part = left_dot(plain_full, proj_grad)
    column_sums = jnp.sum(proj_grad.astype(jnp.float32), axis=0)
    proj_full = proj_own.astype(jnp.float32)
    first_gain_grad = jnp.sum(plain_part * proj_full, axis=1)
    first_shift_grad = jnp.sum(column_sums[None, :] * proj_full, axis=1)
    project_part = plain_part * gain_list[0][:, None] + column_sums[None, :] * gain_list[1][:, None]

    vector_part = jnp.stack(
        [
            first_gain_grad,
            first_shift_grad,
            second_gain_grad,
            second_shift_grad,
            final_gain_grad,
            final_shift_grad,
        ],
        axis=1,
    )
    vector_part = jnp.pad(vector_part, ((0, 0), (0, 128 - vector_part.shape[1])))
    project_part = jnp.concatenate([project_part, vector_part], axis=1)
    project_part = reduce_cores(project_part)
    normed_terms = right_dot(proj_grad, run_after([proj_own], [project_part])[0])
    term_blocks = normed_terms.astype(jnp.bfloat16).reshape(ctx_count, block_len, width)
    term_parts = ctx_trade(
        [
            lax.dynamic_index_in_dim(term_blocks, own_ctx ^ step, 0, keepdims=False)
            for step in range(ctx_count)
        ]
    )
    project_part = exchange(project_part, "ctx")
    second_part = run_after([ctx_reduce(second_half)], [project_part])[0]
    second_total = layer_total(layer_blocks(second_part))
    vector_part = block_sum(project_part[:, :, 3 * own_width :]).astype(jnp.bfloat16)
    project_part = (
        project_part[:, :, : 3 * own_width]
        .reshape(ctx_count, own_rows // 2, 3, own_width)
        .transpose(1, 2, 0, 3)
        .reshape(own_rows // 2, 3 * width)
    )
    small_rows = jnp.concatenate([project_part, vector_part], axis=1)
    term_parts = [term_parts[0], *run_after(term_parts[1:], [second_total])]
    small_rows = run_after([small_rows], [second_total])[0]
    small_total = layer_total(layer_blocks(small_rows))
    small_total = run_after([small_total], term_parts[1:])[0]
    input_vjp = jax.vjp(lambda rows: norm_rows(rows, gain_list[0], gain_list[1]), inputs)[1]
    input_grad = hidden_grad + input_vjp(block_sum(term_parts))[0]
    small_grads = layer_gather(small_total)
    second_grads = shard_gather(second_total)
    weight_grads = [
        small_grads[:, : 3 * width],
        second_grads[:, second_grads.shape[1] - width :],
        second_grads[:, : second_grads.shape[1] - width],
        both_halves(
            run_after([lax.all_gather(downward_total, "batch")], [small_total])[0]
        ),
    ]
    vector_grads = small_grads[:, 3 * width : 3 * width + 6].T
    return (
        final_rows.reshape(group_seqs, block_len, width),
        token_loss.reshape(group_seqs, block_len),
        query_grad.reshape(group_seqs, block_len, width),
        input_grad.reshape(group_seqs, block_len, width),
        *weight_grads,
        *[vector_grads[row] for row in range(6)],
    )


def solution(mesh):
    placed = (
        P(("rep", "batch"), "ctx", None),
        P(("rep", "batch"), "ctx", None),
        P(("rep", "batch"), None),
        P("ctx"),
        P("ctx"),
        P("ctx"),
        P("ctx"),
        P("ctx"),
        P("ctx"),
        P("ctx", None),
        P("ctx", None),
        P("ctx", None),
        P("ctx", None),
        P(("batch", "ctx"), None),
        P(("batch", "ctx")),
        P(("rep", "batch"), "ctx", None),
        P("rep", ("batch", "ctx"), None, None, None),
        P(("rep", "batch"), "ctx"),
        P(("rep", "batch"), "ctx"),
    )
    return jax.shard_map(
        local,
        mesh=mesh,
        in_specs=placed,
        out_specs=(
            P(("rep", "batch"), "ctx", None),
            P(("rep", "batch"), "ctx"),
            P(("rep", "batch"), "ctx", None),
            P(("rep", "batch"), "ctx", None),
            P("ctx", None),
            P("ctx", None),
            P("ctx", None),
            P("ctx", None),
            P("ctx"),
            P("ctx"),
            P("ctx"),
            P("ctx"),
            P("ctx"),
            P("ctx"),
        ),
        check_vma=False,
    )
```

time: 1400 us -> 958 us (0.68)
  waiting for transfers between devices: 786 us -> 312 us
  blocking collectives: 182 us -> 25.2 us
  starting transfers between devices: 26 us -> 125 us
  other arithmetic: 39.5 us -> 84.7 us
  Pallas kernels: 179 us -> 214 us
  local copies, waits for them, and re-layouts: 52.7 us -> 86.9 us
  matrix products: 111 us -> 86.8 us
    all_to_all x4 -> x15, waiting for transfers between devices: 327 us -> 69.5 us  [the longest x14 62.6 us: exchange(): return lax.all_to_all(blocks, axis, split_axis=0, concat_axis=0, tiled=True)]
    reduce_scatter x4 -> x0, waiting for transfers between devices: 207 us -> none  [the longest x3 194 us: scatter_grad(): lax.psum_scatter(grad.astype(jnp.bfloat16), ('ctx', 'rep'), scatter_dimen...]
    ppermute x0 -> x37, waiting for transfers between devices: none -> 199 us  [the longest x12 76.4 us: across(): lax.ppermute(rows, 'ctx', [(i, i ^ step) for i in range(lax.axis_size('ct...]
    psum x1 -> x0, waiting for transfers between devices: 116 us -> none  [local(): lax.psum(piece, 'batch')]
    all_gather x7 -> x4, waiting for transfers between devices: 113 us -> 0.01 us  [the longest x2 0.01 us: gather_weight(): return lax.all_gather(own_half(weight), ('ctx', 'rep'), axis=0, tiled=True)]
    all_to_all x4 -> x2, blocking collectives: 110 us -> 25.2 us  [exchange(): return lax.all_to_all(blocks, axis, split_axis=0, concat_axis=0, tiled=True)]
    ppermute x0 -> x37, starting transfers between devices: none -> 52.7 us  [the longest x12 16.5 us: across(): lax.ppermute(rows, 'ctx', [(i, i ^ step) for i in range(lax.axis_size('ct...]
    all_to_all x4 -> x15, starting transfers between devices: 21.5 us -> 68.2 us  [the longest x14 64.7 us: exchange(): return lax.all_to_all(blocks, axis, split_axis=0, concat_axis=0, tiled=True)]
  transfers between devices with their start and end apart: 18 -> 59, of which waited for: 15 -> 27; matrix products, arithmetic and copies ran while one was open for 10% -> 19% of each run, Pallas kernels for 4% -> 18%
where the time goes in v2:
time: 958 us; the launch traced here: 951 us
  waiting for transfers between devices  312 us (33%)
  Pallas kernels  214 us (22%)
  starting transfers between devices  125 us (13%)
  local copies, waits for them, and re-layouts  86.9 us (9%)
  matrix products  86.8 us (9%)
  other arithmetic  84.7 us (9%)
  blocking collectives  25.2 us (3%)
  between operations  15.8 us (2%)
    ppermute x12, waiting for transfers between devices, across(): lax.ppermute(rows, 'ctx', [(i, i ^ step) for i in range(lax.axis_size('ct...  76.4 us
    all_to_all x14, starting transfers between devices, exchange(): return lax.all_to_all(blocks, axis, split_axis=0, concat_axis=0, tiled=True)  64.7 us
    all_to_all x14, waiting for transfers between devices, exchange(): return lax.all_to_all(blocks, axis, split_axis=0, concat_axis=0, tiled=True)  62.6 us
    ppermute x3, waiting for transfers between devices, local(): lax.ppermute(down, 'batch', [(i, i - 1) for i in range(1, layer_count - s...  59.9 us
    pallas_call x4, Pallas kernels, near_scores(): pl.pallas_call(functools.partial(near_kernel, spacing, width ** (-0.5), p...  44.5 us
    pallas_call x4, Pallas kernels, near_back(): pl.pallas_call(later(functools.partial(near_back_kernel, spacing, 2.0 * w...  41.5 us
    dot_general x4, matrix products, right_dot(): lax.dot_general(left_side, right_side, (((1,), (1,)), ((), ())), preferre...  35.4 us
    pallas_call x1, Pallas kernels, attend_back(): pl.pallas_call(later(functools.partial(attend_back_kernel, head_count), 8...  29.9 us
  transfers between devices with their start and end apart: 59, of which 27 were waited for; matrix products, arithmetic and copies ran while one was open for 19% of the time, Pallas kernels for 18%

profile of v2, /device:TPU:0, one launch (start us, length us, event | category | flops | bytes accessed | tf_op | source)
XLA Modules:
  0.0 950.6 jit_solution(16827648183491627803)
XLA Ops:
  22.1 50.8 %collective-permute-done.5.refs_7_.refs_6_ = bf16[256,896]{1,0:T(8,128)(2,1)} collective-permute-done((bf16[256,896]{1,0:T(8,128)(2,1)S(1)}, bf16[256,896]{1,0:T(8,128)(2,1)}, u32[]{:S(2)}, u32[]{:S(2)}) %collective-permute-start.5) | collective-permute-done | bytes 458784 | tf_op jit(solution)/shard_map/ppermute | solution.py:734
  76.1 6.8 collective-permute-done.4.refs_6_.refs_5_
  89.9 6.1 all-to-all-start.1
  108.8 13.0 %project_rows.1 = (bf16[1024,768]{1,0:T(8,128)(2,1)}, bf16[2304,1024]{1,0:T(8,128)(2,1)}, bf16[2304,1024]{1,0:T(8,128)(2,1)}, bf16[2304,256]{1,0:T(8,128)(2,1)},...) custom-call(s32[4]{0:T(128)} %iota_xor_fusion.order_ref, bf16[576,1024]{1,0:T(8,128)(2,1)} %bitcast.241, ...), custom_call_target="tpu_custom_call" | custom-call | flops 12999999488 | bytes 1000 | tf_op jit(solution)/shard_map/project_rows/pallas_call | solution.py:392
  127.5 20.8 %attend.1 = (bf16[2304,256]{1,0:T(8,128)(2,1)}, f32[8,2304]{1,0:T(8,128)}) custom-call(s32[18]{0:T(128)} %pad_add_fusion.refs_0_, bf16[2304,256]{1,0:T(8,128)(2,1)} %get-tuple-element.48.refs_1_, bf16[2304,256]{1,0:T(8,128)(2,1)} %get-tuple-element.49.refs_2_, bf16[2304,256]{1,0:T(8,128)(2,1)} %get-tuple-element.50.refs_3_, ...), custom_call_target="tpu_custom_call" | custom-call | flops 20000000000 | bytes 1000 | tf_op jit(solution)/shard_map/attend/pallas_call | solution.py:193
  153.5 27.8 %all-to-all-done = bf16[4,576,256]{2,1,0:T(8,128)(2,1)S(1)} async-done(((bf16[4,576,256]{2,1,0:T(8,128)(2,1)}), bf16[4,576,256]{2,1,0:T(8,128)(2,1)S(1)}, u32[]{:S(2)}, u32[]{:S(2)}) %all-to-all-start) | async-done | bytes 1179680 | tf_op jit(solution)/shard_map/all_to_all | solution.py:954
  190.4 8.9 place_rows.1
  203.9 7.8 fusion.43
  211.7 12.6 %fusion.49 = (f32[576]{0:T(1024)S(1)}, f32[576,1024]{1,0:T(8,128)S(1)}) fusion(f32[576,1024]{1,0:T(8,128)} %copy-done.22, bf16[4096,1024]{1,0:T(8,128)(2,1)} %all-gather.7.cloned.1.call-done, f32[576,4096]{1,0:T(8,128)} %fusion.43), kind=kOutput, calls=%fused_computation.215 | convolution fusion | flops 4854251008 | bytes 22546688 | tf_op jit(solution)/shard_map/dot_general | solution.py:28
  242.1 6.5 copy.127
  248.6 6.4 copy.130.refs_2_.refs_5_
  271.2 6.1 pack_rows.5
  283.9 28.9 %collective-permute-done.16.refs_1_ = bf16[576,1024]{1,0:T(8,128)(2,1)S(1)} collective-permute-done((bf16[576,1024]{1,0:T(8,128)(2,1)}, bf16[576,1024]{1,0:T(8,128)(2,1)S(1)}, u32[]{:S(2)}, u32[]{:S(2)}) %collective-permute-start.16) | collective-permute-done | bytes 1179680 | tf_op jit(solution)/shard_map/ppermute | solution.py:985
  326.4 25.9 %collective-permute-done.17.refs_1_ = bf16[576,1024]{1,0:T(8,128)(2,1)S(1)} collective-permute-done((bf16[576,1024]{1,0:T(8,128)(2,1)S(1)}, bf16[576,1024]{1,0:T(8,128)(2,1)S(1)}, u32[]{:S(2)}, u32[]{:S(2)}) %collective-permute-start.17) | collective-permute-done | bytes 1179680 | tf_op jit(solution)/shard_map/ppermute | solution.py:985
  367.0 11.1 %near_scores.4 = (f32[1152,256]{1,0:T(8,128)}, f32[4,8,288]{2,1,0:T(8,128)}) custom-call(s32[4]{0:T(128)} %get-tuple-element.150.refs_0_, bf16[1152,1024]{1,0:T(8,128)(2,1)} %bitcast.23.refs_1_.refs_2_, bf16[1024,2048]{1,0:T(8,128)(2,1)} %copy.130.refs_2_.refs_5_, f32[8,256]{1,0:T(8,128)} %bitcast.268, f32[8,256]{1,0:T(8,128)} %bitcast.272, ...), custom_call_target="tpu_custom_call" | custom-call | flops 1000 | bytes 1000 | tf_op jit(solution)/shard_map/near_scores/pallas_call | solution.py:467
  378.1 11.1 %near_scores.5 = (f32[1152,256]{1,0:T(8,128)}, f32[4,8,288]{2,1,0:T(8,128)}) custom-call(s32[4]{0:T(128)} %get-tuple-element.153.refs_0_, bf16[1152,1024]{1,0:T(8,128)(2,1)} %bitcast.36.refs_1_, bf16[1024,2048]{1,0:T(8,128)(2,1)} %copy.130.refs_2_.refs_5_, f32[8,256]{1,0:T(8,128)} %bitcast.269, f32[8,256]{1,0:T(8,128)} %bitcast.273, ...), custom_call_target="tpu_custom_call" | custom-call | flops 1000 | bytes 1000 | tf_op jit(solution)/shard_map/near_scores/pallas_call | solution.py:467
  389.2 11.1 %near_scores.6 = (f32[1152,256]{1,0:T(8,128)}, f32[4,8,288]{2,1,0:T(8,128)}) custom-call(s32[4]{0:T(128)} %get-tuple-element.152.refs_0_, bf16[1152,1024]{1,0:T(8,128)(2,1)} %bitcast.41.refs_1_, bf16[1024,2048]{1,0:T(8,128)(2,1)} %copy.130.refs_2_.refs_5_, f32[8,256]{1,0:T(8,128)} %bitcast.270, f32[8,256]{1,0:T(8,128)} %bitcast.274, ...), custom_call_target="tpu_custom_call" | custom-call | flops 1000 | bytes 1000 | tf_op jit(solution)/shard_map/near_scores/pallas_call | solution.py:467
  400.3 11.2 %near_scores.7 = (f32[1152,256]{1,0:T(8,128)}, f32[4,8,288]{2,1,0:T(8,128)}) custom-call(s32[4]{0:T(128)} %get-tuple-element.151.refs_0_, bf16[1152,1024]{1,0:T(8,128)(2,1)} %bitcast.45.refs_1_, bf16[1024,2048]{1,0:T(8,128)(2,1)} %copy.130.refs_2_.refs_5_, f32[8,256]{1,0:T(8,128)} %bitcast.271, f32[8,256]{1,0:T(8,128)} %bitcast.275, ...), custom_call_target="tpu_custom_call" | custom-call | flops 1000 | bytes 1000 | tf_op jit(solution)/shard_map/near_scores/pallas_call | solution.py:467
  412.9 12.5 %all_to_all.122.stats_ref = f32[16,8,288]{2,1,0:T(8,128)} all-to-all(f32[16,8,288]{2,1,0:T(8,128)S(1)} %bitcast.266), channel_id=1, replica_groups=mesh['rep'=2,'batch'=4,'ctx'=4] {'batch','ctx'}, dimensions={0} | all-to-all | bytes 294912 | tf_op jit(solution)/shard_map/all_to_all | solution.py:766
  425.4 11.8 %mix_losses.1 = (f32[1,576]{1,0:T(1,128)}, f32[16,8,288]{2,1,0:T(8,128)}) custom-call(f32[16,8,288]{2,1,0:T(8,128)} %all_to_all.122.stats_ref, s32[16,576]{1,0:T(8,128)} %copy-done.50, f32[1,576]{1,0:T(1,128)} %prob_ref.1), custom_call_target="tpu_custom_call" | custom-call | tf_op jit(solution)/shard_map/mix_losses/pallas_call | solution.py:658
  437.2 12.7 %all_to_all.123.refs_4_.refs_5_ = f32[16,8,288]{2,1,0:T(8,128)} all-to-all(f32[16,8,288]{2,1,0:T(8,128)} %get-tuple-element.66), channel_id=1, replica_groups=mesh['rep'=2,'batch'=4,'ctx'=4] {'batch','ctx'}, dimensions={0} | all-to-all | bytes 294912 | tf_op jit(solution)/shard_map/all_to_all | solution.py:766
  449.9 10.4 %near_back.5 = bf16[1152,1024]{1,0:T(8,128)(2,1)} custom-call(s32[4]{0:T(128)} %get-tuple-element.151.refs_0_, f32[1152,256]{1,0:T(8,128)} %get-tuple-element.68.refs_1_, s32[16,288,256]{2,1,0:T(8,128)} %bitcast.215, s32[16,288,256]{2,1,0:T(8,128)} %bitcast.216, f32[16,8,288]{2,1,0:T(8,128)} %all_to_all.123.refs_4_.refs_5_, ...), custom_call_target="tpu_custom_call" | custom-call | flops 1000 | bytes 1000 | tf_op jit(solution)/shard_map/near_back/pallas_call | solution.py:520
  464.8 10.4 %near_back.4 = bf16[1152,1024]{1,0:T(8,128)(2,1)} custom-call(s32[4]{0:T(128)} %get-tuple-element.152.refs_0_, f32[1152,256]{1,0:T(8,128)} %get-tuple-element.67.refs_1_, s32[16,288,256]{2,1,0:T(8,128)} %bitcast.217, s32[16,288,256]{2,1,0:T(8,128)} %bitcast.218, f32[16,8,288]{2,1,0:T(8,128)} %all_to_all.123.refs_4_.refs_5_, ...), custom_call_target="tpu_custom_call" | custom-call | flops 1000 | bytes 1000 | tf_op jit(solution)/shard_map/near_back/pallas_call | solution.py:520
  475.1 12.3 %all-to-all-done.10.refs_0_ = bf16[4,288,1024]{2,1,0:T(8,128)(2,1)} async-done(((bf16[4,288,1024]{2,1,0:T(8,128)(2,1)}), bf16[4,288,1024]{2,1,0:T(8,128)(2,1)}, u32[]{:S(2)}, u32[]{:S(2)}) %all-to-all-start.10) | async-done | bytes 2359328 | tf_op jit(solution)/shard_map/all_to_all | solution.py:766
  501.7 10.4 %near_back.7 = bf16[1152,1024]{1,0:T(8,128)(2,1)} custom-call(s32[4]{0:T(128)} %get-tuple-element.153.refs_0_, f32[1152,256]{1,0:T(8,128)} %get-tuple-element.69.refs_1_, s32[16,288,256]{2,1,0:T(8,128)} %bitcast.219, s32[16,288,256]{2,1,0:T(8,128)} %bitcast.220, f32[16,8,288]{2,1,0:T(8,128)} %all_to_all.123.refs_4_.refs_5_, ...), custom_call_target="tpu_custom_call" | custom-call | flops 1000 | bytes 1000 | tf_op jit(solution)/shard_map/near_back/pallas_call | solution.py:520
  512.0 7.1 all-to-all-done.9.refs_0_
  541.5 10.4 %near_back.6 = bf16[1152,1024]{1,0:T(8,128)(2,1)} custom-call(s32[4]{0:T(128)} %get-tuple-element.150.refs_0_, f32[1152,256]{1,0:T(8,128)} %get-tuple-element.65.refs_1_, s32[16,288,256]{2,1,0:T(8,128)} %bitcast.221, s32[16,288,256]{2,1,0:T(8,128)} %bitcast.222, f32[16,8,288]{2,1,0:T(8,128)} %all_to_all.123.refs_4_.refs_5_, ...), custom_call_target="tpu_custom_call" | custom-call | flops 1000 | bytes 1000 | tf_op jit(solution)/shard_map/near_back/pallas_call | solution.py:520
  556.4 7.0 collective-permute-done.21.refs_2_
  575.5 6.6 collective-permute-start.23
  582.6 20.5 %collective-permute-done.24.refs_3_ = bf16[576,1024]{1,0:T(8,128)(2,1)S(1)} collective-permute-done((bf16[576,1024]{1,0:T(8,128)(2,1)}, bf16[576,1024]{1,0:T(8,128)(2,1)S(1)}, u32[]{:S(2)}, u32[]{:S(2)}) %collective-permute-start.24) | collective-permute-done | bytes 1179680 | tf_op jit(solution)/shard_map/ppermute | solution.py:729
  610.7 6.1 multiply_reduce_fusion.1
  617.7 11.4 %convolution_convert_fusion.1 = bf16[4096,1024]{1,0:T(8,128)(2,1)S(1)} fusion(f32[576,1024]{1,0:T(8,128)S(1)} %get-tuple-element.103, f32[576]{0:T(1024)S(1)} %negate_multiply_fusion.2, f32[576,4096]{1,0:T(8,128)} %fusion.43), kind=kOutput, calls=%fused_computation.24 | convolution fusion | flops 4858445824 | bytes 20187392 | tf_op jit(solution)/shard_map/dot_general | solution.py:32
  633.8 16.6 %fusion.7.refs_0_ = bf16[576,4096]{1,0:T(8,128)(2,1)} fusion(f32[576,4096]{1,0:T(8,128)} %fusion.43, bf16[4096,1024]{1,0:T(8,128)(2,1)} %all-gather.7.cloned.1.call-done, f32[576,1024]{1,0:T(8,128)} %copy-done.26, f32[576]{0:T(1024)S(1)} %negate_multiply_fusion.2), kind=kOutput, calls=%fused_computation.18 | convolution fusion | flops 4880203776 | bytes 24905984 | tf_op jit(solution)/shard_map/dot_general | solution.py:38
  650.4 6.3 fusion.8.refs_1_
  656.7 10.0 %multiply_reduce_fusion.2 = (bf16[1024]{0:T(1024)(128)(2,1)S(1)}, f32[576]{0:T(1024)S(1)}, bf16[1024]{0:T(1024)(128)(2,1)S(1)}, f32[576,1024]{1,0:T(8,128)S(1)}) fusion(f32[576,1024]{1,0:T(8,128)} %copy-done.22, f32[576]{0:T(1024)S(1)} %fusion.34, f32[576]{0:T(1024)S(1)} %broadcast_multiply_fusion.2, f32[1024]{0:T(1024)S(1)} %bitcast.295, ...), kind=kOutput, calls=%fused_computation.56 | convolution fusion | flops 4836554240 | bytes 17840896 | tf_op jit(solution)/shard_map/dot_general | solution.py:38
  672.9 7.5 convolution_convert_fusion
  680.4 6.2 pad_maximum_fusion
  695.4 15.1 %reduce-scatter.7.cloned.1.call-done = bf16[1,512,1024]{2,1,0:T(8,128)(2,1)} async-done(((bf16[4,512,1024]{2,1,0:T(8,128)(2,1)}), bf16[1,512,1024]{2,1,0:T(8,128)(2,1)}) %reduce-scatter.7.cloned.1.call-update) | async-done | bytes 1048592
  716.5 8.4 fusion.refs_0_
  724.8 6.9 all-to-all-done.13
  737.4 29.9 %attend_back.1 = (bf16[2304,256]{1,0:T(8,128)(2,1)}, bf16[2304,256]{1,0:T(8,128)(2,1)}, bf16[2304,256]{1,0:T(8,128)(2,1)}) custom-call(s32[18]{0:T(128)} %pad_add_fusion.refs_0_, bf16[2304,256]{1,0:T(8,128)(2,1)} %get-tuple-element.48.refs_1_, bf16[2304,256]{1,0:T(8,128)(2,1)} %get-tuple-element.49.refs_2_, bf16[2304,256]{1,0:T(8,128)(2,1)} %get-tuple-element.50.refs_3_, ...), custom_call_target="tpu_custom_call" | custom-call | flops 1000 | bytes 1000 | tf_op jit(solution)/shard_map/attend_back/pallas_call | solution.py:328
  772.9 6.9 fusion.13
  789.7 12.8 %all-to-all-done.15.refs_1_ = bf16[4,128,896]{2,1,0:T(8,128)(2,1)S(1)} async-done(((bf16[4,128,896]{2,1,0:T(8,128)(2,1)}), bf16[4,128,896]{2,1,0:T(8,128)(2,1)S(1)}, u32[]{:S(2)}, u32[]{:S(2)}) %all-to-all-start.15) | async-done | bytes 917536 | tf_op jit(solution)/shard_map/all_to_all | solution.py:766
  809.4 6.3 convolution_convert_fusion.2
  829.1 27.0 %all-to-all-done.16 = bf16[4,32,5120]{2,1,0:T(8,128)(2,1)} async-done(((bf16[4,32,5120]{2,1,0:T(8,128)(2,1)}), bf16[4,32,5120]{2,1,0:T(8,128)(2,1)}, u32[]{:S(2)}, u32[]{:S(2)}) %all-to-all-start.16) | async-done | bytes 1310752 | tf_op jit(solution)/shard_map/all_to_all | solution.py:766
  869.2 17.1 %collective-permute-done.30.refs_2_ = bf16[576,1024]{1,0:T(8,128)(2,1)} collective-permute-done((bf16[576,1024]{1,0:T(8,128)(2,1)}, bf16[576,1024]{1,0:T(8,128)(2,1)}, u32[]{:S(2)}, u32[]{:S(2)}) %collective-permute-start.30) | collective-permute-done | bytes 1179680 | tf_op jit(solution)/shard_map/ppermute | solution.py:734
  899.9 7.8 collective-permute-done.33
  907.8 13.7 %collective-permute-done.32 = bf16[32,3200]{1,0:T(8,128)(2,1)S(1)} collective-permute-done((bf16[32,3200]{1,0:T(8,128)(2,1)}, bf16[32,3200]{1,0:T(8,128)(2,1)S(1)}, u32[]{:S(2)}, u32[]{:S(2)}) %collective-permute-start.32) | collective-permute-done | bytes 204832 | tf_op jit(solution)/shard_map/ppermute | solution.py:802
  (418 shorter events, 314.1 us)
Async XLA Ops:
  7.2 192.1 %all-gather.5.cloned.1.call-start = ((), (), s32[]{:S(2)}) async-start(), calls=%async_computation.20 | async-start | bytes 2359296 | tf_op jit(solution)/shard_map/all_gather | solution.py:936
  7.2 77.4 %collective-permute-start = (bf16[576,1024]{1,0:T(8,128)(2,1)}, bf16[576,1024]{1,0:T(8,128)(2,1)S(1)}, u32[]{:S(2)}, u32[]{:S(2)}) collective-permute-start(bf16[576,1024]{1,0:T(8,128)(2,1)} %bitcast.238), channel_id=1, source_target_pairs={{0,1},{1,0},{2,3},{3,2},{4,5},{5,4},{6,7},{7,6},{8,9},{9,8},{10,11... | collective-permute-start | bytes 3538952 | tf_op jit(solution)/shard_map/ppermute | solution.py:734
  10.2 74.4 %collective-permute-start.1 = (bf16[576,1024]{1,0:T(8,128)(2,1)}, bf16[576,1024]{1,0:T(8,128)(2,1)}, u32[]{:S(2)}, u32[]{:S(2)}) collective-permute-start(bf16[576,1024]{1,0:T(8,128)(2,1)} %bitcast.239), channel_id=1, source_target_pairs={{0,2},{1,3},{2,0},{3,1},{4,6},{5,7},{6,4},{7,5},{8,10},{9,11},{10,... | collective-permute-start | bytes 3538952 | tf_op jit(solution)/shard_map/ppermute | solution.py:734
  11.8 72.8 %collective-permute-start.2 = (bf16[576,1024]{1,0:T(8,128)(2,1)}, bf16[576,1024]{1,0:T(8,128)(2,1)}, u32[]{:S(2)}, u32[]{:S(2)}) collective-permute-start(bf16[576,1024]{1,0:T(8,128)(2,1)} %bitcast.240), channel_id=1, source_target_pairs={{0,3},{1,2},{2,1},{3,0},{4,7},{5,6},{6,5},{7,4},{8,11},{9,10},{10,... | collective-permute-start | bytes 3538952 | tf_op jit(solution)/shard_map/ppermute | solution.py:734
  18.7 54.2 %collective-permute-start.5 = (bf16[256,896]{1,0:T(8,128)(2,1)S(1)}, bf16[256,896]{1,0:T(8,128)(2,1)}, u32[]{:S(2)}, u32[]{:S(2)}) collective-permute-start(bf16[256,896]{1,0:T(8,128)(2,1)S(1)} %get-tuple-element.134), channel_id=1, source_target_pairs={{0,3},{1,2},{2,1},{3,0},{4,7},{5,6},{6,5},{7,4},{8,11},{9,10},{10,... | collective-permute-start | bytes 1376264 | tf_op jit(solution)/shard_map/ppermute | solution.py:734
  21.6 61.3 %collective-permute-start.4 = (bf16[256,896]{1,0:T(8,128)(2,1)}, bf16[256,896]{1,0:T(8,128)(2,1)}, u32[]{:S(2)}, u32[]{:S(2)}) collective-permute-start(bf16[256,896]{1,0:T(8,128)(2,1)} %get-tuple-element.135), channel_id=1, source_target_pairs={{0,2},{1,3},{2,0},{3,1},{4,6},{5,7},{6,4},{7,5},{8,10},{9,11},{10,... | collective-permute-start | bytes 1376264 | tf_op jit(solution)/shard_map/ppermute | solution.py:734
  85.6 126.1 %all-gather.7.cloned.1.call-start = ((), (), s32[]{:S(2)}) async-start(), calls=%async_computation.21 | async-start | bytes 9437184 | tf_op jit(solution)/shard_map/all_gather | solution.py:936
  89.9 31.8 %all-to-all-start.1 = ((s32[16,1,288]{2,1,0:T(1,128)}), s32[16,1,288]{2,1,0:T(1,128)S(1)}, u32[]{:S(2)}, u32[]{:S(2)}) async-start(s32[16,1,288]{2,1,0:T(1,128)} %copy.126), calls=%async_computation.1 | async-start | bytes 49152 | tf_op jit(solution)/shard_map/all_to_all | solution.py:766
  105.3 77.9 %collective-permute-start.6 = (bf16[128,4096]{1,0:T(8,128)(2,1)}, bf16[128,4096]{1,0:T(8,128)(2,1)S(1)}, u32[]{:S(2)}, u32[]{:S(2)}) collective-permute-start(bf16[128,4096]{1,0:T(8,128)(2,1)} %run_after.20.refs_0_), channel_id=1, source_target_pairs={{0,1},{1,0},{2,3},{3,2},{4,5},{5,4},{6,7},{7,6},{8,9},{9,8},{10,11... | collective-permute-start | bytes 3145736 | tf_op jit(solution)/shard_map/ppermute | solution.py:734
  107.3 75.9 %collective-permute-start.7 = (bf16[128,4096]{1,0:T(8,128)(2,1)}, bf16[128,4096]{1,0:T(8,128)(2,1)}, u32[]{:S(2)}, u32[]{:S(2)}) collective-permute-start(bf16[128,4096]{1,0:T(8,128)(2,1)} %run_after.20.refs_0_), channel_id=1, source_target_pairs={{0,2},{1,3},{2,0},{3,1},{4,6},{5,7},{6,4},{7,5},{8,10},{9,11},{10,... | collective-permute-start | bytes 3145736 | tf_op jit(solution)/shard_map/ppermute | solution.py:734
  108.8 74.5 %collective-permute-start.8 = (bf16[128,4096]{1,0:T(8,128)(2,1)}, bf16[128,4096]{1,0:T(8,128)(2,1)}, u32[]{:S(2)}, u32[]{:S(2)}) collective-permute-start(bf16[128,4096]{1,0:T(8,128)(2,1)} %run_after.20.refs_0_), channel_id=1, source_target_pairs={{0,3},{1,2},{2,1},{3,0},{4,7},{5,6},{6,5},{7,4},{8,11},{9,10},{10,... | collective-permute-start | bytes 3145736 | tf_op jit(solution)/shard_map/ppermute | solution.py:734
  121.8 26.5 %all-to-all-start.2 = ((s32[4,4,576]{2,1,0:T(4,128)}), s32[4,4,576]{2,1,0:T(4,128)S(1)}, u32[]{:S(2)}, u32[]{:S(2)}) async-start(s32[4,4,576]{2,1,0:T(4,128)} %reshape.372), calls=%async_computation.2 | async-start | bytes 81920 | tf_op jit(solution)/shard_map/all_to_all | solution.py:766
  148.3 33.1 %all-to-all-start = ((bf16[4,576,256]{2,1,0:T(8,128)(2,1)}), bf16[4,576,256]{2,1,0:T(8,128)(2,1)S(1)}, u32[]{:S(2)}, u32[]{:S(2)}) async-start(bf16[4,576,256]{2,1,0:T(8,128)(2,1)} %bitcast.256), calls=%async_computation | async-start | bytes 2359296 | tf_op jit(solution)/shard_map/all_to_all | solution.py:954
  153.5 33.1 %collective-permute-start.9 = (bf16[128,4096]{1,0:T(8,128)(2,1)}, bf16[128,4096]{1,0:T(8,128)(2,1)}, u32[]{:S(2)}, u32[]{:S(2)}) collective-permute-start(bf16[128,4096]{1,0:T(8,128)(2,1)} %run_after.20.refs_0_), channel_id=1, source_target_pairs={{0,16},{16,0},{1,17},{17,1},{2,18},{18,2},{3,19},{19,3},{4,20},{20... | collective-permute-start | bytes 3145736 | tf_op jit(solution)/shard_map/ppermute | solution.py:749
  231.3 45.9 %all-to-all-start.3 = ((bf16[4,288,1024]{2,1,0:T(8,128)(2,1)}), bf16[4,288,1024]{2,1,0:T(8,128)(2,1)}, u32[]{:S(2)}, u32[]{:S(2)}) async-start(bf16[4,288,1024]{2,1,0:T(8,128)(2,1)} %pack_rows.4.refs_2_), calls=%async_computation.3 | async-start | bytes 4718592 | tf_op jit(solution)/shard_map/all_to_all | solution.py:766
  236.0 29.0 %collective-permute-start.13 = (bf16[576,1024]{1,0:T(8,128)(2,1)S(1)}, bf16[576,1024]{1,0:T(8,128)(2,1)}, u32[]{:S(2)}, u32[]{:S(2)}) collective-permute-start(bf16[576,1024]{1,0:T(8,128)(2,1)S(1)} %copy-done.38), channel_id=1, source_target_pairs={{0,4},{4,8},{8,12},{1,5},{5,9},{9,13},{2,6},{6,10},{10,14},{3,7},{... | collective-permute-start | bytes 3538952 | tf_op jit(solution)/shard_map/ppermute | solution.py:982
  240.4 29.7 %collective-permute-start.14 = (bf16[576,1024]{1,0:T(8,128)(2,1)S(1)}, bf16[576,1024]{1,0:T(8,128)(2,1)S(1)}, u32[]{:S(2)}, u32[]{:S(2)}) collective-permute-start(bf16[576,1024]{1,0:T(8,128)(2,1)S(1)} %copy-done.38), channel_id=1, source_target_pairs={{4,0},{8,4},{12,8},{5,1},{9,5},{13,9},{6,2},{10,6},{14,10},{7,3},{... | collective-permute-start | bytes 3538952 | tf_op jit(solution)/shard_map/ppermute | solution.py:985
  277.3 42.4 %all-to-all-start.4 = ((bf16[4,288,1024]{2,1,0:T(8,128)(2,1)}), bf16[4,288,1024]{2,1,0:T(8,128)(2,1)}, u32[]{:S(2)}, u32[]{:S(2)}) async-start(bf16[4,288,1024]{2,1,0:T(8,128)(2,1)} %pack_rows.5), calls=%async_computation.4 | async-start | bytes 4718592 | tf_op jit(solution)/shard_map/all_to_all | solution.py:766
  282.5 30.3 %collective-permute-start.16 = (bf16[576,1024]{1,0:T(8,128)(2,1)}, bf16[576,1024]{1,0:T(8,128)(2,1)S(1)}, u32[]{:S(2)}, u32[]{:S(2)}) collective-permute-start(bf16[576,1024]{1,0:T(8,128)(2,1)} %get-tuple-element.56.refs_1_.refs_2_), channel_id=1, source_target_pairs={{4,0},{8,4},{5,1},{9,5},{6,2},{10,6},{7,3},{11,7},{20,16},{24,20},... | collective-permute-start | bytes 3538952 | tf_op jit(solution)/shard_map/ppermute | solution.py:985
  319.7 40.5 %all-to-all-start.5 = ((bf16[4,288,1024]{2,1,0:T(8,128)(2,1)}), bf16[4,288,1024]{2,1,0:T(8,128)(2,1)}, u32[]{:S(2)}, u32[]{:S(2)}) async-start(bf16[4,288,1024]{2,1,0:T(8,128)(2,1)} %pack_rows.6), calls=%async_computation.5 | async-start | bytes 4718592 | tf_op jit(solution)/shard_map/all_to_all | solution.py:766
  324.4 27.9 %collective-permute-start.17 = (bf16[576,1024]{1,0:T(8,128)(2,1)S(1)}, bf16[576,1024]{1,0:T(8,128)(2,1)S(1)}, u32[]{:S(2)}, u32[]{:S(2)}) collective-permute-start(bf16[576,1024]{1,0:T(8,128)(2,1)S(1)} %copy-done.14), channel_id=1, source_target_pairs={{4,0},{5,1},{6,2},{7,3},{20,16},{21,17},{22,18},{23,19}} | collective-permute-start | bytes 3538952 | tf_op jit(solution)/shard_map/ppermute | solution.py:985
  325.7 26.6 %collective-permute-start.18 = (bf16[576,1024]{1,0:T(8,128)(2,1)S(1)}, bf16[576,1024]{1,0:T(8,128)(2,1)S(1)}, u32[]{:S(2)}, u32[]{:S(2)}) collective-permute-start(bf16[576,1024]{1,0:T(8,128)(2,1)S(1)} %copy-done.12), channel_id=1, source_target_pairs={{8,12},{9,13},{10,14},{11,15},{24,28},{25,29},{26,30},{27,31}} | collective-permute-start | bytes 3538952 | tf_op jit(solution)/shard_map/ppermute | solution.py:982
  360.3 40.0 %all-to-all-start.6 = ((bf16[4,288,1024]{2,1,0:T(8,128)(2,1)}), bf16[4,288,1024]{2,1,0:T(8,128)(2,1)}, u32[]{:S(2)}, u32[]{:S(2)}) async-start(bf16[4,288,1024]{2,1,0:T(8,128)(2,1)} %pack_rows.7), calls=%async_computation.6 | async-start | bytes 4718592 | tf_op jit(solution)/shard_map/all_to_all | solution.py:766
  460.2 27.2 %all-to-all-start.10 = ((bf16[4,288,1024]{2,1,0:T(8,128)(2,1)}), bf16[4,288,1024]{2,1,0:T(8,128)(2,1)}, u32[]{:S(2)}, u32[]{:S(2)}) async-start(bf16[4,288,1024]{2,1,0:T(8,128)(2,1)} %bitcast.243), calls=%async_computation.10 | async-start | bytes 4718592 | tf_op jit(solution)/shard_map/all_to_all | solution.py:766
  487.5 31.7 %all-to-all-start.9 = ((bf16[4,288,1024]{2,1,0:T(8,128)(2,1)}), bf16[4,288,1024]{2,1,0:T(8,128)(2,1)}, u32[]{:S(2)}, u32[]{:S(2)}) async-start(bf16[4,288,1024]{2,1,0:T(8,128)(2,1)} %bitcast.242), calls=%async_computation.9 | async-start | bytes 4718592 | tf_op jit(solution)/shard_map/all_to_all | solution.py:766
  497.2 27.4 %collective-permute-start.19 = (bf16[576,1024]{1,0:T(8,128)(2,1)}, bf16[576,1024]{1,0:T(8,128)(2,1)S(1)}, u32[]{:S(2)}, u32[]{:S(2)}) collective-permute-start(bf16[576,1024]{1,0:T(8,128)(2,1)} %unpack_rows.4.refs_7_), channel_id=1, source_target_pairs={{0,4},{1,5},{2,6},{3,7},{16,20},{17,21},{18,22},{19,23}} | collective-permute-start | bytes 3538952 | tf_op jit(solution)/shard_map/ppermute | solution.py:728
  500.0 24.6 %collective-permute-start.20 = (bf16[576,1024]{1,0:T(8,128)(2,1)}, bf16[576,1024]{1,0:T(8,128)(2,1)}, u32[]{:S(2)}, u32[]{:S(2)}) collective-permute-start(bf16[576,1024]{1,0:T(8,128)(2,1)} %unpack_rows.4.refs_7_), channel_id=1, source_target_pairs={{12,8},{13,9},{14,10},{15,11},{28,24},{29,25},{30,26},{31,27}} | collective-permute-start | bytes 3538952 | tf_op jit(solution)/shard_map/ppermute | solution.py:729
  519.2 32.7 %all-to-all-start.12 = ((bf16[4,288,1024]{2,1,0:T(8,128)(2,1)}), bf16[4,288,1024]{2,1,0:T(8,128)(2,1)}, u32[]{:S(2)}, u32[]{:S(2)}) async-start(bf16[4,288,1024]{2,1,0:T(8,128)(2,1)} %bitcast.245), calls=%async_computation.12 | async-start | bytes 4718592 | tf_op jit(solution)/shard_map/all_to_all | solution.py:766
  535.4 28.1 %collective-permute-start.21 = (bf16[576,1024]{1,0:T(8,128)(2,1)}, bf16[576,1024]{1,0:T(8,128)(2,1)S(1)}, u32[]{:S(2)}, u32[]{:S(2)}) collective-permute-start(bf16[576,1024]{1,0:T(8,128)(2,1)} %get-tuple-element.114), channel_id=1, source_target_pairs={{0,4},{4,8},{1,5},{5,9},{2,6},{6,10},{3,7},{7,11},{16,20},{20,24},... | collective-permute-start | bytes 3538952 | tf_op jit(solution)/shard_map/ppermute | solution.py:728
  539.8 23.7 %collective-permute-start.22 = (bf16[576,1024]{1,0:T(8,128)(2,1)}, bf16[576,1024]{1,0:T(8,128)(2,1)}, u32[]{:S(2)}, u32[]{:S(2)}) collective-permute-start(bf16[576,1024]{1,0:T(8,128)(2,1)} %get-tuple-element.115), channel_id=1, source_target_pairs={{8,4},{12,8},{9,5},{13,9},{10,6},{14,10},{11,7},{15,11},{24,20},{2... | collective-permute-start | bytes 3538952 | tf_op jit(solution)/shard_map/ppermute | solution.py:729
  551.8 30.7 %all-to-all-start.11 = ((bf16[4,288,1024]{2,1,0:T(8,128)(2,1)}), bf16[4,288,1024]{2,1,0:T(8,128)(2,1)}, u32[]{:S(2)}, u32[]{:S(2)}) async-start(bf16[4,288,1024]{2,1,0:T(8,128)(2,1)} %bitcast.244), calls=%async_computation.11 | async-start | bytes 4718592 | tf_op jit(solution)/shard_map/all_to_all | solution.py:766
  556.4 154.1 %reduce-scatter.7.cloned.1.call-start = ((), (), s32[]{:S(2)}) async-start(), calls=%async_computation.24 | async-start | bytes 5242880
  574.2 28.9 %collective-permute-start.24 = (bf16[576,1024]{1,0:T(8,128)(2,1)}, bf16[576,1024]{1,0:T(8,128)(2,1)S(1)}, u32[]{:S(2)}, u32[]{:S(2)}) collective-permute-start(bf16[576,1024]{1,0:T(8,128)(2,1)} %get-tuple-element.113), channel_id=1, source_target_pairs={{4,0},{8,4},{12,8},{5,1},{9,5},{13,9},{6,2},{10,6},{14,10},{7,3},{... | collective-permute-start | bytes 3538952 | tf_op jit(solution)/shard_map/ppermute | solution.py:729
  575.5 28.9 %collective-permute-start.23 = (bf16[576,1024]{1,0:T(8,128)(2,1)}, bf16[576,1024]{1,0:T(8,128)(2,1)S(1)}, u32[]{:S(2)}, u32[]{:S(2)}) collective-permute-start(bf16[576,1024]{1,0:T(8,128)(2,1)} %get-tuple-element.112), channel_id=1, source_target_pairs={{0,4},{4,8},{8,12},{1,5},{5,9},{9,13},{2,6},{6,10},{10,14},{3,7},{... | collective-permute-start | bytes 3538952 | tf_op jit(solution)/shard_map/ppermute | solution.py:728
  692.6 23.9 %collective-permute-start.26 = (bf16[4,128,5120]{2,1,0:T(8,128)(2,1)}, bf16[4,128,5120]{2,1,0:T(8,128)(2,1)}, u32[]{:S(2)}, u32[]{:S(2)}) collective-permute-start(bf16[4,128,5120]{2,1,0:T(8,128)(2,1)} %dynamic-slice_bitcast_fusion), channel_id=1, source_target_pairs={{0,16},{16,0},{1,17},{17,1},{2,18},{18,2},{3,19},{19,3},{4,20},{20... | collective-permute-start | bytes 15728648 | tf_op jit(solution)/shard_map/ppermute | solution.py:749
  712.9 18.8 %all-to-all-start.13 = ((bf16[576,4,256]{2,0,1:T(8,128)(2,1)}), bf16[576,4,256]{2,0,1:T(8,128)(2,1)S(1)}, u32[]{:S(2)}, u32[]{:S(2)}) async-start(bf16[576,4,256]{2,0,1:T(8,128)(2,1)} %bitcast.204), calls=%async_computation.13 | async-start | bytes 2359296 | tf_op jit(solution)/shard_map/all_to_all | solution.py:1082
  716.4 86.1 %reduce-scatter.9.cloned.1.call-start = ((), (), s32[]{:S(2)}) async-start(), calls=%async_computation.25 | async-start | bytes 6553600
  732.7 34.5 %all-to-all-start.14 = ((bf16[4,128,1024]{2,1,0:T(8,128)(2,1)}), bf16[4,128,1024]{2,1,0:T(8,128)(2,1)S(1)}, u32[]{:S(2)}, u32[]{:S(2)}) async-start(bf16[4,128,1024]{2,1,0:T(8,128)(2,1)} %bitcast.233), calls=%async_computation.14 | async-start | bytes 2097152 | tf_op jit(solution)/shard_map/all_to_all | solution.py:766
  785.9 16.6 %all-to-all-start.15 = ((bf16[4,128,896]{2,1,0:T(8,128)(2,1)}), bf16[4,128,896]{2,1,0:T(8,128)(2,1)S(1)}, u32[]{:S(2)}, u32[]{:S(2)}) async-start(bf16[4,128,896]{2,1,0:T(8,128)(2,1)} %fusion.19.refs_1_), calls=%async_computation.15 | async-start | bytes 1835008 | tf_op jit(solution)/shard_map/all_to_all | solution.py:766
  803.4 52.6 %all-to-all-start.16 = ((bf16[4,32,5120]{2,1,0:T(8,128)(2,1)}), bf16[4,32,5120]{2,1,0:T(8,128)(2,1)}, u32[]{:S(2)}, u32[]{:S(2)}) async-start(bf16[4,32,5120]{2,1,0:T(8,128)(2,1)} %bitcast.255), calls=%async_computation.16 | async-start | bytes 2621440 | tf_op jit(solution)/shard_map/all_to_all | solution.py:766
  808.2 122.2 %all-gather.11.cloned.1.call-start = ((), (), s32[]{:S(2)}) async-start(), calls=%async_computation.23 | async-start | bytes 1310720 | tf_op jit(solution)/shard_map/all_gather | solution.py:1158
  819.0 50.2 %collective-permute-start.28 = (bf16[576,1024]{1,0:T(8,128)(2,1)}, bf16[576,1024]{1,0:T(8,128)(2,1)S(1)}, u32[]{:S(2)}, u32[]{:S(2)}) collective-permute-start(bf16[576,1024]{1,0:T(8,128)(2,1)} %get-tuple-element.107), channel_id=1, source_target_pairs={{0,1},{1,0},{2,3},{3,2},{4,5},{5,4},{6,7},{7,6},{8,9},{9,8},{10,11... | collective-permute-start | bytes 3538952 | tf_op jit(solution)/shard_map/ppermute | solution.py:734
  820.4 48.8 %collective-permute-start.29 = (bf16[576,1024]{1,0:T(8,128)(2,1)}, bf16[576,1024]{1,0:T(8,128)(2,1)S(1)}, u32[]{:S(2)}, u32[]{:S(2)}) collective-permute-start(bf16[576,1024]{1,0:T(8,128)(2,1)} %get-tuple-element.106), channel_id=1, source_target_pairs={{0,2},{1,3},{2,0},{3,1},{4,6},{5,7},{6,4},{7,5},{8,10},{9,11},{10,... | collective-permute-start | bytes 3538952 | tf_op jit(solution)/shard_map/ppermute | solution.py:734
  858.2 28.1 %collective-permute-start.30 = (bf16[576,1024]{1,0:T(8,128)(2,1)}, bf16[576,1024]{1,0:T(8,128)(2,1)}, u32[]{:S(2)}, u32[]{:S(2)}) collective-permute-start(bf16[576,1024]{1,0:T(8,128)(2,1)} %get-tuple-element.105), channel_id=1, source_target_pairs={{0,3},{1,2},{2,1},{3,0},{4,7},{5,6},{6,5},{7,4},{8,11},{9,10},{10,... | collective-permute-start | bytes 3538952 | tf_op jit(solution)/shard_map/ppermute | solution.py:734
  859.8 29.3 %all-to-all-start.17 = ((bf16[4,32,3200]{2,1,0:T(8,128)(2,1)}), bf16[4,32,3200]{2,1,0:T(8,128)(2,1)S(1)}, u32[]{:S(2)}, u32[]{:S(2)}) async-start(bf16[4,32,3200]{2,1,0:T(8,128)(2,1)} %bitcast.248), calls=%async_computation.17 | async-start | bytes 1638400 | tf_op jit(solution)/shard_map/all_to_all | solution.py:766
  863.9 67.1 %all-gather.9.cloned.1.call-start = ((), (), s32[]{:S(2)}) async-start(), calls=%async_computation.22 | async-start | bytes 1638400 | tf_op jit(solution)/shard_map/all_gather | solution.py:796
  899.1 22.4 %collective-permute-start.32 = (bf16[32,3200]{1,0:T(8,128)(2,1)}, bf16[32,3200]{1,0:T(8,128)(2,1)S(1)}, u32[]{:S(2)}, u32[]{:S(2)}) collective-permute-start(bf16[32,3200]{1,0:T(8,128)(2,1)} %run_after.34.refs_1_), channel_id=1, source_target_pairs={{0,8},{4,12},{8,0},{12,4},{1,9},{5,13},{9,1},{13,5},{2,10},{6,14},... | collective-permute-start | bytes 614408 | tf_op jit(solution)/shard_map/ppermute | solution.py:802
  899.1 22.4 %collective-permute-start.31 = (bf16[32,3200]{1,0:T(8,128)(2,1)}, bf16[32,3200]{1,0:T(8,128)(2,1)S(1)}, u32[]{:S(2)}, u32[]{:S(2)}) collective-permute-start(bf16[32,3200]{1,0:T(8,128)(2,1)} %run_after.34.refs_1_), channel_id=1, source_target_pairs={{0,4},{4,8},{8,12},{12,0},{1,5},{5,9},{9,13},{13,1},{2,6},{6,10},{... | collective-permute-start | bytes 614408 | tf_op jit(solution)/shard_map/ppermute | solution.py:802
  (85 other events, 719.4 us)
Sparse Core Ops, SparseCore 0:
  85.8 33.1 all-gather.4
  121.5 86.3 all-gather.6
  656.8 53.6 reduce-scatter.6
  732.9 61.7 reduce-scatter.8
  810.4 44.5 all-gather.10
  869.3 49.7 all-gather.8

commit v3 on v2

--- a/solution.py
+++ b/solution.py
@@ -414,9 +414,46 @@
     )(order, *blocks, *weights, vectors)
 
 
-def to_columns(block, rows):
-    parts = [block[group].T for group in range(block.shape[0])]
-    return parts[0] if len(parts) == 1 else jnp.concatenate(parts, axis=0)
+def planes_kernel(spacing, keys_ref, planes_ref, turned_ref, square_ref, wide_ref):
+    near_count = keys_ref.shape[0] // spacing
+
+    @pl.when(pl.program_id(0) == 0)
+    def _():
+        square_ref[...] = jnp.zeros_like(square_ref)
+
+    wide_ref[...] = keys_ref[...].astype(jnp.float32)
+    for plane in range(spacing):
+        rows = slice(plane * near_count, (plane + 1) * near_count)
+        keys = wide_ref[pl.ds(plane, near_count, stride=spacing), :]
+        planes_ref[rows, :] = keys.astype(jnp.bfloat16)
+        turned = keys.T
+        turned_ref[:, rows] = turned.astype(jnp.bfloat16)
+        square_ref[plane : plane + 1, :] += jnp.sum(turned * turned, axis=0, keepdims=True)
+
+
+def key_planes(keys, spacing):
+    count, width = keys.shape
+    columns = row_chunk(width, (128,))
+    near_count = count // spacing
+    return pl.pallas_call(
+        functools.partial(planes_kernel, spacing),
+        grid=(width // columns,),
+        in_specs=[spec((count, columns), lambda i: (0, i))],
+        out_specs=[
+            spec((count, columns), lambda i: (0, i)),
+            spec((columns, count), lambda i: (i, 0)),
+            spec((spacing, near_count), lambda i: (0, 0)),
+        ],
+        out_shape=[
+            jax.ShapeDtypeStruct((count, width), jnp.bfloat16),
+            jax.ShapeDtypeStruct((width, count), jnp.bfloat16),
+            jax.ShapeDtypeStruct((spacing, near_count), jnp.float32),
+        ],
+        scratch_shapes=[pltpu.VMEM((count, columns), jnp.float32)],
+        compiler_params=kernel_params(),
+        cost_estimate=small_cost,
+        name="key_planes",
+    )(keys)
 
 
 def near_kernel(spacing, dist_scale, parts, *refs):
@@ -579,7 +616,9 @@
         ),
         out_shape=jax.ShapeDtypeStruct((owners, capacity, width), options[0].dtype),
         compiler_params=kernel_params(),
-        cost_estimate=small_cost,
+        cost_estimate=pl.CostEstimate(
+            flops=30_000_000_000, bytes_accessed=1000, transcendentals=0
+        ),
         name="pack_rows",
     )(pick, *options, slot_map, *after)
 
@@ -792,16 +831,16 @@
     return both.reshape(-1, half.shape[-1]).astype(jnp.float32)
 
 
-def shard_gather(rows):
-    return both_halves(lax.all_gather(rows, "batch"))
-
-
 def layer_gather(rows):
-    count, layer = lax.axis_size("batch"), lax.axis_index("batch")
-    parts = [rows] + [
+    count = lax.axis_size("batch")
+    return [rows] + [
         lax.ppermute(rows, "batch", [(i, (i + hops) % count) for i in range(count)])
         for hops in range(1, count)
     ]
+
+
+def whole_shard(parts):
+    count, layer = len(parts), lax.axis_index("batch")
     return both_halves(jnp.stack(parts)[(layer - jnp.arange(count, dtype=jnp.int32)) % count])
 
 
@@ -902,11 +941,7 @@
         jnp.where(slot_picker(slot_map, capacity), targets.reshape(1, 1, -1), 0), axis=2
     )
     got_targets = exchange(send_targets.astype(jnp.int32), everyone).astype(jnp.float32)
-    planes = store_keys.reshape(near_count, spacing, width).transpose(1, 0, 2)
-    planes = planes.reshape(key_count, width)
-    planes_turned = planes.T
-    key_square = jnp.sum(jnp.square(store_keys.astype(jnp.float32)), axis=1)
-    key_square = key_square.reshape(near_count, spacing).T
+    planes, planes_turned, key_square = key_planes(store_keys, spacing)
     value_planes = store_values.astype(jnp.float32).reshape(near_count, spacing).T
     by_layer = capacity % 16 == 0
     if by_layer:
@@ -1041,7 +1076,7 @@
                 back,
                 maps[step],
                 jnp.bfloat16 if step > 0 else jnp.float32,
-                [above, below] if hop > 0 else [],
+                [above, below] if 0 < hop < layer_count - 1 else [],
             )
         query_grad = returned[0] + above.astype(jnp.float32) + below.astype(jnp.float32)
     else:
@@ -1083,6 +1118,8 @@
     second_half = run_after([second_half], [grad_own])[0]
     downward_half = run_after([downward_half], [second_half])[0]
     downward_total = layer_total(layer_blocks(downward_half))
+    second_start = second_half
+    second_half = ctx_reduce(second_half)
     proj_grad = jnp.concatenate(
         run_after(
             attend_back(
@@ -1096,12 +1133,18 @@
                 low_blocks,
                 own_heads,
                 attend_size,
-                (second_half, downward_half),
+                (second_start, downward_half),
             ),
             [downward_total],
         ),
         axis=1,
     )
+    normed_terms = right_dot(proj_grad, proj_own).astype(jnp.bfloat16)
+    normed_grad = lax.psum_scatter(normed_terms, "ctx", scatter_dimension=0, tiled=True)
+
+    second_half = run_after([second_half], [normed_terms])[0]
+    second_total = layer_total(layer_blocks(second_half))
+    second_parts = layer_gather(second_total)
     plain_part = left_dot(plain_full, proj_grad)
     column_sums = jnp.sum(proj_grad.astype(jnp.float32), axis=0)
     proj_full = proj_own.astype(jnp.float32)
@@ -1121,19 +1164,17 @@
         axis=1,
     )
     vector_part = jnp.pad(vector_part, ((0, 0), (0, 128 - vector_part.shape[1])))
-    project_part = jnp.concatenate([project_part, vector_part], axis=1)
-    project_part = reduce_cores(project_part)
-    normed_terms = right_dot(proj_grad, run_after([proj_own], [project_part])[0])
-    term_blocks = normed_terms.astype(jnp.bfloat16).reshape(ctx_count, block_len, width)
-    term_parts = ctx_trade(
-        [
-            lax.dynamic_index_in_dim(term_blocks, own_ctx ^ step, 0, keepdims=False)
-            for step in range(ctx_count)
-        ]
-    )
-    project_part = exchange(project_part, "ctx")
-    second_part = run_after([ctx_reduce(second_half)], [project_part])[0]
-    second_total = layer_total(layer_blocks(second_part))
+    project_part = jnp.concatenate([project_part, vector_part], axis=1).astype(jnp.bfloat16)
+    project_part = reduce_cores(run_after([project_part], [second_total])[0])
+    downward_parts = layer_gather(run_after([downward_total], [project_part])[0])
+    project_part = in_ctx_order(
+        ctx_trade(
+            [
+                lax.dynamic_index_in_dim(project_part, own_ctx ^ step, 0, keepdims=False)
+                for step in range(ctx_count)
+            ]
+        )
+    )
     vector_part = block_sum(project_part[:, :, 3 * own_width :]).astype(jnp.bfloat16)
     project_part = (
         project_part[:, :, : 3 * own_width]
@@ -1142,21 +1183,18 @@
         .reshape(own_rows // 2, 3 * width)
     )
     small_rows = jnp.concatenate([project_part, vector_part], axis=1)
-    term_parts = [term_parts[0], *run_after(term_parts[1:], [second_total])]
-    small_rows = run_after([small_rows], [second_total])[0]
+    small_rows = run_after([small_rows], second_parts[1:])[0]
     small_total = layer_total(layer_blocks(small_rows))
-    small_total = run_after([small_total], term_parts[1:])[0]
     input_vjp = jax.vjp(lambda rows: norm_rows(rows, gain_list[0], gain_list[1]), inputs)[1]
-    input_grad = hidden_grad + input_vjp(block_sum(term_parts))[0]
-    small_grads = layer_gather(small_total)
-    second_grads = shard_gather(second_total)
+    normed_grad = run_after([normed_grad], [small_total])[0]
+    input_grad = hidden_grad + input_vjp(normed_grad.astype(jnp.float32))[0]
+    small_grads = whole_shard(layer_gather(small_total))
+    second_grads = whole_shard(second_parts)
     weight_grads = [
         small_grads[:, : 3 * width],
         second_grads[:, second_grads.shape[1] - width :],
         second_grads[:, : second_grads.shape[1] - width],
-        both_halves(
-            run_after([lax.all_gather(downward_total, "batch")], [small_total])[0]
-        ),
+        whole_shard(downward_parts),
     ]
     vector_grads = small_grads[:, 3 * width : 3 * width + 6].T
     return (

time: 958 us -> 940 us (0.981)
  waiting for transfers between devices: 312 us -> 266 us
  starting transfers between devices: 125 us -> 135 us
    all_to_all x14 -> x13, waiting for transfers between devices: 62.6 us -> 38.9 us  [exchange(): return lax.all_to_all(blocks, axis, split_axis=0, concat_axis=0, tiled=True)]
    ppermute x3, waiting for transfers between devices: 59.9 us -> 39.8 us  [local(): lax.ppermute(down, 'batch', [(i, i - 1) for i in range(1, layer_count - s...]
    ppermute x12, waiting for transfers between devices: 76.4 us -> 59.3 us  [across(): lax.ppermute(rows, 'ctx', [(i, i ^ step) for i in range(lax.axis_size('ct...]
    unnamed x8 -> x7, waiting for transfers between devices: 15.2 us -> 31.7 us
    all_to_all x14 -> x13, starting transfers between devices: 64.7 us -> 58.6 us  [exchange(): return lax.all_to_all(blocks, axis, split_axis=0, concat_axis=0, tiled=True)]
    unnamed x151 -> x166, local copies, waits for them, and re-layouts: 27.6 us -> 23.6 us
    ppermute x3 -> x9, waiting for transfers between devices: 21.5 us -> 24.1 us  [layer_gather(): lax.ppermute(rows, 'batch', [(i, (i + hops) % count) for i in range(count)])]
  transfers between devices with their start and end apart: 59 -> 63, of which waited for: 27 -> 27; matrix products, arithmetic and copies ran while one was open for 19% -> 21% of each run, Pallas kernels for 18% -> 20%
where the time goes in v3:
time: 940 us; the launch traced here: 933 us
  waiting for transfers between devices  266 us (28%)
  Pallas kernels  220 us (23%)
  starting transfers between devices  135 us (14%)
  matrix products  89.5 us (10%)
  local copies, waits for them, and re-layouts  89.3 us (10%)
  other arithmetic  87.6 us (9%)
  blocking collectives  29.9 us (3%)
  between operations  15.3 us (2%)
    ppermute x12, waiting for transfers between devices, across(): lax.ppermute(rows, 'ctx', [(i, i ^ step) for i in range(lax.axis_size('ct...  59.3 us
    all_to_all x13, starting transfers between devices, exchange(): return lax.all_to_all(blocks, axis, split_axis=0, concat_axis=0, tiled=True)  58.6 us
    pallas_call x4, Pallas kernels, near_scores(): pl.pallas_call(functools.partial(near_kernel, spacing, width ** (-0.5), p...  44.4 us
    pallas_call x4, Pallas kernels, near_back(): pl.pallas_call(later(functools.partial(near_back_kernel, spacing, 2.0 * w...  41.5 us
    ppermute x3, waiting for transfers between devices, local(): lax.ppermute(down, 'batch', [(i, i - 1) for i in range(1, layer_count - s...  39.8 us
    all_to_all x13, waiting for transfers between devices, exchange(): return lax.all_to_all(blocks, axis, split_axis=0, concat_axis=0, tiled=True)  38.9 us
    dot_general x4, matrix products, right_dot(): lax.dot_general(left_side, right_side, (((1,), (1,)), ((), ())), preferre...  35.1 us
    unnamed x7, waiting for transfers between devices  31.7 us
  transfers between devices with their start and end apart: 63, of which 27 were waited for; matrix products, arithmetic and copies ran while one was open for 21% of the time, Pallas kernels for 20%

profile of v3, /device:TPU:0, one launch (start us, length us, event | category | flops | bytes accessed | tf_op | source)
XLA Modules:
  0.0 932.7 jit_solution(2882257607961165868)
XLA Ops:
  22.1 50.8 %collective-permute-done.5.refs_7_.refs_6_ = bf16[256,896]{1,0:T(8,128)(2,1)} collective-permute-done((bf16[256,896]{1,0:T(8,128)(2,1)S(1)}, bf16[256,896]{1,0:T(8,128)(2,1)}, u32[]{:S(2)}, u32[]{:S(2)}) %collective-permute-start.5) | collective-permute-done | bytes 458784 | tf_op jit(solution)/shard_map/ppermute | solution.py:773
  76.1 6.8 collective-permute-done.4.refs_6_.refs_5_
  89.9 6.2 all-to-all-start.1
  108.9 13.0 %project_rows.1 = (bf16[1024,768]{1,0:T(8,128)(2,1)}, bf16[2304,1024]{1,0:T(8,128)(2,1)}, bf16[2304,1024]{1,0:T(8,128)(2,1)}, bf16[2304,256]{1,0:T(8,128)(2,1)},...) custom-call(s32[4]{0:T(128)} %iota_xor_fusion.order_ref, bf16[576,1024]{1,0:T(8,128)(2,1)} %bitcast.218, ...), custom_call_target="tpu_custom_call" | custom-call | flops 12999999488 | bytes 1000 | tf_op jit(solution)/shard_map/project_rows/pallas_call | solution.py:392
  127.7 19.5 %attend.1 = (bf16[2304,256]{1,0:T(8,128)(2,1)}, f32[8,2304]{1,0:T(8,128)}) custom-call(s32[18]{0:T(128)} %pad_add_fusion.refs_0_, bf16[2304,256]{1,0:T(8,128)(2,1)} %get-tuple-element.48.refs_1_, bf16[2304,256]{1,0:T(8,128)(2,1)} %get-tuple-element.49.refs_2_, bf16[2304,256]{1,0:T(8,128)(2,1)} %get-tuple-element.50.refs_3_, ...), custom_call_target="tpu_custom_call" | custom-call | flops 20000000000 | bytes 1000 | tf_op jit(solution)/shard_map/attend/pallas_call | solution.py:193
  153.6 27.7 %all-to-all-done = bf16[4,576,256]{2,1,0:T(8,128)(2,1)S(1)} async-done(((bf16[4,576,256]{2,1,0:T(8,128)(2,1)}), bf16[4,576,256]{2,1,0:T(8,128)(2,1)S(1)}, u32[]{:S(2)}, u32[]{:S(2)}) %all-to-all-start) | async-done | bytes 1179680 | tf_op jit(solution)/shard_map/all_to_all | solution.py:989
  184.8 8.5 key_planes.1
  195.8 9.0 place_rows.1
  209.5 7.8 fusion.39
  217.3 12.6 %fusion.44 = (f32[576]{0:T(1024)S(1)}, f32[576,1024]{1,0:T(8,128)S(1)}) fusion(f32[576,1024]{1,0:T(8,128)} %copy-done.16, bf16[4096,1024]{1,0:T(8,128)(2,1)} %all-gather.5.cloned.1.call-done, f32[576,4096]{1,0:T(8,128)} %fusion.39), kind=kOutput, calls=%fused_computation.214 | convolution fusion | flops 4854251008 | bytes 22546688 | tf_op jit(solution)/shard_map/dot_general | solution.py:28
  246.4 14.8 %collective-permute-done.13.refs_0_ = bf16[576,1024]{1,0:T(8,128)(2,1)} collective-permute-done((bf16[576,1024]{1,0:T(8,128)(2,1)S(1)}, bf16[576,1024]{1,0:T(8,128)(2,1)}, u32[]{:S(2)}, u32[]{:S(2)}) %collective-permute-start.13) | collective-permute-done | bytes 1179680 | tf_op jit(solution)/shard_map/ppermute | solution.py:1017
  268.4 6.1 pack_rows.5
  279.4 18.7 %collective-permute-done.16.refs_1_ = bf16[576,1024]{1,0:T(8,128)(2,1)} collective-permute-done((bf16[576,1024]{1,0:T(8,128)(2,1)}, bf16[576,1024]{1,0:T(8,128)(2,1)}, u32[]{:S(2)}, u32[]{:S(2)}) %collective-permute-start.16) | collective-permute-done | bytes 1179680 | tf_op jit(solution)/shard_map/ppermute | solution.py:1020
  301.1 5.9 pack_rows.6
  310.9 15.9 %collective-permute-done.17.refs_1_ = bf16[576,1024]{1,0:T(8,128)(2,1)S(1)} collective-permute-done((bf16[576,1024]{1,0:T(8,128)(2,1)}, bf16[576,1024]{1,0:T(8,128)(2,1)S(1)}, u32[]{:S(2)}, u32[]{:S(2)}) %collective-permute-start.17) | collective-permute-done | bytes 1179680 | tf_op jit(solution)/shard_map/ppermute | solution.py:1020
  327.8 5.9 pack_rows.7
  344.6 11.1 %near_scores.4 = (f32[1152,256]{1,0:T(8,128)}, f32[4,8,288]{2,1,0:T(8,128)}) custom-call(s32[4]{0:T(128)} %get-tuple-element.149.refs_0_, bf16[1152,1024]{1,0:T(8,128)(2,1)} %bitcast.214, bf16[1024,2048]{1,0:T(8,128)(2,1)} %get-tuple-element.55.refs_2_.refs_5_, f32[8,256]{1,0:T(8,128)} %get-tuple-element.56.refs_3_.refs_6_, f32[8,256]{1,0:T(8,128)} %bitcast.247, ...), custom_call_target="tpu_custom_call" | custom-call | flops 1000 | bytes 1000 | tf_op jit(solution)/shard_map/near_scores/pallas_call | solution.py:504
  355.7 11.1 %near_scores.5 = (f32[1152,256]{1,0:T(8,128)}, f32[4,8,288]{2,1,0:T(8,128)}) custom-call(s32[4]{0:T(128)} %get-tuple-element.152.refs_0_, bf16[1152,1024]{1,0:T(8,128)(2,1)} %bitcast.29.refs_1_, bf16[1024,2048]{1,0:T(8,128)(2,1)} %get-tuple-element.55.refs_2_.refs_5_, f32[8,256]{1,0:T(8,128)} %get-tuple-element.56.refs_3_.refs_6_, f32[8,256]{1,0:T(8,128)} %bitcast.248, ...), custom_call_target="tpu_custom_call" | custom-call | flops 1000 | bytes 1000 | tf_op jit(solution)/shard_map/near_scores/pallas_call | solution.py:504
  366.7 11.1 %near_scores.6 = (f32[1152,256]{1,0:T(8,128)}, f32[4,8,288]{2,1,0:T(8,128)}) custom-call(s32[4]{0:T(128)} %get-tuple-element.151.refs_0_, bf16[1152,1024]{1,0:T(8,128)(2,1)} %bitcast.229, bf16[1024,2048]{1,0:T(8,128)(2,1)} %get-tuple-element.55.refs_2_.refs_5_, f32[8,256]{1,0:T(8,128)} %get-tuple-element.56.refs_3_.refs_6_, f32[8,256]{1,0:T(8,128)} %bitcast.249, ...), custom_call_target="tpu_custom_call" | custom-call | flops 1000 | bytes 1000 | tf_op jit(solution)/shard_map/near_scores/pallas_call | solution.py:504
  377.8 11.2 %near_scores.7 = (f32[1152,256]{1,0:T(8,128)}, f32[4,8,288]{2,1,0:T(8,128)}) custom-call(s32[4]{0:T(128)} %get-tuple-element.150.refs_0_, bf16[1152,1024]{1,0:T(8,128)(2,1)} %bitcast.38.refs_1_, bf16[1024,2048]{1,0:T(8,128)(2,1)} %get-tuple-element.55.refs_2_.refs_5_, f32[8,256]{1,0:T(8,128)} %get-tuple-element.56.refs_3_.refs_6_, f32[8,256]{1,0:T(8,128)} %bitcast.250, ...), custom_call_target="tpu_custom_call" | custom-call | flops 1000 | bytes 1000 | tf_op jit(solution)/shard_map/near_scores/pallas_call | solution.py:504
  390.5 17.5 %all_to_all.117.stats_ref = f32[16,8,288]{2,1,0:T(8,128)} all-to-all(f32[16,8,288]{2,1,0:T(8,128)S(1)} %bitcast.246), channel_id=1, replica_groups=mesh['rep'=2,'batch'=4,'ctx'=4] {'batch','ctx'}, dimensions={0} | all-to-all | bytes 294912 | tf_op jit(solution)/shard_map/all_to_all | solution.py:805
  408.0 11.8 %mix_losses.1 = (f32[1,576]{1,0:T(1,128)}, f32[16,8,288]{2,1,0:T(8,128)}) custom-call(f32[16,8,288]{2,1,0:T(8,128)} %all_to_all.117.stats_ref, s32[16,576]{1,0:T(8,128)} %copy-done.41, f32[1,576]{1,0:T(1,128)} %prob_ref.1), custom_call_target="tpu_custom_call" | custom-call | tf_op jit(solution)/shard_map/mix_losses/pallas_call | solution.py:697
  419.8 12.4 %all_to_all.118.refs_4_.refs_5_ = f32[16,8,288]{2,1,0:T(8,128)} all-to-all(f32[16,8,288]{2,1,0:T(8,128)} %get-tuple-element.69), channel_id=1, replica_groups=mesh['rep'=2,'batch'=4,'ctx'=4] {'batch','ctx'}, dimensions={0} | all-to-all | bytes 294912 | tf_op jit(solution)/shard_map/all_to_all | solution.py:805
  432.2 10.4 %near_back.5 = bf16[1152,1024]{1,0:T(8,128)(2,1)} custom-call(s32[4]{0:T(128)} %get-tuple-element.150.refs_0_, f32[1152,256]{1,0:T(8,128)} %get-tuple-element.71.refs_1_, s32[16,288,256]{2,1,0:T(8,128)} %bitcast.203, s32[16,288,256]{2,1,0:T(8,128)} %bitcast.204, f32[16,8,288]{2,1,0:T(8,128)} %all_to_all.118.refs_4_.refs_5_, ...), custom_call_target="tpu_custom_call" | custom-call | flops 1000 | bytes 1000 | tf_op jit(solution)/shard_map/near_back/pallas_call | solution.py:557
  446.2 10.4 %near_back.4 = bf16[1152,1024]{1,0:T(8,128)(2,1)} custom-call(s32[4]{0:T(128)} %get-tuple-element.151.refs_0_, f32[1152,256]{1,0:T(8,128)} %get-tuple-element.70.refs_1_, s32[16,288,256]{2,1,0:T(8,128)} %bitcast.205, s32[16,288,256]{2,1,0:T(8,128)} %bitcast.206, f32[16,8,288]{2,1,0:T(8,128)} %all_to_all.118.refs_4_.refs_5_, ...), custom_call_target="tpu_custom_call" | custom-call | flops 1000 | bytes 1000 | tf_op jit(solution)/shard_map/near_back/pallas_call | solution.py:557
  456.6 13.9 %all-to-all-done.10.refs_0_ = bf16[4,288,1024]{2,1,0:T(8,128)(2,1)S(1)} async-done(((bf16[4,288,1024]{2,1,0:T(8,128)(2,1)}), bf16[4,288,1024]{2,1,0:T(8,128)(2,1)S(1)}, u32[]{:S(2)}, u32[]{:S(2)}) %all-to-all-start.10) | async-done | bytes 2359328 | tf_op jit(solution)/shard_map/all_to_all | solution.py:805
  487.0 10.4 %near_back.7 = bf16[1152,1024]{1,0:T(8,128)(2,1)} custom-call(s32[4]{0:T(128)} %get-tuple-element.152.refs_0_, f32[1152,256]{1,0:T(8,128)} %get-tuple-element.72.refs_1_, s32[16,288,256]{2,1,0:T(8,128)} %bitcast.207, s32[16,288,256]{2,1,0:T(8,128)} %bitcast.208, f32[16,8,288]{2,1,0:T(8,128)} %all_to_all.118.refs_4_.refs_5_, ...), custom_call_target="tpu_custom_call" | custom-call | flops 1000 | bytes 1000 | tf_op jit(solution)/shard_map/near_back/pallas_call | solution.py:557
  497.4 6.2 all-to-all-done.9.refs_0_
  525.9 10.4 %near_back.6 = bf16[1152,1024]{1,0:T(8,128)(2,1)} custom-call(s32[4]{0:T(128)} %get-tuple-element.149.refs_0_, f32[1152,256]{1,0:T(8,128)} %get-tuple-element.68.refs_1_, s32[16,288,256]{2,1,0:T(8,128)} %bitcast.209, s32[16,288,256]{2,1,0:T(8,128)} %bitcast.210, f32[16,8,288]{2,1,0:T(8,128)} %all_to_all.118.refs_4_.refs_5_, ...), custom_call_target="tpu_custom_call" | custom-call | flops 1000 | bytes 1000 | tf_op jit(solution)/shard_map/near_back/pallas_call | solution.py:557
  558.0 10.6 %collective-permute-start.23 = (bf16[576,1024]{1,0:T(8,128)(2,1)}, bf16[576,1024]{1,0:T(8,128)(2,1)}, u32[]{:S(2)}, u32[]{:S(2)}) collective-permute-start(bf16[576,1024]{1,0:T(8,128)(2,1)} %get-tuple-element.107), channel_id=1, source_target_pairs={{0,4},{4,8},{8,12},{1,5},{5,9},{9,13},{2,6},{6,10},{10,14},{3,7},{... | collective-permute-start | bytes 3538952 | tf_op jit(solution)/shard_map/ppermute | solution.py:767
  574.2 14.4 %collective-permute-done.24 = bf16[576,1024]{1,0:T(8,128)(2,1)} collective-permute-done((bf16[576,1024]{1,0:T(8,128)(2,1)}, bf16[576,1024]{1,0:T(8,128)(2,1)}, u32[]{:S(2)}, u32[]{:S(2)}) %collective-permute-start.24) | collective-permute-done | bytes 1179680 | tf_op jit(solution)/shard_map/ppermute | solution.py:768
  596.1 11.4 %convolution_convert_fusion.1 = bf16[4096,1024]{1,0:T(8,128)(2,1)S(1)} fusion(f32[576,1024]{1,0:T(8,128)S(1)} %get-tuple-element.101, f32[576]{0:T(1024)S(1)} %negate_multiply_fusion.2, f32[576,4096]{1,0:T(8,128)} %fusion.39), kind=kOutput, calls=%fused_computation.26 | convolution fusion | flops 4858445824 | bytes 20187392 | tf_op jit(solution)/shard_map/dot_general | solution.py:32
  612.2 16.3 %fusion.7.refs_0_ = bf16[576,4096]{1,0:T(8,128)(2,1)} fusion(f32[576,4096]{1,0:T(8,128)} %fusion.39, bf16[4096,1024]{1,0:T(8,128)(2,1)} %all-gather.5.cloned.1.call-done, f32[576,1024]{1,0:T(8,128)} %copy-done.21, f32[576]{0:T(1024)S(1)} %negate_multiply_fusion.2), kind=kOutput, calls=%fused_computation.21 | convolution fusion | flops 4880203776 | bytes 24905984 | tf_op jit(solution)/shard_map/dot_general | solution.py:38
  628.5 6.3 fusion.8.refs_1_
  635.5 10.6 %multiply_reduce_fusion.1 = (bf16[1024]{0:T(1024)(128)(2,1)}, f32[576]{0:T(1024)S(1)}, bf16[1024]{0:T(1024)(128)(2,1)}, f32[576,1024]{1,0:T(8,128)S(1)}) fusion(f32[576,1024]{1,0:T(8,128)} %copy-done.16, f32[576]{0:T(1024)S(1)} %copy-done.65, f32[576]{0:T(1024)S(1)} %copy-done.57, f32[1024]{0:T(1024)S(1)} %bitcast.268, bf16[576,4096]{1,0:T(8,128)(2,1)} %run_after.24, ...), kind=kOutput, calls=%fused_computation.55 | convolution fusion | flops 4836554240 | bytes 17840896 | tf_op jit(solution)/shard_map/dot_general | solution.py:38
  652.3 7.5 convolution_convert_fusion
  659.8 6.3 pad_maximum_fusion
  675.9 13.2 %reduce-scatter.10.cloned.1.call-done = bf16[1,512,1024]{2,1,0:T(8,128)(2,1)} async-done(((bf16[4,512,1024]{2,1,0:T(8,128)(2,1)}), bf16[1,512,1024]{2,1,0:T(8,128)(2,1)}) %reduce-scatter.10.cloned.1.call-update) | async-done | bytes 1048592
  695.0 8.4 fusion.refs_0_
  703.4 6.9 all-to-all-done.13
  715.9 28.0 %attend_back.1 = (bf16[2304,256]{1,0:T(8,128)(2,1)}, bf16[2304,256]{1,0:T(8,128)(2,1)}, bf16[2304,256]{1,0:T(8,128)(2,1)}) custom-call(s32[18]{0:T(128)} %pad_add_fusion.refs_0_, bf16[2304,256]{1,0:T(8,128)(2,1)} %get-tuple-element.48.refs_1_, bf16[2304,256]{1,0:T(8,128)(2,1)} %get-tuple-element.49.refs_2_, bf16[2304,256]{1,0:T(8,128)(2,1)} %get-tuple-element.50.refs_3_, ...), custom_call_target="tpu_custom_call" | custom-call | flops 1000 | bytes 1000 | tf_op jit(solution)/shard_map/attend_back/pallas_call | solution.py:328
  748.7 5.8 convolution_convert_fusion.2.refs_1_
  754.5 18.4 %reduce-scatter.12.cloned.1.call-done = bf16[1,128,5120]{2,1,0:T(8,128)(2,1)} async-done(((bf16[4,128,5120]{2,1,0:T(8,128)(2,1)}), bf16[1,128,5120]{2,1,0:T(8,128)(2,1)}) %reduce-scatter.12.cloned.1.call-update) | async-done | bytes 1310736
  787.0 8.4 fusion.14
  802.5 6.6 all-to-all-done.15
  825.5 10.8 %collective-permute-done.32.refs_2_ = bf16[32,5120]{1,0:T(8,128)(2,1)} collective-permute-done((bf16[32,5120]{1,0:T(8,128)(2,1)}, bf16[32,5120]{1,0:T(8,128)(2,1)}, u32[]{:S(2)}, u32[]{:S(2)}) %collective-permute-start.32) | collective-permute-done | bytes 327712 | tf_op jit(solution)/shard_map/ppermute | solution.py:837
  889.4 7.3 all-to-all-done.16
  903.8 10.3 %collective-permute-done.35 = bf16[32,3200]{1,0:T(8,128)(2,1)} collective-permute-done((bf16[32,3200]{1,0:T(8,128)(2,1)S(1)}, bf16[32,3200]{1,0:T(8,128)(2,1)}, u32[]{:S(2)}, u32[]{:S(2)}) %collective-permute-start.35) | collective-permute-done | bytes 204832 | tf_op jit(solution)/shard_map/ppermute | solution.py:837
  (441 shorter events, 332.8 us)
Async XLA Ops:
  7.2 197.7 %all-gather.3.cloned.1.call-start = ((), (), s32[]{:S(2)}) async-start(), calls=%async_computation.20 | async-start | bytes 2359296 | tf_op jit(solution)/shard_map/all_gather | solution.py:971
  7.2 77.4 %collective-permute-start = (bf16[576,1024]{1,0:T(8,128)(2,1)}, bf16[576,1024]{1,0:T(8,128)(2,1)S(1)}, u32[]{:S(2)}, u32[]{:S(2)}) collective-permute-start(bf16[576,1024]{1,0:T(8,128)(2,1)} %bitcast.215), channel_id=1, source_target_pairs={{0,1},{1,0},{2,3},{3,2},{4,5},{5,4},{6,7},{7,6},{8,9},{9,8},{10,11... | collective-permute-start | bytes 3538952 | tf_op jit(solution)/shard_map/ppermute | solution.py:773
  10.2 74.4 %collective-permute-start.1 = (bf16[576,1024]{1,0:T(8,128)(2,1)}, bf16[576,1024]{1,0:T(8,128)(2,1)}, u32[]{:S(2)}, u32[]{:S(2)}) collective-permute-start(bf16[576,1024]{1,0:T(8,128)(2,1)} %bitcast.216), channel_id=1, source_target_pairs={{0,2},{1,3},{2,0},{3,1},{4,6},{5,7},{6,4},{7,5},{8,10},{9,11},{10,... | collective-permute-start | bytes 3538952 | tf_op jit(solution)/shard_map/ppermute | solution.py:773
  11.8 72.8 %collective-permute-start.2 = (bf16[576,1024]{1,0:T(8,128)(2,1)}, bf16[576,1024]{1,0:T(8,128)(2,1)}, u32[]{:S(2)}, u32[]{:S(2)}) collective-permute-start(bf16[576,1024]{1,0:T(8,128)(2,1)} %bitcast.217), channel_id=1, source_target_pairs={{0,3},{1,2},{2,1},{3,0},{4,7},{5,6},{6,5},{7,4},{8,11},{9,10},{10,... | collective-permute-start | bytes 3538952 | tf_op jit(solution)/shard_map/ppermute | solution.py:773
  18.7 54.2 %collective-permute-start.5 = (bf16[256,896]{1,0:T(8,128)(2,1)S(1)}, bf16[256,896]{1,0:T(8,128)(2,1)}, u32[]{:S(2)}, u32[]{:S(2)}) collective-permute-start(bf16[256,896]{1,0:T(8,128)(2,1)S(1)} %get-tuple-element.133), channel_id=1, source_target_pairs={{0,3},{1,2},{2,1},{3,0},{4,7},{5,6},{6,5},{7,4},{8,11},{9,10},{10,... | collective-permute-start | bytes 1376264 | tf_op jit(solution)/shard_map/ppermute | solution.py:773
  21.6 61.3 %collective-permute-start.4 = (bf16[256,896]{1,0:T(8,128)(2,1)}, bf16[256,896]{1,0:T(8,128)(2,1)}, u32[]{:S(2)}, u32[]{:S(2)}) collective-permute-start(bf16[256,896]{1,0:T(8,128)(2,1)} %get-tuple-element.134), channel_id=1, source_target_pairs={{0,2},{1,3},{2,0},{3,1},{4,6},{5,7},{6,4},{7,5},{8,10},{9,11},{10,... | collective-permute-start | bytes 1376264 | tf_op jit(solution)/shard_map/ppermute | solution.py:773
  85.6 131.7 %all-gather.5.cloned.1.call-start = ((), (), s32[]{:S(2)}) async-start(), calls=%async_computation.21 | async-start | bytes 9437184 | tf_op jit(solution)/shard_map/all_gather | solution.py:971
  89.9 32.1 %all-to-all-start.1 = ((s32[16,1,288]{2,1,0:T(1,128)}), s32[16,1,288]{2,1,0:T(1,128)S(1)}, u32[]{:S(2)}, u32[]{:S(2)}) async-start(s32[16,1,288]{2,1,0:T(1,128)} %copy.112), calls=%async_computation.1 | async-start | bytes 49152 | tf_op jit(solution)/shard_map/all_to_all | solution.py:805
  105.4 77.8 %collective-permute-start.6 = (bf16[128,4096]{1,0:T(8,128)(2,1)}, bf16[128,4096]{1,0:T(8,128)(2,1)S(1)}, u32[]{:S(2)}, u32[]{:S(2)}) collective-permute-start(bf16[128,4096]{1,0:T(8,128)(2,1)} %run_after.19.refs_0_), channel_id=1, source_target_pairs={{0,1},{1,0},{2,3},{3,2},{4,5},{5,4},{6,7},{7,6},{8,9},{9,8},{10,11... | collective-permute-start | bytes 3145736 | tf_op jit(solution)/shard_map/ppermute | solution.py:773
  107.4 75.8 %collective-permute-start.7 = (bf16[128,4096]{1,0:T(8,128)(2,1)}, bf16[128,4096]{1,0:T(8,128)(2,1)}, u32[]{:S(2)}, u32[]{:S(2)}) collective-permute-start(bf16[128,4096]{1,0:T(8,128)(2,1)} %run_after.19.refs_0_), channel_id=1, source_target_pairs={{0,2},{1,3},{2,0},{3,1},{4,6},{5,7},{6,4},{7,5},{8,10},{9,11},{10,... | collective-permute-start | bytes 3145736 | tf_op jit(solution)/shard_map/ppermute | solution.py:773
  108.9 74.3 %collective-permute-start.8 = (bf16[128,4096]{1,0:T(8,128)(2,1)}, bf16[128,4096]{1,0:T(8,128)(2,1)}, u32[]{:S(2)}, u32[]{:S(2)}) collective-permute-start(bf16[128,4096]{1,0:T(8,128)(2,1)} %run_after.19.refs_0_), channel_id=1, source_target_pairs={{0,3},{1,2},{2,1},{3,0},{4,7},{5,6},{6,5},{7,4},{8,11},{9,10},{10,... | collective-permute-start | bytes 3145736 | tf_op jit(solution)/shard_map/ppermute | solution.py:773
  122.0 25.2 %all-to-all-start.2 = ((s32[4,4,576]{2,1,0:T(4,128)}), s32[4,4,576]{2,1,0:T(4,128)S(1)}, u32[]{:S(2)}, u32[]{:S(2)}) async-start(s32[4,4,576]{2,1,0:T(4,128)} %reshape.356), calls=%async_computation.2 | async-start | bytes 81920 | tf_op jit(solution)/shard_map/all_to_all | solution.py:805
  147.2 34.1 %all-to-all-start = ((bf16[4,576,256]{2,1,0:T(8,128)(2,1)}), bf16[4,576,256]{2,1,0:T(8,128)(2,1)S(1)}, u32[]{:S(2)}, u32[]{:S(2)}) async-start(bf16[4,576,256]{2,1,0:T(8,128)(2,1)} %bitcast.237), calls=%async_computation | async-start | bytes 2359296 | tf_op jit(solution)/shard_map/all_to_all | solution.py:989
  153.6 42.2 %collective-permute-start.9 = (bf16[128,4096]{1,0:T(8,128)(2,1)S(1)}, bf16[128,4096]{1,0:T(8,128)(2,1)}, u32[]{:S(2)}, u32[]{:S(2)}) collective-permute-start(bf16[128,4096]{1,0:T(8,128)(2,1)S(1)} %copy-done.18), channel_id=1, source_target_pairs={{0,16},{16,0},{1,17},{17,1},{2,18},{18,2},{3,19},{19,3},{4,20},{20... | collective-permute-start | bytes 3145736 | tf_op jit(solution)/shard_map/ppermute | solution.py:788
  231.7 29.4 %collective-permute-start.13 = (bf16[576,1024]{1,0:T(8,128)(2,1)S(1)}, bf16[576,1024]{1,0:T(8,128)(2,1)}, u32[]{:S(2)}, u32[]{:S(2)}) collective-permute-start(bf16[576,1024]{1,0:T(8,128)(2,1)S(1)} %add_convert_fusion.5.refs_1_), channel_id=1, source_target_pairs={{0,4},{4,8},{8,12},{1,5},{5,9},{9,13},{2,6},{6,10},{10,14},{3,7},{... | collective-permute-start | bytes 3538952 | tf_op jit(solution)/shard_map/ppermute | solution.py:1017
  236.1 30.3 %collective-permute-start.14 = (bf16[576,1024]{1,0:T(8,128)(2,1)S(1)}, bf16[576,1024]{1,0:T(8,128)(2,1)}, u32[]{:S(2)}, u32[]{:S(2)}) collective-permute-start(bf16[576,1024]{1,0:T(8,128)(2,1)S(1)} %add_convert_fusion.5.refs_1_), channel_id=1, source_target_pairs={{4,0},{8,4},{12,8},{5,1},{9,5},{13,9},{6,2},{10,6},{14,10},{7,3},{... | collective-permute-start | bytes 3538952 | tf_op jit(solution)/shard_map/ppermute | solution.py:1020
  242.8 32.1 %all-to-all-start.3 = ((bf16[4,288,1024]{2,1,0:T(8,128)(2,1)}), bf16[4,288,1024]{2,1,0:T(8,128)(2,1)S(1)}, u32[]{:S(2)}, u32[]{:S(2)}) async-start(bf16[4,288,1024]{2,1,0:T(8,128)(2,1)} %pack_rows.4.refs_2_), calls=%async_computation.3 | async-start | bytes 4718592 | tf_op jit(solution)/shard_map/all_to_all | solution.py:805
  267.1 31.0 %collective-permute-start.16 = (bf16[576,1024]{1,0:T(8,128)(2,1)}, bf16[576,1024]{1,0:T(8,128)(2,1)}, u32[]{:S(2)}, u32[]{:S(2)}) collective-permute-start(bf16[576,1024]{1,0:T(8,128)(2,1)} %get-tuple-element.58.refs_1_.refs_2_), channel_id=1, source_target_pairs={{4,0},{8,4},{5,1},{9,5},{6,2},{10,6},{7,3},{11,7},{20,16},{24,20},... | collective-permute-start | bytes 3538952 | tf_op jit(solution)/shard_map/ppermute | solution.py:1020
  274.9 32.4 %all-to-all-start.4 = ((bf16[4,288,1024]{2,1,0:T(8,128)(2,1)}), bf16[4,288,1024]{2,1,0:T(8,128)(2,1)}, u32[]{:S(2)}, u32[]{:S(2)}) async-start(bf16[4,288,1024]{2,1,0:T(8,128)(2,1)} %pack_rows.5), calls=%async_computation.4 | async-start | bytes 4718592 | tf_op jit(solution)/shard_map/all_to_all | solution.py:805
  298.1 28.7 %collective-permute-start.17 = (bf16[576,1024]{1,0:T(8,128)(2,1)}, bf16[576,1024]{1,0:T(8,128)(2,1)S(1)}, u32[]{:S(2)}, u32[]{:S(2)}) collective-permute-start(bf16[576,1024]{1,0:T(8,128)(2,1)} %get-tuple-element.62.refs_1_.refs_2_), channel_id=1, source_target_pairs={{4,0},{5,1},{6,2},{7,3},{20,16},{21,17},{22,18},{23,19}} | collective-permute-start | bytes 3538952 | tf_op jit(solution)/shard_map/ppermute | solution.py:1020
  299.4 27.4 %collective-permute-start.18 = (bf16[576,1024]{1,0:T(8,128)(2,1)}, bf16[576,1024]{1,0:T(8,128)(2,1)}, u32[]{:S(2)}, u32[]{:S(2)}) collective-permute-start(bf16[576,1024]{1,0:T(8,128)(2,1)} %get-tuple-element.63.refs_4_.refs_3_), channel_id=1, source_target_pairs={{8,12},{9,13},{10,14},{11,15},{24,28},{25,29},{26,30},{27,31}} | collective-permute-start | bytes 3538952 | tf_op jit(solution)/shard_map/ppermute | solution.py:1017
  307.3 30.8 %all-to-all-start.5 = ((bf16[4,288,1024]{2,1,0:T(8,128)(2,1)}), bf16[4,288,1024]{2,1,0:T(8,128)(2,1)S(1)}, u32[]{:S(2)}, u32[]{:S(2)}) async-start(bf16[4,288,1024]{2,1,0:T(8,128)(2,1)} %pack_rows.6), calls=%async_computation.5 | async-start | bytes 4718592 | tf_op jit(solution)/shard_map/all_to_all | solution.py:805
  338.0 39.8 %all-to-all-start.6 = ((bf16[4,288,1024]{2,1,0:T(8,128)(2,1)}), bf16[4,288,1024]{2,1,0:T(8,128)(2,1)}, u32[]{:S(2)}, u32[]{:S(2)}) async-start(bf16[4,288,1024]{2,1,0:T(8,128)(2,1)} %pack_rows.7), calls=%async_computation.6 | async-start | bytes 4718592 | tf_op jit(solution)/shard_map/all_to_all | solution.py:805
  442.6 27.9 %all-to-all-start.10 = ((bf16[4,288,1024]{2,1,0:T(8,128)(2,1)}), bf16[4,288,1024]{2,1,0:T(8,128)(2,1)S(1)}, u32[]{:S(2)}, u32[]{:S(2)}) async-start(bf16[4,288,1024]{2,1,0:T(8,128)(2,1)} %bitcast.228), calls=%async_computation.10 | async-start | bytes 4718592 | tf_op jit(solution)/shard_map/all_to_all | solution.py:805
  471.9 31.7 %all-to-all-start.9 = ((bf16[4,288,1024]{2,1,0:T(8,128)(2,1)}), bf16[4,288,1024]{2,1,0:T(8,128)(2,1)}, u32[]{:S(2)}, u32[]{:S(2)}) async-start(bf16[4,288,1024]{2,1,0:T(8,128)(2,1)} %bitcast.227), calls=%async_computation.9 | async-start | bytes 4718592 | tf_op jit(solution)/shard_map/all_to_all | solution.py:805
  481.6 27.4 %collective-permute-start.19 = (bf16[576,1024]{1,0:T(8,128)(2,1)}, bf16[576,1024]{1,0:T(8,128)(2,1)}, u32[]{:S(2)}, u32[]{:S(2)}) collective-permute-start(bf16[576,1024]{1,0:T(8,128)(2,1)} %unpack_rows.4.refs_7_), channel_id=1, source_target_pairs={{0,4},{1,5},{2,6},{3,7},{16,20},{17,21},{18,22},{19,23}} | collective-permute-start | bytes 3538952 | tf_op jit(solution)/shard_map/ppermute | solution.py:767
  485.4 23.7 %collective-permute-start.20 = (bf16[576,1024]{1,0:T(8,128)(2,1)}, bf16[576,1024]{1,0:T(8,128)(2,1)}, u32[]{:S(2)}, u32[]{:S(2)}) collective-permute-start(bf16[576,1024]{1,0:T(8,128)(2,1)} %unpack_rows.4.refs_7_), channel_id=1, source_target_pairs={{12,8},{13,9},{14,10},{15,11},{28,24},{29,25},{30,26},{31,27}} | collective-permute-start | bytes 3538952 | tf_op jit(solution)/shard_map/ppermute | solution.py:768
  503.6 32.7 %all-to-all-start.12 = ((bf16[4,288,1024]{2,1,0:T(8,128)(2,1)}), bf16[4,288,1024]{2,1,0:T(8,128)(2,1)S(1)}, u32[]{:S(2)}, u32[]{:S(2)}) async-start(bf16[4,288,1024]{2,1,0:T(8,128)(2,1)} %bitcast.231), calls=%async_computation.12 | async-start | bytes 4718592 | tf_op jit(solution)/shard_map/all_to_all | solution.py:805
  518.8 28.1 %collective-permute-start.21 = (bf16[576,1024]{1,0:T(8,128)(2,1)}, bf16[576,1024]{1,0:T(8,128)(2,1)}, u32[]{:S(2)}, u32[]{:S(2)}) collective-permute-start(bf16[576,1024]{1,0:T(8,128)(2,1)} %get-tuple-element.109), channel_id=1, source_target_pairs={{0,4},{4,8},{1,5},{5,9},{2,6},{6,10},{3,7},{7,11},{16,20},{20,24},... | collective-permute-start | bytes 3538952 | tf_op jit(solution)/shard_map/ppermute | solution.py:767
  524.3 22.7 %collective-permute-start.22 = (bf16[576,1024]{1,0:T(8,128)(2,1)}, bf16[576,1024]{1,0:T(8,128)(2,1)}, u32[]{:S(2)}, u32[]{:S(2)}) collective-permute-start(bf16[576,1024]{1,0:T(8,128)(2,1)} %get-tuple-element.110), channel_id=1, source_target_pairs={{8,4},{12,8},{9,5},{13,9},{10,6},{14,10},{11,7},{15,11},{24,20},{2... | collective-permute-start | bytes 3538952 | tf_op jit(solution)/shard_map/ppermute | solution.py:768
  537.7 31.0 %all-to-all-start.11 = ((bf16[4,288,1024]{2,1,0:T(8,128)(2,1)}), bf16[4,288,1024]{2,1,0:T(8,128)(2,1)}, u32[]{:S(2)}, u32[]{:S(2)}) async-start(bf16[4,288,1024]{2,1,0:T(8,128)(2,1)} %bitcast.230), calls=%async_computation.11 | async-start | bytes 4718592 | tf_op jit(solution)/shard_map/all_to_all | solution.py:805
  542.2 146.8 %reduce-scatter.10.cloned.1.call-start = ((), (), s32[]{:S(2)}) async-start(), calls=%async_computation.23 | async-start | bytes 5242880
  556.7 31.8 %collective-permute-start.24 = (bf16[576,1024]{1,0:T(8,128)(2,1)}, bf16[576,1024]{1,0:T(8,128)(2,1)}, u32[]{:S(2)}, u32[]{:S(2)}) collective-permute-start(bf16[576,1024]{1,0:T(8,128)(2,1)} %get-tuple-element.108), channel_id=1, source_target_pairs={{4,0},{8,4},{12,8},{5,1},{9,5},{13,9},{6,2},{10,6},{14,10},{7,3},{... | collective-permute-start | bytes 3538952 | tf_op jit(solution)/shard_map/ppermute | solution.py:768
  558.0 31.7 %collective-permute-start.23 = (bf16[576,1024]{1,0:T(8,128)(2,1)}, bf16[576,1024]{1,0:T(8,128)(2,1)}, u32[]{:S(2)}, u32[]{:S(2)}) collective-permute-start(bf16[576,1024]{1,0:T(8,128)(2,1)} %get-tuple-element.107), channel_id=1, source_target_pairs={{0,4},{4,8},{8,12},{1,5},{5,9},{9,13},{2,6},{6,10},{10,14},{3,7},{... | collective-permute-start | bytes 3538952 | tf_op jit(solution)/shard_map/ppermute | solution.py:767
  695.0 77.9 %reduce-scatter.12.cloned.1.call-start = ((), (), s32[]{:S(2)}) async-start(), calls=%async_computation.24 | async-start | bytes 6553600
  711.3 32.6 %all-to-all-start.14 = ((bf16[4,128,1024]{2,1,0:T(8,128)(2,1)}), bf16[4,128,1024]{2,1,0:T(8,128)(2,1)S(1)}, u32[]{:S(2)}, u32[]{:S(2)}) async-start(bf16[4,128,1024]{2,1,0:T(8,128)(2,1)} %bitcast.221), calls=%async_computation.14 | async-start | bytes 2097152 | tf_op jit(solution)/shard_map/all_to_all | solution.py:805
  772.9 36.2 %all-to-all-start.15 = ((bf16[4,32,5120]{2,1,0:T(8,128)(2,1)}), bf16[4,32,5120]{2,1,0:T(8,128)(2,1)}, u32[]{:S(2)}, u32[]{:S(2)}) async-start(bf16[4,32,5120]{2,1,0:T(8,128)(2,1)} %bitcast.236), calls=%async_computation.16 | async-start | bytes 2621440 | tf_op jit(solution)/shard_map/all_to_all | solution.py:805
  777.6 121.2 %reduce-scatter.8.cloned.1.call-start = ((), (), s32[]{:S(2)}) async-start(), calls=%async_computation.22 | async-start | bytes 5898240 | tf_op jit(solution)/shard_map/reduce_scatter | solution.py:1143
  811.3 25.0 %collective-permute-start.32 = (bf16[32,5120]{1,0:T(8,128)(2,1)}, bf16[32,5120]{1,0:T(8,128)(2,1)}, u32[]{:S(2)}, u32[]{:S(2)}) collective-permute-start(bf16[32,5120]{1,0:T(8,128)(2,1)} %fusion.61.refs_1_), channel_id=1, source_target_pairs={{0,8},{4,12},{8,0},{12,4},{1,9},{5,13},{9,1},{13,5},{2,10},{6,14},... | collective-permute-start | bytes 983048 | tf_op jit(solution)/shard_map/ppermute | solution.py:837
  813.4 22.9 %collective-permute-start.33 = (bf16[32,5120]{1,0:T(8,128)(2,1)}, bf16[32,5120]{1,0:T(8,128)(2,1)}, u32[]{:S(2)}, u32[]{:S(2)}) collective-permute-start(bf16[32,5120]{1,0:T(8,128)(2,1)} %fusion.61.refs_1_), channel_id=1, source_target_pairs={{0,12},{4,0},{8,4},{12,8},{1,13},{5,1},{9,5},{13,9},{2,14},{6,2},{... | collective-permute-start | bytes 983048 | tf_op jit(solution)/shard_map/ppermute | solution.py:837
  821.1 27.4 %collective-permute-start.30 = (bf16[128,896]{1,0:T(8,128)(2,1)}, bf16[128,896]{1,0:T(8,128)(2,1)}, u32[]{:S(2)}, u32[]{:S(2)}) collective-permute-start(bf16[128,896]{1,0:T(8,128)(2,1)} %get-tuple-element.128), channel_id=1, source_target_pairs={{0,3},{1,2},{2,1},{3,0},{4,7},{5,6},{6,5},{7,4},{8,11},{9,10},{10,... | collective-permute-start | bytes 688136 | tf_op jit(solution)/shard_map/ppermute | solution.py:773
  822.6 28.5 %collective-permute-start.29 = (bf16[128,896]{1,0:T(8,128)(2,1)}, bf16[128,896]{1,0:T(8,128)(2,1)}, u32[]{:S(2)}, u32[]{:S(2)}) collective-permute-start(bf16[128,896]{1,0:T(8,128)(2,1)} %get-tuple-element.129), channel_id=1, source_target_pairs={{0,2},{1,3},{2,0},{3,1},{4,6},{5,7},{6,4},{7,5},{8,10},{9,11},{10,... | collective-permute-start | bytes 688136 | tf_op jit(solution)/shard_map/ppermute | solution.py:773
  824.1 27.0 %collective-permute-start.28 = (bf16[128,896]{1,0:T(8,128)(2,1)}, bf16[128,896]{1,0:T(8,128)(2,1)}, u32[]{:S(2)}, u32[]{:S(2)}) collective-permute-start(bf16[128,896]{1,0:T(8,128)(2,1)} %get-tuple-element.130), channel_id=1, source_target_pairs={{0,1},{1,0},{2,3},{3,2},{4,5},{5,4},{6,7},{7,6},{8,9},{9,8},{10,11... | collective-permute-start | bytes 688136 | tf_op jit(solution)/shard_map/ppermute | solution.py:773
  841.8 38.3 %collective-permute-start.38 = (bf16[4,32,5120]{2,1,0:T(8,128)(2,1)}, bf16[4,32,5120]{2,1,0:T(8,128)(2,1)}, u32[]{:S(2)}, u32[]{:S(2)}) collective-permute-start(bf16[4,32,5120]{2,1,0:T(8,128)(2,1)} %gather_fusion.5), channel_id=1, source_target_pairs={{0,16},{16,0},{1,17},{17,1},{2,18},{18,2},{3,19},{19,3},{4,20},{20... | collective-permute-start | bytes 3932168 | tf_op jit(solution)/shard_map/ppermute | solution.py:788
  843.1 32.8 %collective-permute-start.41 = (bf16[128,1024]{1,0:T(8,128)(2,1)}, bf16[128,1024]{1,0:T(8,128)(2,1)}, u32[]{:S(2)}, u32[]{:S(2)}) collective-permute-start(bf16[128,1024]{1,0:T(8,128)(2,1)} %run_after.33), channel_id=1, source_target_pairs={{0,12},{4,0},{8,4},{12,8},{1,13},{5,1},{9,5},{13,9},{2,14},{6,2},{... | collective-permute-start | bytes 786440 | tf_op jit(solution)/shard_map/ppermute | solution.py:837
  848.6 27.3 %collective-permute-start.40 = (bf16[128,1024]{1,0:T(8,128)(2,1)}, bf16[128,1024]{1,0:T(8,128)(2,1)}, u32[]{:S(2)}, u32[]{:S(2)}) collective-permute-start(bf16[128,1024]{1,0:T(8,128)(2,1)} %run_after.33), channel_id=1, source_target_pairs={{0,8},{4,12},{8,0},{12,4},{1,9},{5,13},{9,1},{13,5},{2,10},{6,14},... | collective-permute-start | bytes 786440 | tf_op jit(solution)/shard_map/ppermute | solution.py:837
  851.1 24.7 %collective-permute-start.39 = (bf16[128,1024]{1,0:T(8,128)(2,1)}, bf16[128,1024]{1,0:T(8,128)(2,1)}, u32[]{:S(2)}, u32[]{:S(2)}) collective-permute-start(bf16[128,1024]{1,0:T(8,128)(2,1)} %run_after.33), channel_id=1, source_target_pairs={{0,4},{4,8},{8,12},{12,0},{1,5},{5,9},{9,13},{13,1},{2,6},{6,10},{... | collective-permute-start | bytes 786440 | tf_op jit(solution)/shard_map/ppermute | solution.py:837
  870.4 26.2 %all-to-all-start.16 = ((bf16[4,32,3200]{2,1,0:T(8,128)(2,1)}), bf16[4,32,3200]{2,1,0:T(8,128)(2,1)S(1)}, u32[]{:S(2)}, u32[]{:S(2)}) async-start(bf16[4,32,3200]{2,1,0:T(8,128)(2,1)} %bitcast.234), calls=%async_computation.17 | async-start | bytes 1638400 | tf_op jit(solution)/shard_map/all_to_all | solution.py:805
  (96 other events, 909.5 us)
Sparse Core Ops, SparseCore 0:
  85.8 33.1 all-gather.2
  121.4 86.0 all-gather.4
  634.9 54.0 reduce-scatter.9
  711.4 61.4 reduce-scatter.11
  784.1 64.9 reduce-scatter.7

commit v4 on v3

--- a/solution.py
+++ b/solution.py
@@ -431,14 +431,14 @@
         square_ref[plane : plane + 1, :] += jnp.sum(turned * turned, axis=0, keepdims=True)
 
 
-def key_planes(keys, spacing):
+def key_planes(keys, spacing, after=()):
     count, width = keys.shape
     columns = row_chunk(width, (128,))
     near_count = count // spacing
     return pl.pallas_call(
-        functools.partial(planes_kernel, spacing),
+        later(functools.partial(planes_kernel, spacing), 1, len(after)),
         grid=(width // columns,),
-        in_specs=[spec((count, columns), lambda i: (0, i))],
+        in_specs=[spec((count, columns), lambda i: (0, i)), *later_specs(after)],
         out_specs=[
             spec((count, columns), lambda i: (0, i)),
             spec((columns, count), lambda i: (i, 0)),
@@ -453,7 +453,7 @@
         compiler_params=kernel_params(),
         cost_estimate=small_cost,
         name="key_planes",
-    )(keys)
+    )(keys, *after)
 
 
 def near_kernel(spacing, dist_scale, parts, *refs):
@@ -941,7 +941,6 @@
         jnp.where(slot_picker(slot_map, capacity), targets.reshape(1, 1, -1), 0), axis=2
     )
     got_targets = exchange(send_targets.astype(jnp.int32), everyone).astype(jnp.float32)
-    planes, planes_turned, key_square = key_planes(store_keys, spacing)
     value_planes = store_values.astype(jnp.float32).reshape(near_count, spacing).T
     by_layer = capacity % 16 == 0
     if by_layer:
@@ -1020,10 +1019,15 @@
                     lax.ppermute(down, "batch", [(i, i - 1) for i in range(1, layer_count - step)])
                 )
             options, pick = layer_step(step, ups, downs)
-            between = (planes, planes_turned, key_square) if step == 1 else ()
+            between = ()
+            if step == 1:
+                between = planes, planes_turned, key_square = key_planes(
+                    store_keys, spacing, packed
+                )
             packed.append(pack_rows(options, pick, maps[step], capacity, between))
             queries.append(exchange(packed[step], "ctx").reshape(-1, width))
     else:
+        planes, planes_turned, key_square = key_planes(store_keys, spacing)
         packed = jnp.einsum(
             "ost,tw->osw", chosen_slots, final_rows, preferred_element_type=jnp.float32
         )

time: 940 us -> 934 us (level)
  waiting for transfers between devices: 266 us -> 256 us
    ppermute x3, waiting for transfers between devices: 7.67 us -> 20.6 us  [layer_hop(): lax.ppermute(up, 'batch', [(i, i + 1) for i in range(hop)])]
  transfers between devices with their start and end apart: 63 -> 63, of which waited for: 27 -> 31; matrix products, arithmetic and copies ran while one was open for 21% -> 21% of each run, Pallas kernels for 20% -> 21%
where the time goes in v4:
time: 934 us; the launch traced here: 926 us
  waiting for transfers between devices  256 us (27%)
  Pallas kernels  223 us (24%)
  starting transfers between devices  135 us (14%)
  matrix products  89.6 us (10%)
  local copies, waits for them, and re-layouts  89.4 us (10%)
  other arithmetic  87.6 us (9%)
  blocking collectives  29.9 us (3%)
  between operations  15.3 us (2%)
    ppermute x12, waiting for transfers between devices, across(): lax.ppermute(rows, 'ctx', [(i, i ^ step) for i in range(lax.axis_size('ct...  59.3 us
    all_to_all x13, starting transfers between devices, exchange(): return lax.all_to_all(blocks, axis, split_axis=0, concat_axis=0, tiled=True)  57.1 us
    pallas_call x4, Pallas kernels, near_scores(): pl.pallas_call(functools.partial(near_kernel, spacing, width ** (-0.5), p...  44.4 us
    pallas_call x4, Pallas kernels, near_back(): pl.pallas_call(later(functools.partial(near_back_kernel, spacing, 2.0 * w...  41.5 us
    all_to_all x13, waiting for transfers between devices, exchange(): return lax.all_to_all(blocks, axis, split_axis=0, concat_axis=0, tiled=True)  40.1 us
    ppermute x3, waiting for transfers between devices, local(): lax.ppermute(down, 'batch', [(i, i - 1) for i in range(1, layer_count - s...  38.6 us
    dot_general x4, matrix products, right_dot(): lax.dot_general(left_side, right_side, (((1,), (1,)), ((), ())), preferre...  35.3 us
    dot_general x5, matrix products, left_dot(): lax.dot_general(left_side, right_side, (((0,), (0,)), ((), ())), preferre...  30.7 us
  transfers between devices with their start and end apart: 63, of which 31 were waited for; matrix products, arithmetic and copies ran while one was open for 21% of the time, Pallas kernels for 21%

profile of v4, /device:TPU:0, one launch (start us, length us, event | category | flops | bytes accessed | tf_op | source)
XLA Modules:
  0.0 925.8 jit_solution(4743336793860378731)
XLA Ops:
  22.1 50.8 %collective-permute-done.5.refs_7_.refs_6_ = bf16[256,896]{1,0:T(8,128)(2,1)} collective-permute-done((bf16[256,896]{1,0:T(8,128)(2,1)S(1)}, bf16[256,896]{1,0:T(8,128)(2,1)}, u32[]{:S(2)}, u32[]{:S(2)}) %collective-permute-start.5) | collective-permute-done | bytes 458784 | tf_op jit(solution)/shard_map/ppermute | solution.py:773
  76.1 6.8 collective-permute-done.4.refs_6_.refs_5_
  89.9 6.2 all-to-all-start.1
  108.9 13.1 %project_rows.1 = (bf16[1024,768]{1,0:T(8,128)(2,1)}, bf16[2304,1024]{1,0:T(8,128)(2,1)}, bf16[2304,1024]{1,0:T(8,128)(2,1)}, bf16[2304,256]{1,0:T(8,128)(2,1)},...) custom-call(s32[4]{0:T(128)} %iota_xor_fusion.order_ref, bf16[576,1024]{1,0:T(8,128)(2,1)} %bitcast.218, ...), custom_call_target="tpu_custom_call" | custom-call | flops 12999999488 | bytes 1000 | tf_op jit(solution)/shard_map/project_rows/pallas_call | solution.py:392
  127.7 20.8 %attend.1 = (bf16[2304,256]{1,0:T(8,128)(2,1)}, f32[8,2304]{1,0:T(8,128)}) custom-call(s32[18]{0:T(128)} %pad_add_fusion.refs_0_, bf16[2304,256]{1,0:T(8,128)(2,1)} %get-tuple-element.48.refs_1_, bf16[2304,256]{1,0:T(8,128)(2,1)} %get-tuple-element.49.refs_2_, bf16[2304,256]{1,0:T(8,128)(2,1)} %get-tuple-element.50.refs_3_, ...), custom_call_target="tpu_custom_call" | custom-call | flops 20000000000 | bytes 1000 | tf_op jit(solution)/shard_map/attend/pallas_call | solution.py:193
  154.9 26.4 %all-to-all-done = bf16[4,576,256]{2,1,0:T(8,128)(2,1)S(1)} async-done(((bf16[4,576,256]{2,1,0:T(8,128)(2,1)}), bf16[4,576,256]{2,1,0:T(8,128)(2,1)S(1)}, u32[]{:S(2)}, u32[]{:S(2)}) %all-to-all-start) | async-done | bytes 1179680 | tf_op jit(solution)/shard_map/all_to_all | solution.py:988
  190.9 9.0 place_rows.1
  204.6 7.8 fusion.39
  212.4 12.6 %fusion.44 = (f32[576]{0:T(1024)S(1)}, f32[576,1024]{1,0:T(8,128)S(1)}) fusion(f32[576,1024]{1,0:T(8,128)} %copy-done.16, bf16[4096,1024]{1,0:T(8,128)(2,1)} %all-gather.5.cloned.1.call-done, f32[576,4096]{1,0:T(8,128)} %fusion.39), kind=kOutput, calls=%fused_computation.214 | convolution fusion | flops 4854251008 | bytes 22546688 | tf_op jit(solution)/shard_map/dot_general | solution.py:28
  241.5 8.5 key_planes.1
  263.0 6.1 pack_rows.5
  274.0 18.1 %collective-permute-done.16.refs_1_ = bf16[576,1024]{1,0:T(8,128)(2,1)} collective-permute-done((bf16[576,1024]{1,0:T(8,128)(2,1)}, bf16[576,1024]{1,0:T(8,128)(2,1)}, u32[]{:S(2)}, u32[]{:S(2)}) %collective-permute-start.16) | collective-permute-done | bytes 1179680 | tf_op jit(solution)/shard_map/ppermute | solution.py:1019
  295.0 5.9 pack_rows.6
  304.9 15.3 %collective-permute-done.17.refs_1_ = bf16[576,1024]{1,0:T(8,128)(2,1)S(1)} collective-permute-done((bf16[576,1024]{1,0:T(8,128)(2,1)}, bf16[576,1024]{1,0:T(8,128)(2,1)S(1)}, u32[]{:S(2)}, u32[]{:S(2)}) %collective-permute-start.17) | collective-permute-done | bytes 1179680 | tf_op jit(solution)/shard_map/ppermute | solution.py:1019
  321.2 5.9 pack_rows.7
  338.6 11.1 %near_scores.4 = (f32[1152,256]{1,0:T(8,128)}, f32[4,8,288]{2,1,0:T(8,128)}) custom-call(s32[4]{0:T(128)} %get-tuple-element.149.refs_0_, bf16[1152,1024]{1,0:T(8,128)(2,1)} %bitcast.214, bf16[1024,2048]{1,0:T(8,128)(2,1)} %get-tuple-element.55.refs_2_.refs_5_, f32[8,256]{1,0:T(8,128)} %get-tuple-element.56.refs_3_.refs_6_, f32[8,256]{1,0:T(8,128)} %bitcast.247, ...), custom_call_target="tpu_custom_call" | custom-call | flops 1000 | bytes 1000 | tf_op jit(solution)/shard_map/near_scores/pallas_call | solution.py:504
  349.7 11.1 %near_scores.5 = (f32[1152,256]{1,0:T(8,128)}, f32[4,8,288]{2,1,0:T(8,128)}) custom-call(s32[4]{0:T(128)} %get-tuple-element.152.refs_0_, bf16[1152,1024]{1,0:T(8,128)(2,1)} %bitcast.29.refs_1_, bf16[1024,2048]{1,0:T(8,128)(2,1)} %get-tuple-element.55.refs_2_.refs_5_, f32[8,256]{1,0:T(8,128)} %get-tuple-element.56.refs_3_.refs_6_, f32[8,256]{1,0:T(8,128)} %bitcast.248, ...), custom_call_target="tpu_custom_call" | custom-call | flops 1000 | bytes 1000 | tf_op jit(solution)/shard_map/near_scores/pallas_call | solution.py:504
  360.7 11.1 %near_scores.6 = (f32[1152,256]{1,0:T(8,128)}, f32[4,8,288]{2,1,0:T(8,128)}) custom-call(s32[4]{0:T(128)} %get-tuple-element.151.refs_0_, bf16[1152,1024]{1,0:T(8,128)(2,1)} %bitcast.229, bf16[1024,2048]{1,0:T(8,128)(2,1)} %get-tuple-element.55.refs_2_.refs_5_, f32[8,256]{1,0:T(8,128)} %get-tuple-element.56.refs_3_.refs_6_, f32[8,256]{1,0:T(8,128)} %bitcast.249, ...), custom_call_target="tpu_custom_call" | custom-call | flops 1000 | bytes 1000 | tf_op jit(solution)/shard_map/near_scores/pallas_call | solution.py:504
  371.8 11.2 %near_scores.7 = (f32[1152,256]{1,0:T(8,128)}, f32[4,8,288]{2,1,0:T(8,128)}) custom-call(s32[4]{0:T(128)} %get-tuple-element.150.refs_0_, bf16[1152,1024]{1,0:T(8,128)(2,1)} %bitcast.38.refs_1_, bf16[1024,2048]{1,0:T(8,128)(2,1)} %get-tuple-element.55.refs_2_.refs_5_, f32[8,256]{1,0:T(8,128)} %get-tuple-element.56.refs_3_.refs_6_, f32[8,256]{1,0:T(8,128)} %bitcast.250, ...), custom_call_target="tpu_custom_call" | custom-call | flops 1000 | bytes 1000 | tf_op jit(solution)/shard_map/near_scores/pallas_call | solution.py:504
  384.5 17.5 %all_to_all.117.stats_ref = f32[16,8,288]{2,1,0:T(8,128)} all-to-all(f32[16,8,288]{2,1,0:T(8,128)S(1)} %bitcast.246), channel_id=1, replica_groups=mesh['rep'=2,'batch'=4,'ctx'=4] {'batch','ctx'}, dimensions={0} | all-to-all | bytes 294912 | tf_op jit(solution)/shard_map/all_to_all | solution.py:805
  401.9 11.8 %mix_losses.1 = (f32[1,576]{1,0:T(1,128)}, f32[16,8,288]{2,1,0:T(8,128)}) custom-call(f32[16,8,288]{2,1,0:T(8,128)} %all_to_all.117.stats_ref, s32[16,576]{1,0:T(8,128)} %copy-done.41, f32[1,576]{1,0:T(1,128)} %prob_ref.1), custom_call_target="tpu_custom_call" | custom-call | tf_op jit(solution)/shard_map/mix_losses/pallas_call | solution.py:697
  413.7 12.4 %all_to_all.118.refs_4_.refs_5_ = f32[16,8,288]{2,1,0:T(8,128)} all-to-all(f32[16,8,288]{2,1,0:T(8,128)} %get-tuple-element.69), channel_id=1, replica_groups=mesh['rep'=2,'batch'=4,'ctx'=4] {'batch','ctx'}, dimensions={0} | all-to-all | bytes 294912 | tf_op jit(solution)/shard_map/all_to_all | solution.py:805
  426.2 10.4 %near_back.5 = bf16[1152,1024]{1,0:T(8,128)(2,1)} custom-call(s32[4]{0:T(128)} %get-tuple-element.150.refs_0_, f32[1152,256]{1,0:T(8,128)} %get-tuple-element.71.refs_1_, s32[16,288,256]{2,1,0:T(8,128)} %bitcast.203, s32[16,288,256]{2,1,0:T(8,128)} %bitcast.204, f32[16,8,288]{2,1,0:T(8,128)} %all_to_all.118.refs_4_.refs_5_, ...), custom_call_target="tpu_custom_call" | custom-call | flops 1000 | bytes 1000 | tf_op jit(solution)/shard_map/near_back/pallas_call | solution.py:557
  440.2 10.4 %near_back.4 = bf16[1152,1024]{1,0:T(8,128)(2,1)} custom-call(s32[4]{0:T(128)} %get-tuple-element.151.refs_0_, f32[1152,256]{1,0:T(8,128)} %get-tuple-element.70.refs_1_, s32[16,288,256]{2,1,0:T(8,128)} %bitcast.205, s32[16,288,256]{2,1,0:T(8,128)} %bitcast.206, f32[16,8,288]{2,1,0:T(8,128)} %all_to_all.118.refs_4_.refs_5_, ...), custom_call_target="tpu_custom_call" | custom-call | flops 1000 | bytes 1000 | tf_op jit(solution)/shard_map/near_back/pallas_call | solution.py:557
  450.5 13.9 %all-to-all-done.10.refs_0_ = bf16[4,288,1024]{2,1,0:T(8,128)(2,1)S(1)} async-done(((bf16[4,288,1024]{2,1,0:T(8,128)(2,1)}), bf16[4,288,1024]{2,1,0:T(8,128)(2,1)S(1)}, u32[]{:S(2)}, u32[]{:S(2)}) %all-to-all-start.10) | async-done | bytes 2359328 | tf_op jit(solution)/shard_map/all_to_all | solution.py:805
  481.1 10.4 %near_back.7 = bf16[1152,1024]{1,0:T(8,128)(2,1)} custom-call(s32[4]{0:T(128)} %get-tuple-element.152.refs_0_, f32[1152,256]{1,0:T(8,128)} %get-tuple-element.72.refs_1_, s32[16,288,256]{2,1,0:T(8,128)} %bitcast.207, s32[16,288,256]{2,1,0:T(8,128)} %bitcast.208, f32[16,8,288]{2,1,0:T(8,128)} %all_to_all.118.refs_4_.refs_5_, ...), custom_call_target="tpu_custom_call" | custom-call | flops 1000 | bytes 1000 | tf_op jit(solution)/shard_map/near_back/pallas_call | solution.py:557
  491.5 6.1 all-to-all-done.9.refs_0_
  520.0 10.4 %near_back.6 = bf16[1152,1024]{1,0:T(8,128)(2,1)} custom-call(s32[4]{0:T(128)} %get-tuple-element.149.refs_0_, f32[1152,256]{1,0:T(8,128)} %get-tuple-element.68.refs_1_, s32[16,288,256]{2,1,0:T(8,128)} %bitcast.209, s32[16,288,256]{2,1,0:T(8,128)} %bitcast.210, f32[16,8,288]{2,1,0:T(8,128)} %all_to_all.118.refs_4_.refs_5_, ...), custom_call_target="tpu_custom_call" | custom-call | flops 1000 | bytes 1000 | tf_op jit(solution)/shard_map/near_back/pallas_call | solution.py:557
  550.8 9.5 %collective-permute-start.23 = (bf16[576,1024]{1,0:T(8,128)(2,1)}, bf16[576,1024]{1,0:T(8,128)(2,1)}, u32[]{:S(2)}, u32[]{:S(2)}) collective-permute-start(bf16[576,1024]{1,0:T(8,128)(2,1)} %get-tuple-element.107), channel_id=1, source_target_pairs={{0,4},{4,8},{8,12},{1,5},{5,9},{9,13},{2,6},{6,10},{10,14},{3,7},{... | collective-permute-start | bytes 3538952 | tf_op jit(solution)/shard_map/ppermute | solution.py:767
  567.8 14.0 %collective-permute-done.23 = bf16[576,1024]{1,0:T(8,128)(2,1)} collective-permute-done((bf16[576,1024]{1,0:T(8,128)(2,1)}, bf16[576,1024]{1,0:T(8,128)(2,1)}, u32[]{:S(2)}, u32[]{:S(2)}) %collective-permute-start.23) | collective-permute-done | bytes 1179680 | tf_op jit(solution)/shard_map/ppermute | solution.py:767
  593.3 11.4 %convolution_convert_fusion.1 = bf16[4096,1024]{1,0:T(8,128)(2,1)S(1)} fusion(f32[576,1024]{1,0:T(8,128)S(1)} %get-tuple-element.101, f32[576]{0:T(1024)S(1)} %negate_multiply_fusion.2, f32[576,4096]{1,0:T(8,128)} %fusion.39), kind=kOutput, calls=%fused_computation.26 | convolution fusion | flops 4858445824 | bytes 20187392 | tf_op jit(solution)/shard_map/dot_general | solution.py:32
  609.4 16.3 %fusion.7.refs_0_ = bf16[576,4096]{1,0:T(8,128)(2,1)} fusion(f32[576,4096]{1,0:T(8,128)} %fusion.39, bf16[4096,1024]{1,0:T(8,128)(2,1)} %all-gather.5.cloned.1.call-done, f32[576,1024]{1,0:T(8,128)} %copy-done.21, f32[576]{0:T(1024)S(1)} %negate_multiply_fusion.2), kind=kOutput, calls=%fused_computation.21 | convolution fusion | flops 4880203776 | bytes 24905984 | tf_op jit(solution)/shard_map/dot_general | solution.py:38
  625.7 6.3 fusion.8.refs_1_
  632.7 10.8 %multiply_reduce_fusion.1 = (bf16[1024]{0:T(1024)(128)(2,1)}, f32[576]{0:T(1024)S(1)}, bf16[1024]{0:T(1024)(128)(2,1)}, f32[576,1024]{1,0:T(8,128)S(1)}) fusion(f32[576,1024]{1,0:T(8,128)} %copy-done.16, f32[576]{0:T(1024)S(1)} %copy-done.65, f32[576]{0:T(1024)S(1)} %copy-done.57, f32[1024]{0:T(1024)S(1)} %bitcast.268, bf16[576,4096]{1,0:T(8,128)(2,1)} %run_after.24, ...), kind=kOutput, calls=%fused_computation.55 | convolution fusion | flops 4836554240 | bytes 17840896 | tf_op jit(solution)/shard_map/dot_general | solution.py:38
  649.8 7.5 convolution_convert_fusion
  657.3 6.3 pad_maximum_fusion
  673.4 9.4 %reduce-scatter.10.cloned.1.call-done = bf16[1,512,1024]{2,1,0:T(8,128)(2,1)} async-done(((bf16[4,512,1024]{2,1,0:T(8,128)(2,1)}), bf16[1,512,1024]{2,1,0:T(8,128)(2,1)}) %reduce-scatter.10.cloned.1.call-update) | async-done | bytes 1048592
  688.8 8.4 fusion.refs_0_
  697.1 6.9 all-to-all-done.13
  709.7 30.0 %attend_back.1 = (bf16[2304,256]{1,0:T(8,128)(2,1)}, bf16[2304,256]{1,0:T(8,128)(2,1)}, bf16[2304,256]{1,0:T(8,128)(2,1)}) custom-call(s32[18]{0:T(128)} %pad_add_fusion.refs_0_, bf16[2304,256]{1,0:T(8,128)(2,1)} %get-tuple-element.48.refs_1_, bf16[2304,256]{1,0:T(8,128)(2,1)} %get-tuple-element.49.refs_2_, bf16[2304,256]{1,0:T(8,128)(2,1)} %get-tuple-element.50.refs_3_, ...), custom_call_target="tpu_custom_call" | custom-call | flops 1000 | bytes 1000 | tf_op jit(solution)/shard_map/attend_back/pallas_call | solution.py:328
  744.4 5.8 convolution_convert_fusion.2.refs_1_
  750.2 16.5 %reduce-scatter.12.cloned.1.call-done = bf16[1,128,5120]{2,1,0:T(8,128)(2,1)} async-done(((bf16[4,128,5120]{2,1,0:T(8,128)(2,1)}), bf16[1,128,5120]{2,1,0:T(8,128)(2,1)}) %reduce-scatter.12.cloned.1.call-update) | async-done | bytes 1310736
  780.8 8.4 fusion.14
  796.3 6.6 all-to-all-done.15
  819.3 10.7 %collective-permute-done.32.refs_2_ = bf16[32,5120]{1,0:T(8,128)(2,1)} collective-permute-done((bf16[32,5120]{1,0:T(8,128)(2,1)}, bf16[32,5120]{1,0:T(8,128)(2,1)}, u32[]{:S(2)}, u32[]{:S(2)}) %collective-permute-start.32) | collective-permute-done | bytes 327712 | tf_op jit(solution)/shard_map/ppermute | solution.py:837
  836.8 6.6 collective-permute-start.39
  882.5 7.6 all-to-all-done.16
  900.3 7.0 collective-permute-done.35
  (441 shorter events, 343.8 us)
Async XLA Ops:
  7.2 192.7 %all-gather.3.cloned.1.call-start = ((), (), s32[]{:S(2)}) async-start(), calls=%async_computation.20 | async-start | bytes 2359296 | tf_op jit(solution)/shard_map/all_gather | solution.py:970
  7.2 77.4 %collective-permute-start = (bf16[576,1024]{1,0:T(8,128)(2,1)}, bf16[576,1024]{1,0:T(8,128)(2,1)S(1)}, u32[]{:S(2)}, u32[]{:S(2)}) collective-permute-start(bf16[576,1024]{1,0:T(8,128)(2,1)} %bitcast.215), channel_id=1, source_target_pairs={{0,1},{1,0},{2,3},{3,2},{4,5},{5,4},{6,7},{7,6},{8,9},{9,8},{10,11... | collective-permute-start | bytes 3538952 | tf_op jit(solution)/shard_map/ppermute | solution.py:773
  10.2 74.4 %collective-permute-start.1 = (bf16[576,1024]{1,0:T(8,128)(2,1)}, bf16[576,1024]{1,0:T(8,128)(2,1)}, u32[]{:S(2)}, u32[]{:S(2)}) collective-permute-start(bf16[576,1024]{1,0:T(8,128)(2,1)} %bitcast.216), channel_id=1, source_target_pairs={{0,2},{1,3},{2,0},{3,1},{4,6},{5,7},{6,4},{7,5},{8,10},{9,11},{10,... | collective-permute-start | bytes 3538952 | tf_op jit(solution)/shard_map/ppermute | solution.py:773
  11.8 72.8 %collective-permute-start.2 = (bf16[576,1024]{1,0:T(8,128)(2,1)}, bf16[576,1024]{1,0:T(8,128)(2,1)}, u32[]{:S(2)}, u32[]{:S(2)}) collective-permute-start(bf16[576,1024]{1,0:T(8,128)(2,1)} %bitcast.217), channel_id=1, source_target_pairs={{0,3},{1,2},{2,1},{3,0},{4,7},{5,6},{6,5},{7,4},{8,11},{9,10},{10,... | collective-permute-start | bytes 3538952 | tf_op jit(solution)/shard_map/ppermute | solution.py:773
  18.7 54.2 %collective-permute-start.5 = (bf16[256,896]{1,0:T(8,128)(2,1)S(1)}, bf16[256,896]{1,0:T(8,128)(2,1)}, u32[]{:S(2)}, u32[]{:S(2)}) collective-permute-start(bf16[256,896]{1,0:T(8,128)(2,1)S(1)} %get-tuple-element.133), channel_id=1, source_target_pairs={{0,3},{1,2},{2,1},{3,0},{4,7},{5,6},{6,5},{7,4},{8,11},{9,10},{10,... | collective-permute-start | bytes 1376264 | tf_op jit(solution)/shard_map/ppermute | solution.py:773
  21.6 61.3 %collective-permute-start.4 = (bf16[256,896]{1,0:T(8,128)(2,1)}, bf16[256,896]{1,0:T(8,128)(2,1)}, u32[]{:S(2)}, u32[]{:S(2)}) collective-permute-start(bf16[256,896]{1,0:T(8,128)(2,1)} %get-tuple-element.134), channel_id=1, source_target_pairs={{0,2},{1,3},{2,0},{3,1},{4,6},{5,7},{6,4},{7,5},{8,10},{9,11},{10,... | collective-permute-start | bytes 1376264 | tf_op jit(solution)/shard_map/ppermute | solution.py:773
  85.6 126.7 %all-gather.5.cloned.1.call-start = ((), (), s32[]{:S(2)}) async-start(), calls=%async_computation.21 | async-start | bytes 9437184 | tf_op jit(solution)/shard_map/all_gather | solution.py:970
  89.9 32.1 %all-to-all-start.1 = ((s32[16,1,288]{2,1,0:T(1,128)}), s32[16,1,288]{2,1,0:T(1,128)S(1)}, u32[]{:S(2)}, u32[]{:S(2)}) async-start(s32[16,1,288]{2,1,0:T(1,128)} %copy.112), calls=%async_computation.1 | async-start | bytes 49152 | tf_op jit(solution)/shard_map/all_to_all | solution.py:805
  105.4 77.8 %collective-permute-start.6 = (bf16[128,4096]{1,0:T(8,128)(2,1)}, bf16[128,4096]{1,0:T(8,128)(2,1)S(1)}, u32[]{:S(2)}, u32[]{:S(2)}) collective-permute-start(bf16[128,4096]{1,0:T(8,128)(2,1)} %run_after.19.refs_0_), channel_id=1, source_target_pairs={{0,1},{1,0},{2,3},{3,2},{4,5},{5,4},{6,7},{7,6},{8,9},{9,8},{10,11... | collective-permute-start | bytes 3145736 | tf_op jit(solution)/shard_map/ppermute | solution.py:773
  107.4 75.8 %collective-permute-start.7 = (bf16[128,4096]{1,0:T(8,128)(2,1)}, bf16[128,4096]{1,0:T(8,128)(2,1)}, u32[]{:S(2)}, u32[]{:S(2)}) collective-permute-start(bf16[128,4096]{1,0:T(8,128)(2,1)} %run_after.19.refs_0_), channel_id=1, source_target_pairs={{0,2},{1,3},{2,0},{3,1},{4,6},{5,7},{6,4},{7,5},{8,10},{9,11},{10,... | collective-permute-start | bytes 3145736 | tf_op jit(solution)/shard_map/ppermute | solution.py:773
  108.9 74.4 %collective-permute-start.8 = (bf16[128,4096]{1,0:T(8,128)(2,1)}, bf16[128,4096]{1,0:T(8,128)(2,1)}, u32[]{:S(2)}, u32[]{:S(2)}) collective-permute-start(bf16[128,4096]{1,0:T(8,128)(2,1)} %run_after.19.refs_0_), channel_id=1, source_target_pairs={{0,3},{1,2},{2,1},{3,0},{4,7},{5,6},{6,5},{7,4},{8,11},{9,10},{10,... | collective-permute-start | bytes 3145736 | tf_op jit(solution)/shard_map/ppermute | solution.py:773
  122.0 26.5 %all-to-all-start.2 = ((s32[4,4,576]{2,1,0:T(4,128)}), s32[4,4,576]{2,1,0:T(4,128)S(1)}, u32[]{:S(2)}, u32[]{:S(2)}) async-start(s32[4,4,576]{2,1,0:T(4,128)} %reshape.356), calls=%async_computation.2 | async-start | bytes 81920 | tf_op jit(solution)/shard_map/all_to_all | solution.py:805
  148.5 32.8 %all-to-all-start = ((bf16[4,576,256]{2,1,0:T(8,128)(2,1)}), bf16[4,576,256]{2,1,0:T(8,128)(2,1)S(1)}, u32[]{:S(2)}, u32[]{:S(2)}) async-start(bf16[4,576,256]{2,1,0:T(8,128)(2,1)} %bitcast.237), calls=%async_computation | async-start | bytes 2359296 | tf_op jit(solution)/shard_map/all_to_all | solution.py:988
  154.9 32.3 %collective-permute-start.9 = (bf16[128,4096]{1,0:T(8,128)(2,1)S(1)}, bf16[128,4096]{1,0:T(8,128)(2,1)}, u32[]{:S(2)}, u32[]{:S(2)}) collective-permute-start(bf16[128,4096]{1,0:T(8,128)(2,1)S(1)} %copy-done.18), channel_id=1, source_target_pairs={{0,16},{16,0},{1,17},{17,1},{2,18},{18,2},{3,19},{19,3},{4,20},{20... | collective-permute-start | bytes 3145736 | tf_op jit(solution)/shard_map/ppermute | solution.py:788
  226.8 29.0 %collective-permute-start.13 = (bf16[576,1024]{1,0:T(8,128)(2,1)S(1)}, bf16[576,1024]{1,0:T(8,128)(2,1)}, u32[]{:S(2)}, u32[]{:S(2)}) collective-permute-start(bf16[576,1024]{1,0:T(8,128)(2,1)S(1)} %add_convert_fusion.5.refs_1_), channel_id=1, source_target_pairs={{0,4},{4,8},{8,12},{1,5},{5,9},{9,13},{2,6},{6,10},{10,14},{3,7},{... | collective-permute-start | bytes 3538952 | tf_op jit(solution)/shard_map/ppermute | solution.py:1016
  231.2 29.8 %collective-permute-start.14 = (bf16[576,1024]{1,0:T(8,128)(2,1)S(1)}, bf16[576,1024]{1,0:T(8,128)(2,1)}, u32[]{:S(2)}, u32[]{:S(2)}) collective-permute-start(bf16[576,1024]{1,0:T(8,128)(2,1)S(1)} %add_convert_fusion.5.refs_1_), channel_id=1, source_target_pairs={{4,0},{8,4},{12,8},{5,1},{9,5},{13,9},{6,2},{10,6},{14,10},{7,3},{... | collective-permute-start | bytes 3538952 | tf_op jit(solution)/shard_map/ppermute | solution.py:1019
  237.6 31.8 %all-to-all-start.3 = ((bf16[4,288,1024]{2,1,0:T(8,128)(2,1)}), bf16[4,288,1024]{2,1,0:T(8,128)(2,1)S(1)}, u32[]{:S(2)}, u32[]{:S(2)}) async-start(bf16[4,288,1024]{2,1,0:T(8,128)(2,1)} %pack_rows.4.refs_1_.refs_2_), calls=%async_computation.3 | async-start | bytes 4718592 | tf_op jit(solution)/shard_map/all_to_all | solution.py:805
  261.7 30.4 %collective-permute-start.16 = (bf16[576,1024]{1,0:T(8,128)(2,1)}, bf16[576,1024]{1,0:T(8,128)(2,1)}, u32[]{:S(2)}, u32[]{:S(2)}) collective-permute-start(bf16[576,1024]{1,0:T(8,128)(2,1)} %get-tuple-element.58.refs_1_.refs_2_), channel_id=1, source_target_pairs={{4,0},{8,4},{5,1},{9,5},{6,2},{10,6},{7,3},{11,7},{20,16},{24,20},... | collective-permute-start | bytes 3538952 | tf_op jit(solution)/shard_map/ppermute | solution.py:1019
  269.5 31.8 %all-to-all-start.4 = ((bf16[4,288,1024]{2,1,0:T(8,128)(2,1)}), bf16[4,288,1024]{2,1,0:T(8,128)(2,1)}, u32[]{:S(2)}, u32[]{:S(2)}) async-start(bf16[4,288,1024]{2,1,0:T(8,128)(2,1)} %pack_rows.5), calls=%async_computation.4 | async-start | bytes 4718592 | tf_op jit(solution)/shard_map/all_to_all | solution.py:805
  292.1 28.1 %collective-permute-start.17 = (bf16[576,1024]{1,0:T(8,128)(2,1)}, bf16[576,1024]{1,0:T(8,128)(2,1)S(1)}, u32[]{:S(2)}, u32[]{:S(2)}) collective-permute-start(bf16[576,1024]{1,0:T(8,128)(2,1)} %get-tuple-element.62.refs_1_.refs_2_), channel_id=1, source_target_pairs={{4,0},{5,1},{6,2},{7,3},{20,16},{21,17},{22,18},{23,19}} | collective-permute-start | bytes 3538952 | tf_op jit(solution)/shard_map/ppermute | solution.py:1019
  293.4 26.8 %collective-permute-start.18 = (bf16[576,1024]{1,0:T(8,128)(2,1)}, bf16[576,1024]{1,0:T(8,128)(2,1)}, u32[]{:S(2)}, u32[]{:S(2)}) collective-permute-start(bf16[576,1024]{1,0:T(8,128)(2,1)} %get-tuple-element.63.refs_4_.refs_3_), channel_id=1, source_target_pairs={{8,12},{9,13},{10,14},{11,15},{24,28},{25,29},{26,30},{27,31}} | collective-permute-start | bytes 3538952 | tf_op jit(solution)/shard_map/ppermute | solution.py:1016
  301.3 30.7 %all-to-all-start.5 = ((bf16[4,288,1024]{2,1,0:T(8,128)(2,1)}), bf16[4,288,1024]{2,1,0:T(8,128)(2,1)S(1)}, u32[]{:S(2)}, u32[]{:S(2)}) async-start(bf16[4,288,1024]{2,1,0:T(8,128)(2,1)} %pack_rows.6), calls=%async_computation.5 | async-start | bytes 4718592 | tf_op jit(solution)/shard_map/all_to_all | solution.py:805
  332.0 39.8 %all-to-all-start.6 = ((bf16[4,288,1024]{2,1,0:T(8,128)(2,1)}), bf16[4,288,1024]{2,1,0:T(8,128)(2,1)}, u32[]{:S(2)}, u32[]{:S(2)}) async-start(bf16[4,288,1024]{2,1,0:T(8,128)(2,1)} %pack_rows.7), calls=%async_computation.6 | async-start | bytes 4718592 | tf_op jit(solution)/shard_map/all_to_all | solution.py:805
  436.5 27.9 %all-to-all-start.10 = ((bf16[4,288,1024]{2,1,0:T(8,128)(2,1)}), bf16[4,288,1024]{2,1,0:T(8,128)(2,1)S(1)}, u32[]{:S(2)}, u32[]{:S(2)}) async-start(bf16[4,288,1024]{2,1,0:T(8,128)(2,1)} %bitcast.228), calls=%async_computation.10 | async-start | bytes 4718592 | tf_op jit(solution)/shard_map/all_to_all | solution.py:805
  465.9 31.7 %all-to-all-start.9 = ((bf16[4,288,1024]{2,1,0:T(8,128)(2,1)}), bf16[4,288,1024]{2,1,0:T(8,128)(2,1)}, u32[]{:S(2)}, u32[]{:S(2)}) async-start(bf16[4,288,1024]{2,1,0:T(8,128)(2,1)} %bitcast.227), calls=%async_computation.9 | async-start | bytes 4718592 | tf_op jit(solution)/shard_map/all_to_all | solution.py:805
  475.6 27.5 %collective-permute-start.19 = (bf16[576,1024]{1,0:T(8,128)(2,1)}, bf16[576,1024]{1,0:T(8,128)(2,1)}, u32[]{:S(2)}, u32[]{:S(2)}) collective-permute-start(bf16[576,1024]{1,0:T(8,128)(2,1)} %unpack_rows.4.refs_7_), channel_id=1, source_target_pairs={{0,4},{1,5},{2,6},{3,7},{16,20},{17,21},{18,22},{19,23}} | collective-permute-start | bytes 3538952 | tf_op jit(solution)/shard_map/ppermute | solution.py:767
  479.5 23.7 %collective-permute-start.20 = (bf16[576,1024]{1,0:T(8,128)(2,1)}, bf16[576,1024]{1,0:T(8,128)(2,1)}, u32[]{:S(2)}, u32[]{:S(2)}) collective-permute-start(bf16[576,1024]{1,0:T(8,128)(2,1)} %unpack_rows.4.refs_7_), channel_id=1, source_target_pairs={{12,8},{13,9},{14,10},{15,11},{28,24},{29,25},{30,26},{31,27}} | collective-permute-start | bytes 3538952 | tf_op jit(solution)/shard_map/ppermute | solution.py:768
  497.6 32.8 %all-to-all-start.12 = ((bf16[4,288,1024]{2,1,0:T(8,128)(2,1)}), bf16[4,288,1024]{2,1,0:T(8,128)(2,1)S(1)}, u32[]{:S(2)}, u32[]{:S(2)}) async-start(bf16[4,288,1024]{2,1,0:T(8,128)(2,1)} %bitcast.231), calls=%async_computation.12 | async-start | bytes 4718592 | tf_op jit(solution)/shard_map/all_to_all | solution.py:805
  512.9 28.1 %collective-permute-start.21 = (bf16[576,1024]{1,0:T(8,128)(2,1)}, bf16[576,1024]{1,0:T(8,128)(2,1)}, u32[]{:S(2)}, u32[]{:S(2)}) collective-permute-start(bf16[576,1024]{1,0:T(8,128)(2,1)} %get-tuple-element.109), channel_id=1, source_target_pairs={{0,4},{4,8},{1,5},{5,9},{2,6},{6,10},{3,7},{7,11},{16,20},{20,24},... | collective-permute-start | bytes 3538952 | tf_op jit(solution)/shard_map/ppermute | solution.py:767
  518.4 22.7 %collective-permute-start.22 = (bf16[576,1024]{1,0:T(8,128)(2,1)}, bf16[576,1024]{1,0:T(8,128)(2,1)}, u32[]{:S(2)}, u32[]{:S(2)}) collective-permute-start(bf16[576,1024]{1,0:T(8,128)(2,1)} %get-tuple-element.110), channel_id=1, source_target_pairs={{8,4},{12,8},{9,5},{13,9},{10,6},{14,10},{11,7},{15,11},{24,20},{2... | collective-permute-start | bytes 3538952 | tf_op jit(solution)/shard_map/ppermute | solution.py:768
  531.8 30.5 %all-to-all-start.11 = ((bf16[4,288,1024]{2,1,0:T(8,128)(2,1)}), bf16[4,288,1024]{2,1,0:T(8,128)(2,1)}, u32[]{:S(2)}, u32[]{:S(2)}) async-start(bf16[4,288,1024]{2,1,0:T(8,128)(2,1)} %bitcast.230), calls=%async_computation.11 | async-start | bytes 4718592 | tf_op jit(solution)/shard_map/all_to_all | solution.py:805
  536.4 146.5 %reduce-scatter.10.cloned.1.call-start = ((), (), s32[]{:S(2)}) async-start(), calls=%async_computation.23 | async-start | bytes 5242880
  550.8 31.0 %collective-permute-start.23 = (bf16[576,1024]{1,0:T(8,128)(2,1)}, bf16[576,1024]{1,0:T(8,128)(2,1)}, u32[]{:S(2)}, u32[]{:S(2)}) collective-permute-start(bf16[576,1024]{1,0:T(8,128)(2,1)} %get-tuple-element.107), channel_id=1, source_target_pairs={{0,4},{4,8},{8,12},{1,5},{5,9},{9,13},{2,6},{6,10},{10,14},{3,7},{... | collective-permute-start | bytes 3538952 | tf_op jit(solution)/shard_map/ppermute | solution.py:767
  560.3 26.7 %collective-permute-start.24 = (bf16[576,1024]{1,0:T(8,128)(2,1)}, bf16[576,1024]{1,0:T(8,128)(2,1)}, u32[]{:S(2)}, u32[]{:S(2)}) collective-permute-start(bf16[576,1024]{1,0:T(8,128)(2,1)} %get-tuple-element.108), channel_id=1, source_target_pairs={{4,0},{8,4},{12,8},{5,1},{9,5},{13,9},{6,2},{10,6},{14,10},{7,3},{... | collective-permute-start | bytes 3538952 | tf_op jit(solution)/shard_map/ppermute | solution.py:768
  688.7 77.9 %reduce-scatter.12.cloned.1.call-start = ((), (), s32[]{:S(2)}) async-start(), calls=%async_computation.24 | async-start | bytes 6553600
  705.1 34.6 %all-to-all-start.14 = ((bf16[4,128,1024]{2,1,0:T(8,128)(2,1)}), bf16[4,128,1024]{2,1,0:T(8,128)(2,1)S(1)}, u32[]{:S(2)}, u32[]{:S(2)}) async-start(bf16[4,128,1024]{2,1,0:T(8,128)(2,1)} %bitcast.221), calls=%async_computation.14 | async-start | bytes 2097152 | tf_op jit(solution)/shard_map/all_to_all | solution.py:805
  766.7 36.2 %all-to-all-start.15 = ((bf16[4,32,5120]{2,1,0:T(8,128)(2,1)}), bf16[4,32,5120]{2,1,0:T(8,128)(2,1)}, u32[]{:S(2)}, u32[]{:S(2)}) async-start(bf16[4,32,5120]{2,1,0:T(8,128)(2,1)} %bitcast.236), calls=%async_computation.16 | async-start | bytes 2621440 | tf_op jit(solution)/shard_map/all_to_all | solution.py:805
  771.4 122.7 %reduce-scatter.8.cloned.1.call-start = ((), (), s32[]{:S(2)}) async-start(), calls=%async_computation.22 | async-start | bytes 5898240 | tf_op jit(solution)/shard_map/reduce_scatter | solution.py:1147
  805.0 25.0 %collective-permute-start.32 = (bf16[32,5120]{1,0:T(8,128)(2,1)}, bf16[32,5120]{1,0:T(8,128)(2,1)}, u32[]{:S(2)}, u32[]{:S(2)}) collective-permute-start(bf16[32,5120]{1,0:T(8,128)(2,1)} %fusion.61.refs_1_), channel_id=1, source_target_pairs={{0,8},{4,12},{8,0},{12,4},{1,9},{5,13},{9,1},{13,5},{2,10},{6,14},... | collective-permute-start | bytes 983048 | tf_op jit(solution)/shard_map/ppermute | solution.py:837
  807.2 22.9 %collective-permute-start.33 = (bf16[32,5120]{1,0:T(8,128)(2,1)}, bf16[32,5120]{1,0:T(8,128)(2,1)}, u32[]{:S(2)}, u32[]{:S(2)}) collective-permute-start(bf16[32,5120]{1,0:T(8,128)(2,1)} %fusion.61.refs_1_), channel_id=1, source_target_pairs={{0,12},{4,0},{8,4},{12,8},{1,13},{5,1},{9,5},{13,9},{2,14},{6,2},{... | collective-permute-start | bytes 983048 | tf_op jit(solution)/shard_map/ppermute | solution.py:837
  814.9 28.5 %collective-permute-start.28 = (bf16[128,896]{1,0:T(8,128)(2,1)}, bf16[128,896]{1,0:T(8,128)(2,1)}, u32[]{:S(2)}, u32[]{:S(2)}) collective-permute-start(bf16[128,896]{1,0:T(8,128)(2,1)} %get-tuple-element.130), channel_id=1, source_target_pairs={{0,1},{1,0},{2,3},{3,2},{4,5},{5,4},{6,7},{7,6},{8,9},{9,8},{10,11... | collective-permute-start | bytes 688136 | tf_op jit(solution)/shard_map/ppermute | solution.py:773
  816.2 27.2 %collective-permute-start.29 = (bf16[128,896]{1,0:T(8,128)(2,1)}, bf16[128,896]{1,0:T(8,128)(2,1)}, u32[]{:S(2)}, u32[]{:S(2)}) collective-permute-start(bf16[128,896]{1,0:T(8,128)(2,1)} %get-tuple-element.129), channel_id=1, source_target_pairs={{0,2},{1,3},{2,0},{3,1},{4,6},{5,7},{6,4},{7,5},{8,10},{9,11},{10,... | collective-permute-start | bytes 688136 | tf_op jit(solution)/shard_map/ppermute | solution.py:773
  817.9 28.0 %collective-permute-start.30 = (bf16[128,896]{1,0:T(8,128)(2,1)}, bf16[128,896]{1,0:T(8,128)(2,1)}, u32[]{:S(2)}, u32[]{:S(2)}) collective-permute-start(bf16[128,896]{1,0:T(8,128)(2,1)} %get-tuple-element.128), channel_id=1, source_target_pairs={{0,3},{1,2},{2,1},{3,0},{4,7},{5,6},{6,5},{7,4},{8,11},{9,10},{10,... | collective-permute-start | bytes 688136 | tf_op jit(solution)/shard_map/ppermute | solution.py:773
  835.6 37.7 %collective-permute-start.38 = (bf16[4,32,5120]{2,1,0:T(8,128)(2,1)}, bf16[4,32,5120]{2,1,0:T(8,128)(2,1)}, u32[]{:S(2)}, u32[]{:S(2)}) collective-permute-start(bf16[4,32,5120]{2,1,0:T(8,128)(2,1)} %gather_fusion.5), channel_id=1, source_target_pairs={{0,16},{16,0},{1,17},{17,1},{2,18},{18,2},{3,19},{19,3},{4,20},{20... | collective-permute-start | bytes 3932168 | tf_op jit(solution)/shard_map/ppermute | solution.py:788
  836.8 32.1 %collective-permute-start.39 = (bf16[128,1024]{1,0:T(8,128)(2,1)}, bf16[128,1024]{1,0:T(8,128)(2,1)}, u32[]{:S(2)}, u32[]{:S(2)}) collective-permute-start(bf16[128,1024]{1,0:T(8,128)(2,1)} %run_after.33), channel_id=1, source_target_pairs={{0,4},{4,8},{8,12},{12,0},{1,5},{5,9},{9,13},{13,1},{2,6},{6,10},{... | collective-permute-start | bytes 786440 | tf_op jit(solution)/shard_map/ppermute | solution.py:837
  843.4 25.5 %collective-permute-start.40 = (bf16[128,1024]{1,0:T(8,128)(2,1)}, bf16[128,1024]{1,0:T(8,128)(2,1)}, u32[]{:S(2)}, u32[]{:S(2)}) collective-permute-start(bf16[128,1024]{1,0:T(8,128)(2,1)} %run_after.33), channel_id=1, source_target_pairs={{0,8},{4,12},{8,0},{12,4},{1,9},{5,13},{9,1},{13,5},{2,10},{6,14},... | collective-permute-start | bytes 786440 | tf_op jit(solution)/shard_map/ppermute | solution.py:837
  843.4 25.6 %collective-permute-start.41 = (bf16[128,1024]{1,0:T(8,128)(2,1)}, bf16[128,1024]{1,0:T(8,128)(2,1)}, u32[]{:S(2)}, u32[]{:S(2)}) collective-permute-start(bf16[128,1024]{1,0:T(8,128)(2,1)} %run_after.33), channel_id=1, source_target_pairs={{0,12},{4,0},{8,4},{12,8},{1,13},{5,1},{9,5},{13,9},{2,14},{6,2},{... | collective-permute-start | bytes 786440 | tf_op jit(solution)/shard_map/ppermute | solution.py:837
  865.1 25.0 %all-to-all-start.16 = ((bf16[4,32,3200]{2,1,0:T(8,128)(2,1)}), bf16[4,32,3200]{2,1,0:T(8,128)(2,1)S(1)}, u32[]{:S(2)}, u32[]{:S(2)}) async-start(bf16[4,32,3200]{2,1,0:T(8,128)(2,1)} %bitcast.234), calls=%async_computation.17 | async-start | bytes 1638400 | tf_op jit(solution)/shard_map/all_to_all | solution.py:805
  (96 other events, 910.8 us)
Sparse Core Ops, SparseCore 0:
  85.8 33.1 all-gather.2
  121.4 84.6 all-gather.4
  632.2 50.6 reduce-scatter.9
  705.2 61.4 reduce-scatter.11
  777.8 65.0 reduce-scatter.7

commit v5 on v4

--- a/solution.py
+++ b/solution.py
@@ -74,23 +74,23 @@
 
 
 def place_kernel(count, start_ref, *refs):
+    rows = refs[0].shape[0]
     for place in range(count):
-
-        @pl.when(pl.program_id(0) == place)
-        def _():
-            refs[count][...] = refs[place][...]
+        there = pl.ds(pl.multiple_of(start_ref[place] * rows, rows), rows)
+        refs[count][there, :] = refs[place][...]
 
 
 def place_rows(pieces, places):
     count = len(pieces)
     rows, width = pieces[0].shape
+    columns = row_chunk(width, (512, 256, 128))
     return pl.pallas_call(
         functools.partial(place_kernel, count),
         grid_spec=pltpu.PrefetchScalarGridSpec(
             num_scalar_prefetch=1,
-            grid=(count,),
-            in_specs=[spec((rows, width), lambda i, places: (0, 0))] * count,
-            out_specs=spec((rows, width), lambda i, places: (places[i], 0)),
+            grid=(width // columns,),
+            in_specs=[spec((rows, columns), lambda i, places: (0, i))] * count,
+            out_specs=spec((count * rows, columns), lambda i, places: (0, i)),
         ),
         out_shape=jax.ShapeDtypeStruct((count * rows, width), pieces[0].dtype),
         compiler_params=kernel_params(),

time: 934 us -> 935 us (level)
  transfers between devices with their start and end apart: 63 -> 63, of which waited for: 31 -> 28; matrix products, arithmetic and copies ran while one was open for 21% -> 21% of each run, Pallas kernels for 21% -> 20%
where the time goes in v5:
time: 935 us; the launch traced here: 926 us
  waiting for transfers between devices  257 us (27%)
  Pallas kernels  222 us (24%)
  starting transfers between devices  135 us (14%)
  matrix products  89.7 us (10%)
  local copies, waits for them, and re-layouts  89.5 us (10%)
  other arithmetic  87.6 us (9%)
  blocking collectives  30.2 us (3%)
  between operations  15.3 us (2%)
    ppermute x12, waiting for transfers between devices, across(): lax.ppermute(rows, 'ctx', [(i, i ^ step) for i in range(lax.axis_size('ct...  59.3 us
    all_to_all x13, starting transfers between devices, exchange(): return lax.all_to_all(blocks, axis, split_axis=0, concat_axis=0, tiled=True)  57 us
    pallas_call x4, Pallas kernels, near_scores(): pl.pallas_call(functools.partial(near_kernel, spacing, width ** (-0.5), p...  44.4 us
    pallas_call x4, Pallas kernels, near_back(): pl.pallas_call(later(functools.partial(near_back_kernel, spacing, 2.0 * w...  41.5 us
    all_to_all x13, waiting for transfers between devices, exchange(): return lax.all_to_all(blocks, axis, split_axis=0, concat_axis=0, tiled=True)  39.1 us
    ppermute x3, waiting for transfers between devices, local(): lax.ppermute(down, 'batch', [(i, i - 1) for i in range(1, layer_count - s...  39.1 us
    dot_general x4, matrix products, right_dot(): lax.dot_general(left_side, right_side, (((1,), (1,)), ((), ())), preferre...  35.3 us
    dot_general x5, matrix products, left_dot(): lax.dot_general(left_side, right_side, (((0,), (0,)), ((), ())), preferre...  30.7 us
  transfers between devices with their start and end apart: 63, of which 28 were waited for; matrix products, arithmetic and copies ran while one was open for 21% of the time, Pallas kernels for 20%

profile of v5, /device:TPU:0, one launch (start us, length us, event | category | flops | bytes accessed | tf_op | source)
XLA Modules:
  0.0 926.1 jit_solution(13778317126029062877)
XLA Ops:
  22.1 50.8 %collective-permute-done.5.refs_7_.refs_6_ = bf16[256,896]{1,0:T(8,128)(2,1)} collective-permute-done((bf16[256,896]{1,0:T(8,128)(2,1)S(1)}, bf16[256,896]{1,0:T(8,128)(2,1)}, u32[]{:S(2)}, u32[]{:S(2)}) %collective-permute-start.5) | collective-permute-done | bytes 458784 | tf_op jit(solution)/shard_map/ppermute | solution.py:773
  76.1 6.8 collective-permute-done.4.refs_6_.refs_5_
  89.9 6.2 all-to-all-start.1
  108.9 13.1 %project_rows.1 = (bf16[1024,768]{1,0:T(8,128)(2,1)}, bf16[2304,1024]{1,0:T(8,128)(2,1)}, bf16[2304,1024]{1,0:T(8,128)(2,1)}, bf16[2304,256]{1,0:T(8,128)(2,1)},...) custom-call(s32[4]{0:T(128)} %iota_xor_fusion.order_ref, bf16[576,1024]{1,0:T(8,128)(2,1)} %bitcast.218, ...), custom_call_target="tpu_custom_call" | custom-call | flops 12999999488 | bytes 1000 | tf_op jit(solution)/shard_map/project_rows/pallas_call | solution.py:392
  127.7 20.1 %attend.1 = (bf16[2304,256]{1,0:T(8,128)(2,1)}, f32[8,2304]{1,0:T(8,128)}) custom-call(s32[18]{0:T(128)} %pad_add_fusion.refs_0_, bf16[2304,256]{1,0:T(8,128)(2,1)} %get-tuple-element.48.refs_1_, bf16[2304,256]{1,0:T(8,128)(2,1)} %get-tuple-element.49.refs_2_, bf16[2304,256]{1,0:T(8,128)(2,1)} %get-tuple-element.50.refs_3_, ...), custom_call_target="tpu_custom_call" | custom-call | flops 20000000000 | bytes 1000 | tf_op jit(solution)/shard_map/attend/pallas_call | solution.py:193
  154.2 27.1 %all-to-all-done = bf16[4,576,256]{2,1,0:T(8,128)(2,1)S(1)} async-done(((bf16[4,576,256]{2,1,0:T(8,128)(2,1)}), bf16[4,576,256]{2,1,0:T(8,128)(2,1)S(1)}, u32[]{:S(2)}, u32[]{:S(2)}) %all-to-all-start) | async-done | bytes 1179680 | tf_op jit(solution)/shard_map/all_to_all | solution.py:988
  190.4 9.7 %place_rows.1 = bf16[1024,4096]{1,0:T(8,128)(2,1)} custom-call(s32[8]{0:T(128)} %pad_add_fusion.1.start_ref, bf16[128,4096]{1,0:T(8,128)(2,1)} %run_after.19.refs_0_, bf16[128,4096]{1,0:T(8,128)(2,1)} %get-tuple-element.52.refs_1_, bf16[128,4096]{1,0:T(8,128)(2,1)} %get-tuple-element.53.refs_2_, bf16[128,4096]{1,0:T(8,128)(2,1)} %get-tuple-element.54.refs_3_, ...), custom_call_target="tpu_custom_call" | custom-call | flops 1000 | bytes 1000 | tf_op jit(solution)/shard_map/place_rows/pallas_call | solution.py:87
  204.8 7.8 fusion.39
  212.6 12.6 %fusion.44 = (f32[576]{0:T(1024)S(1)}, f32[576,1024]{1,0:T(8,128)S(1)}) fusion(f32[576,1024]{1,0:T(8,128)} %copy-done.16, bf16[4096,1024]{1,0:T(8,128)(2,1)} %all-gather.5.cloned.1.call-done, f32[576,4096]{1,0:T(8,128)} %fusion.39), kind=kOutput, calls=%fused_computation.214 | convolution fusion | flops 4854251008 | bytes 22546688 | tf_op jit(solution)/shard_map/dot_general | solution.py:28
  241.5 8.5 key_planes.1
  250.0 5.9 collective-permute-done.13.refs_0_
  263.4 6.1 pack_rows.5
  274.0 18.3 %collective-permute-done.16.refs_1_ = bf16[576,1024]{1,0:T(8,128)(2,1)} collective-permute-done((bf16[576,1024]{1,0:T(8,128)(2,1)}, bf16[576,1024]{1,0:T(8,128)(2,1)}, u32[]{:S(2)}, u32[]{:S(2)}) %collective-permute-start.16) | collective-permute-done | bytes 1179680 | tf_op jit(solution)/shard_map/ppermute | solution.py:1019
  295.3 5.9 pack_rows.6
  304.9 15.5 %collective-permute-done.17.refs_1_ = bf16[576,1024]{1,0:T(8,128)(2,1)S(1)} collective-permute-done((bf16[576,1024]{1,0:T(8,128)(2,1)}, bf16[576,1024]{1,0:T(8,128)(2,1)S(1)}, u32[]{:S(2)}, u32[]{:S(2)}) %collective-permute-start.17) | collective-permute-done | bytes 1179680 | tf_op jit(solution)/shard_map/ppermute | solution.py:1019
  321.4 5.9 pack_rows.7
  338.6 11.1 %near_scores.4 = (f32[1152,256]{1,0:T(8,128)}, f32[4,8,288]{2,1,0:T(8,128)}) custom-call(s32[4]{0:T(128)} %get-tuple-element.149.refs_0_, bf16[1152,1024]{1,0:T(8,128)(2,1)} %bitcast.214, bf16[1024,2048]{1,0:T(8,128)(2,1)} %get-tuple-element.55.refs_2_.refs_5_, f32[8,256]{1,0:T(8,128)} %get-tuple-element.56.refs_3_.refs_6_, f32[8,256]{1,0:T(8,128)} %bitcast.247, ...), custom_call_target="tpu_custom_call" | custom-call | flops 1000 | bytes 1000 | tf_op jit(solution)/shard_map/near_scores/pallas_call | solution.py:504
  349.6 11.1 %near_scores.5 = (f32[1152,256]{1,0:T(8,128)}, f32[4,8,288]{2,1,0:T(8,128)}) custom-call(s32[4]{0:T(128)} %get-tuple-element.152.refs_0_, bf16[1152,1024]{1,0:T(8,128)(2,1)} %bitcast.29.refs_1_, bf16[1024,2048]{1,0:T(8,128)(2,1)} %get-tuple-element.55.refs_2_.refs_5_, f32[8,256]{1,0:T(8,128)} %get-tuple-element.56.refs_3_.refs_6_, f32[8,256]{1,0:T(8,128)} %bitcast.248, ...), custom_call_target="tpu_custom_call" | custom-call | flops 1000 | bytes 1000 | tf_op jit(solution)/shard_map/near_scores/pallas_call | solution.py:504
  360.7 11.1 %near_scores.6 = (f32[1152,256]{1,0:T(8,128)}, f32[4,8,288]{2,1,0:T(8,128)}) custom-call(s32[4]{0:T(128)} %get-tuple-element.151.refs_0_, bf16[1152,1024]{1,0:T(8,128)(2,1)} %bitcast.229, bf16[1024,2048]{1,0:T(8,128)(2,1)} %get-tuple-element.55.refs_2_.refs_5_, f32[8,256]{1,0:T(8,128)} %get-tuple-element.56.refs_3_.refs_6_, f32[8,256]{1,0:T(8,128)} %bitcast.249, ...), custom_call_target="tpu_custom_call" | custom-call | flops 1000 | bytes 1000 | tf_op jit(solution)/shard_map/near_scores/pallas_call | solution.py:504
  371.8 11.2 %near_scores.7 = (f32[1152,256]{1,0:T(8,128)}, f32[4,8,288]{2,1,0:T(8,128)}) custom-call(s32[4]{0:T(128)} %get-tuple-element.150.refs_0_, bf16[1152,1024]{1,0:T(8,128)(2,1)} %bitcast.38.refs_1_, bf16[1024,2048]{1,0:T(8,128)(2,1)} %get-tuple-element.55.refs_2_.refs_5_, f32[8,256]{1,0:T(8,128)} %get-tuple-element.56.refs_3_.refs_6_, f32[8,256]{1,0:T(8,128)} %bitcast.250, ...), custom_call_target="tpu_custom_call" | custom-call | flops 1000 | bytes 1000 | tf_op jit(solution)/shard_map/near_scores/pallas_call | solution.py:504
  384.4 17.8 %all_to_all.117.stats_ref = f32[16,8,288]{2,1,0:T(8,128)} all-to-all(f32[16,8,288]{2,1,0:T(8,128)S(1)} %bitcast.246), channel_id=1, replica_groups=mesh['rep'=2,'batch'=4,'ctx'=4] {'batch','ctx'}, dimensions={0} | all-to-all | bytes 294912 | tf_op jit(solution)/shard_map/all_to_all | solution.py:805
  402.2 11.8 %mix_losses.1 = (f32[1,576]{1,0:T(1,128)}, f32[16,8,288]{2,1,0:T(8,128)}) custom-call(f32[16,8,288]{2,1,0:T(8,128)} %all_to_all.117.stats_ref, s32[16,576]{1,0:T(8,128)} %copy-done.41, f32[1,576]{1,0:T(1,128)} %prob_ref.1), custom_call_target="tpu_custom_call" | custom-call | tf_op jit(solution)/shard_map/mix_losses/pallas_call | solution.py:697
  414.1 12.4 %all_to_all.118.refs_4_.refs_5_ = f32[16,8,288]{2,1,0:T(8,128)} all-to-all(f32[16,8,288]{2,1,0:T(8,128)} %get-tuple-element.69), channel_id=1, replica_groups=mesh['rep'=2,'batch'=4,'ctx'=4] {'batch','ctx'}, dimensions={0} | all-to-all | bytes 294912 | tf_op jit(solution)/shard_map/all_to_all | solution.py:805
  426.5 10.4 %near_back.5 = bf16[1152,1024]{1,0:T(8,128)(2,1)} custom-call(s32[4]{0:T(128)} %get-tuple-element.150.refs_0_, f32[1152,256]{1,0:T(8,128)} %get-tuple-element.71.refs_1_, s32[16,288,256]{2,1,0:T(8,128)} %bitcast.203, s32[16,288,256]{2,1,0:T(8,128)} %bitcast.204, f32[16,8,288]{2,1,0:T(8,128)} %all_to_all.118.refs_4_.refs_5_, ...), custom_call_target="tpu_custom_call" | custom-call | flops 1000 | bytes 1000 | tf_op jit(solution)/shard_map/near_back/pallas_call | solution.py:557
  440.5 10.4 %near_back.4 = bf16[1152,1024]{1,0:T(8,128)(2,1)} custom-call(s32[4]{0:T(128)} %get-tuple-element.151.refs_0_, f32[1152,256]{1,0:T(8,128)} %get-tuple-element.70.refs_1_, s32[16,288,256]{2,1,0:T(8,128)} %bitcast.205, s32[16,288,256]{2,1,0:T(8,128)} %bitcast.206, f32[16,8,288]{2,1,0:T(8,128)} %all_to_all.118.refs_4_.refs_5_, ...), custom_call_target="tpu_custom_call" | custom-call | flops 1000 | bytes 1000 | tf_op jit(solution)/shard_map/near_back/pallas_call | solution.py:557
  450.8 13.9 %all-to-all-done.10.refs_0_ = bf16[4,288,1024]{2,1,0:T(8,128)(2,1)S(1)} async-done(((bf16[4,288,1024]{2,1,0:T(8,128)(2,1)}), bf16[4,288,1024]{2,1,0:T(8,128)(2,1)S(1)}, u32[]{:S(2)}, u32[]{:S(2)}) %all-to-all-start.10) | async-done | bytes 2359328 | tf_op jit(solution)/shard_map/all_to_all | solution.py:805
  481.3 10.4 %near_back.7 = bf16[1152,1024]{1,0:T(8,128)(2,1)} custom-call(s32[4]{0:T(128)} %get-tuple-element.152.refs_0_, f32[1152,256]{1,0:T(8,128)} %get-tuple-element.72.refs_1_, s32[16,288,256]{2,1,0:T(8,128)} %bitcast.207, s32[16,288,256]{2,1,0:T(8,128)} %bitcast.208, f32[16,8,288]{2,1,0:T(8,128)} %all_to_all.118.refs_4_.refs_5_, ...), custom_call_target="tpu_custom_call" | custom-call | flops 1000 | bytes 1000 | tf_op jit(solution)/shard_map/near_back/pallas_call | solution.py:557
  491.7 6.2 all-to-all-done.9.refs_0_
  520.2 10.4 %near_back.6 = bf16[1152,1024]{1,0:T(8,128)(2,1)} custom-call(s32[4]{0:T(128)} %get-tuple-element.149.refs_0_, f32[1152,256]{1,0:T(8,128)} %get-tuple-element.68.refs_1_, s32[16,288,256]{2,1,0:T(8,128)} %bitcast.209, s32[16,288,256]{2,1,0:T(8,128)} %bitcast.210, f32[16,8,288]{2,1,0:T(8,128)} %all_to_all.118.refs_4_.refs_5_, ...), custom_call_target="tpu_custom_call" | custom-call | flops 1000 | bytes 1000 | tf_op jit(solution)/shard_map/near_back/pallas_call | solution.py:557
  551.0 9.6 %collective-permute-start.23 = (bf16[576,1024]{1,0:T(8,128)(2,1)}, bf16[576,1024]{1,0:T(8,128)(2,1)}, u32[]{:S(2)}, u32[]{:S(2)}) collective-permute-start(bf16[576,1024]{1,0:T(8,128)(2,1)} %get-tuple-element.107), channel_id=1, source_target_pairs={{0,4},{4,8},{8,12},{1,5},{5,9},{9,13},{2,6},{6,10},{10,14},{3,7},{... | collective-permute-start | bytes 3538952 | tf_op jit(solution)/shard_map/ppermute | solution.py:767
  568.0 14.1 %collective-permute-done.23 = bf16[576,1024]{1,0:T(8,128)(2,1)} collective-permute-done((bf16[576,1024]{1,0:T(8,128)(2,1)}, bf16[576,1024]{1,0:T(8,128)(2,1)}, u32[]{:S(2)}, u32[]{:S(2)}) %collective-permute-start.23) | collective-permute-done | bytes 1179680 | tf_op jit(solution)/shard_map/ppermute | solution.py:767
  593.6 11.4 %convolution_convert_fusion.1 = bf16[4096,1024]{1,0:T(8,128)(2,1)S(1)} fusion(f32[576,1024]{1,0:T(8,128)S(1)} %get-tuple-element.101, f32[576]{0:T(1024)S(1)} %negate_multiply_fusion.2, f32[576,4096]{1,0:T(8,128)} %fusion.39), kind=kOutput, calls=%fused_computation.26 | convolution fusion | flops 4858445824 | bytes 20187392 | tf_op jit(solution)/shard_map/dot_general | solution.py:32
  609.7 16.3 %fusion.7.refs_0_ = bf16[576,4096]{1,0:T(8,128)(2,1)} fusion(f32[576,4096]{1,0:T(8,128)} %fusion.39, bf16[4096,1024]{1,0:T(8,128)(2,1)} %all-gather.5.cloned.1.call-done, f32[576,1024]{1,0:T(8,128)} %copy-done.21, f32[576]{0:T(1024)S(1)} %negate_multiply_fusion.2), kind=kOutput, calls=%fused_computation.21 | convolution fusion | flops 4880203776 | bytes 24905984 | tf_op jit(solution)/shard_map/dot_general | solution.py:38
  626.0 6.3 fusion.8.refs_1_
  633.0 10.8 %multiply_reduce_fusion.1 = (bf16[1024]{0:T(1024)(128)(2,1)}, f32[576]{0:T(1024)S(1)}, bf16[1024]{0:T(1024)(128)(2,1)}, f32[576,1024]{1,0:T(8,128)S(1)}) fusion(f32[576,1024]{1,0:T(8,128)} %copy-done.16, f32[576]{0:T(1024)S(1)} %copy-done.65, f32[576]{0:T(1024)S(1)} %copy-done.57, f32[1024]{0:T(1024)S(1)} %bitcast.268, bf16[576,4096]{1,0:T(8,128)(2,1)} %run_after.24, ...), kind=kOutput, calls=%fused_computation.55 | convolution fusion | flops 4836554240 | bytes 17840896 | tf_op jit(solution)/shard_map/dot_general | solution.py:38
  650.1 7.5 convolution_convert_fusion
  657.7 6.3 pad_maximum_fusion
  673.7 9.4 %reduce-scatter.10.cloned.1.call-done = bf16[1,512,1024]{2,1,0:T(8,128)(2,1)} async-done(((bf16[4,512,1024]{2,1,0:T(8,128)(2,1)}), bf16[1,512,1024]{2,1,0:T(8,128)(2,1)}) %reduce-scatter.10.cloned.1.call-update) | async-done | bytes 1048592
  689.1 8.4 fusion.refs_0_
  697.4 6.9 all-to-all-done.13
  710.0 28.8 %attend_back.1 = (bf16[2304,256]{1,0:T(8,128)(2,1)}, bf16[2304,256]{1,0:T(8,128)(2,1)}, bf16[2304,256]{1,0:T(8,128)(2,1)}) custom-call(s32[18]{0:T(128)} %pad_add_fusion.refs_0_, bf16[2304,256]{1,0:T(8,128)(2,1)} %get-tuple-element.48.refs_1_, bf16[2304,256]{1,0:T(8,128)(2,1)} %get-tuple-element.49.refs_2_, bf16[2304,256]{1,0:T(8,128)(2,1)} %get-tuple-element.50.refs_3_, ...), custom_call_target="tpu_custom_call" | custom-call | flops 1000 | bytes 1000 | tf_op jit(solution)/shard_map/attend_back/pallas_call | solution.py:328
  749.4 17.6 %reduce-scatter.12.cloned.1.call-done = bf16[1,128,5120]{2,1,0:T(8,128)(2,1)} async-done(((bf16[4,128,5120]{2,1,0:T(8,128)(2,1)}), bf16[1,128,5120]{2,1,0:T(8,128)(2,1)}) %reduce-scatter.12.cloned.1.call-update) | async-done | bytes 1310736
  781.1 8.4 fusion.14
  796.6 6.6 all-to-all-done.15
  819.6 10.7 %collective-permute-done.32.refs_2_ = bf16[32,5120]{1,0:T(8,128)(2,1)} collective-permute-done((bf16[32,5120]{1,0:T(8,128)(2,1)}, bf16[32,5120]{1,0:T(8,128)(2,1)}, u32[]{:S(2)}, u32[]{:S(2)}) %collective-permute-start.32) | collective-permute-done | bytes 327712 | tf_op jit(solution)/shard_map/ppermute | solution.py:837
  837.1 6.6 collective-permute-start.39
  882.8 7.6 all-to-all-done.16
  900.6 7.0 collective-permute-done.35
  (441 shorter events, 342.1 us)
Async XLA Ops:
  7.2 192.9 %all-gather.3.cloned.1.call-start = ((), (), s32[]{:S(2)}) async-start(), calls=%async_computation.20 | async-start | bytes 2359296 | tf_op jit(solution)/shard_map/all_gather | solution.py:970
  7.2 77.4 %collective-permute-start = (bf16[576,1024]{1,0:T(8,128)(2,1)}, bf16[576,1024]{1,0:T(8,128)(2,1)S(1)}, u32[]{:S(2)}, u32[]{:S(2)}) collective-permute-start(bf16[576,1024]{1,0:T(8,128)(2,1)} %bitcast.215), channel_id=1, source_target_pairs={{0,1},{1,0},{2,3},{3,2},{4,5},{5,4},{6,7},{7,6},{8,9},{9,8},{10,11... | collective-permute-start | bytes 3538952 | tf_op jit(solution)/shard_map/ppermute | solution.py:773
  10.2 74.4 %collective-permute-start.1 = (bf16[576,1024]{1,0:T(8,128)(2,1)}, bf16[576,1024]{1,0:T(8,128)(2,1)}, u32[]{:S(2)}, u32[]{:S(2)}) collective-permute-start(bf16[576,1024]{1,0:T(8,128)(2,1)} %bitcast.216), channel_id=1, source_target_pairs={{0,2},{1,3},{2,0},{3,1},{4,6},{5,7},{6,4},{7,5},{8,10},{9,11},{10,... | collective-permute-start | bytes 3538952 | tf_op jit(solution)/shard_map/ppermute | solution.py:773
  11.8 72.8 %collective-permute-start.2 = (bf16[576,1024]{1,0:T(8,128)(2,1)}, bf16[576,1024]{1,0:T(8,128)(2,1)}, u32[]{:S(2)}, u32[]{:S(2)}) collective-permute-start(bf16[576,1024]{1,0:T(8,128)(2,1)} %bitcast.217), channel_id=1, source_target_pairs={{0,3},{1,2},{2,1},{3,0},{4,7},{5,6},{6,5},{7,4},{8,11},{9,10},{10,... | collective-permute-start | bytes 3538952 | tf_op jit(solution)/shard_map/ppermute | solution.py:773
  18.7 54.2 %collective-permute-start.5 = (bf16[256,896]{1,0:T(8,128)(2,1)S(1)}, bf16[256,896]{1,0:T(8,128)(2,1)}, u32[]{:S(2)}, u32[]{:S(2)}) collective-permute-start(bf16[256,896]{1,0:T(8,128)(2,1)S(1)} %get-tuple-element.133), channel_id=1, source_target_pairs={{0,3},{1,2},{2,1},{3,0},{4,7},{5,6},{6,5},{7,4},{8,11},{9,10},{10,... | collective-permute-start | bytes 1376264 | tf_op jit(solution)/shard_map/ppermute | solution.py:773
  21.6 61.3 %collective-permute-start.4 = (bf16[256,896]{1,0:T(8,128)(2,1)}, bf16[256,896]{1,0:T(8,128)(2,1)}, u32[]{:S(2)}, u32[]{:S(2)}) collective-permute-start(bf16[256,896]{1,0:T(8,128)(2,1)} %get-tuple-element.134), channel_id=1, source_target_pairs={{0,2},{1,3},{2,0},{3,1},{4,6},{5,7},{6,4},{7,5},{8,10},{9,11},{10,... | collective-permute-start | bytes 1376264 | tf_op jit(solution)/shard_map/ppermute | solution.py:773
  85.6 127.0 %all-gather.5.cloned.1.call-start = ((), (), s32[]{:S(2)}) async-start(), calls=%async_computation.21 | async-start | bytes 9437184 | tf_op jit(solution)/shard_map/all_gather | solution.py:970
  89.9 32.1 %all-to-all-start.1 = ((s32[16,1,288]{2,1,0:T(1,128)}), s32[16,1,288]{2,1,0:T(1,128)S(1)}, u32[]{:S(2)}, u32[]{:S(2)}) async-start(s32[16,1,288]{2,1,0:T(1,128)} %copy.112), calls=%async_computation.1 | async-start | bytes 49152 | tf_op jit(solution)/shard_map/all_to_all | solution.py:805
  105.4 77.8 %collective-permute-start.6 = (bf16[128,4096]{1,0:T(8,128)(2,1)}, bf16[128,4096]{1,0:T(8,128)(2,1)S(1)}, u32[]{:S(2)}, u32[]{:S(2)}) collective-permute-start(bf16[128,4096]{1,0:T(8,128)(2,1)} %run_after.19.refs_0_), channel_id=1, source_target_pairs={{0,1},{1,0},{2,3},{3,2},{4,5},{5,4},{6,7},{7,6},{8,9},{9,8},{10,11... | collective-permute-start | bytes 3145736 | tf_op jit(solution)/shard_map/ppermute | solution.py:773
  107.4 75.8 %collective-permute-start.7 = (bf16[128,4096]{1,0:T(8,128)(2,1)}, bf16[128,4096]{1,0:T(8,128)(2,1)}, u32[]{:S(2)}, u32[]{:S(2)}) collective-permute-start(bf16[128,4096]{1,0:T(8,128)(2,1)} %run_after.19.refs_0_), channel_id=1, source_target_pairs={{0,2},{1,3},{2,0},{3,1},{4,6},{5,7},{6,4},{7,5},{8,10},{9,11},{10,... | collective-permute-start | bytes 3145736 | tf_op jit(solution)/shard_map/ppermute | solution.py:773
  108.9 74.4 %collective-permute-start.8 = (bf16[128,4096]{1,0:T(8,128)(2,1)}, bf16[128,4096]{1,0:T(8,128)(2,1)}, u32[]{:S(2)}, u32[]{:S(2)}) collective-permute-start(bf16[128,4096]{1,0:T(8,128)(2,1)} %run_after.19.refs_0_), channel_id=1, source_target_pairs={{0,3},{1,2},{2,1},{3,0},{4,7},{5,6},{6,5},{7,4},{8,11},{9,10},{10,... | collective-permute-start | bytes 3145736 | tf_op jit(solution)/shard_map/ppermute | solution.py:773
  122.0 25.8 %all-to-all-start.2 = ((s32[4,4,576]{2,1,0:T(4,128)}), s32[4,4,576]{2,1,0:T(4,128)S(1)}, u32[]{:S(2)}, u32[]{:S(2)}) async-start(s32[4,4,576]{2,1,0:T(4,128)} %reshape.356), calls=%async_computation.2 | async-start | bytes 81920 | tf_op jit(solution)/shard_map/all_to_all | solution.py:805
  147.9 33.5 %all-to-all-start = ((bf16[4,576,256]{2,1,0:T(8,128)(2,1)}), bf16[4,576,256]{2,1,0:T(8,128)(2,1)S(1)}, u32[]{:S(2)}, u32[]{:S(2)}) async-start(bf16[4,576,256]{2,1,0:T(8,128)(2,1)} %bitcast.237), calls=%async_computation | async-start | bytes 2359296 | tf_op jit(solution)/shard_map/all_to_all | solution.py:988
  154.2 32.9 %collective-permute-start.9 = (bf16[128,4096]{1,0:T(8,128)(2,1)S(1)}, bf16[128,4096]{1,0:T(8,128)(2,1)}, u32[]{:S(2)}, u32[]{:S(2)}) collective-permute-start(bf16[128,4096]{1,0:T(8,128)(2,1)S(1)} %copy-done.18), channel_id=1, source_target_pairs={{0,16},{16,0},{1,17},{17,1},{2,18},{18,2},{3,19},{19,3},{4,20},{20... | collective-permute-start | bytes 3145736 | tf_op jit(solution)/shard_map/ppermute | solution.py:788
  227.0 28.9 %collective-permute-start.13 = (bf16[576,1024]{1,0:T(8,128)(2,1)S(1)}, bf16[576,1024]{1,0:T(8,128)(2,1)}, u32[]{:S(2)}, u32[]{:S(2)}) collective-permute-start(bf16[576,1024]{1,0:T(8,128)(2,1)S(1)} %add_convert_fusion.5.refs_1_), channel_id=1, source_target_pairs={{0,4},{4,8},{8,12},{1,5},{5,9},{9,13},{2,6},{6,10},{10,14},{3,7},{... | collective-permute-start | bytes 3538952 | tf_op jit(solution)/shard_map/ppermute | solution.py:1016
  231.4 29.7 %collective-permute-start.14 = (bf16[576,1024]{1,0:T(8,128)(2,1)S(1)}, bf16[576,1024]{1,0:T(8,128)(2,1)}, u32[]{:S(2)}, u32[]{:S(2)}) collective-permute-start(bf16[576,1024]{1,0:T(8,128)(2,1)S(1)} %add_convert_fusion.5.refs_1_), channel_id=1, source_target_pairs={{4,0},{8,4},{12,8},{5,1},{9,5},{13,9},{6,2},{10,6},{14,10},{7,3},{... | collective-permute-start | bytes 3538952 | tf_op jit(solution)/shard_map/ppermute | solution.py:1019
  237.9 31.6 %all-to-all-start.3 = ((bf16[4,288,1024]{2,1,0:T(8,128)(2,1)}), bf16[4,288,1024]{2,1,0:T(8,128)(2,1)S(1)}, u32[]{:S(2)}, u32[]{:S(2)}) async-start(bf16[4,288,1024]{2,1,0:T(8,128)(2,1)} %pack_rows.4.refs_1_.refs_2_), calls=%async_computation.3 | async-start | bytes 4718592 | tf_op jit(solution)/shard_map/all_to_all | solution.py:805
  261.9 30.5 %collective-permute-start.16 = (bf16[576,1024]{1,0:T(8,128)(2,1)}, bf16[576,1024]{1,0:T(8,128)(2,1)}, u32[]{:S(2)}, u32[]{:S(2)}) collective-permute-start(bf16[576,1024]{1,0:T(8,128)(2,1)} %get-tuple-element.58.refs_1_.refs_2_), channel_id=1, source_target_pairs={{4,0},{8,4},{5,1},{9,5},{6,2},{10,6},{7,3},{11,7},{20,16},{24,20},... | collective-permute-start | bytes 3538952 | tf_op jit(solution)/shard_map/ppermute | solution.py:1019
  269.5 31.7 %all-to-all-start.4 = ((bf16[4,288,1024]{2,1,0:T(8,128)(2,1)}), bf16[4,288,1024]{2,1,0:T(8,128)(2,1)}, u32[]{:S(2)}, u32[]{:S(2)}) async-start(bf16[4,288,1024]{2,1,0:T(8,128)(2,1)} %pack_rows.5), calls=%async_computation.4 | async-start | bytes 4718592 | tf_op jit(solution)/shard_map/all_to_all | solution.py:805
  292.4 28.0 %collective-permute-start.17 = (bf16[576,1024]{1,0:T(8,128)(2,1)}, bf16[576,1024]{1,0:T(8,128)(2,1)S(1)}, u32[]{:S(2)}, u32[]{:S(2)}) collective-permute-start(bf16[576,1024]{1,0:T(8,128)(2,1)} %get-tuple-element.62.refs_1_.refs_2_), channel_id=1, source_target_pairs={{4,0},{5,1},{6,2},{7,3},{20,16},{21,17},{22,18},{23,19}} | collective-permute-start | bytes 3538952 | tf_op jit(solution)/shard_map/ppermute | solution.py:1019
  293.7 26.8 %collective-permute-start.18 = (bf16[576,1024]{1,0:T(8,128)(2,1)}, bf16[576,1024]{1,0:T(8,128)(2,1)}, u32[]{:S(2)}, u32[]{:S(2)}) collective-permute-start(bf16[576,1024]{1,0:T(8,128)(2,1)} %get-tuple-element.63.refs_4_.refs_3_), channel_id=1, source_target_pairs={{8,12},{9,13},{10,14},{11,15},{24,28},{25,29},{26,30},{27,31}} | collective-permute-start | bytes 3538952 | tf_op jit(solution)/shard_map/ppermute | solution.py:1016
  301.2 30.7 %all-to-all-start.5 = ((bf16[4,288,1024]{2,1,0:T(8,128)(2,1)}), bf16[4,288,1024]{2,1,0:T(8,128)(2,1)S(1)}, u32[]{:S(2)}, u32[]{:S(2)}) async-start(bf16[4,288,1024]{2,1,0:T(8,128)(2,1)} %pack_rows.6), calls=%async_computation.5 | async-start | bytes 4718592 | tf_op jit(solution)/shard_map/all_to_all | solution.py:805
  332.0 39.8 %all-to-all-start.6 = ((bf16[4,288,1024]{2,1,0:T(8,128)(2,1)}), bf16[4,288,1024]{2,1,0:T(8,128)(2,1)}, u32[]{:S(2)}, u32[]{:S(2)}) async-start(bf16[4,288,1024]{2,1,0:T(8,128)(2,1)} %pack_rows.7), calls=%async_computation.6 | async-start | bytes 4718592 | tf_op jit(solution)/shard_map/all_to_all | solution.py:805
  436.8 27.9 %all-to-all-start.10 = ((bf16[4,288,1024]{2,1,0:T(8,128)(2,1)}), bf16[4,288,1024]{2,1,0:T(8,128)(2,1)S(1)}, u32[]{:S(2)}, u32[]{:S(2)}) async-start(bf16[4,288,1024]{2,1,0:T(8,128)(2,1)} %bitcast.228), calls=%async_computation.10 | async-start | bytes 4718592 | tf_op jit(solution)/shard_map/all_to_all | solution.py:805
  466.2 31.7 %all-to-all-start.9 = ((bf16[4,288,1024]{2,1,0:T(8,128)(2,1)}), bf16[4,288,1024]{2,1,0:T(8,128)(2,1)}, u32[]{:S(2)}, u32[]{:S(2)}) async-start(bf16[4,288,1024]{2,1,0:T(8,128)(2,1)} %bitcast.227), calls=%async_computation.9 | async-start | bytes 4718592 | tf_op jit(solution)/shard_map/all_to_all | solution.py:805
  475.9 27.4 %collective-permute-start.19 = (bf16[576,1024]{1,0:T(8,128)(2,1)}, bf16[576,1024]{1,0:T(8,128)(2,1)}, u32[]{:S(2)}, u32[]{:S(2)}) collective-permute-start(bf16[576,1024]{1,0:T(8,128)(2,1)} %unpack_rows.4.refs_7_), channel_id=1, source_target_pairs={{0,4},{1,5},{2,6},{3,7},{16,20},{17,21},{18,22},{19,23}} | collective-permute-start | bytes 3538952 | tf_op jit(solution)/shard_map/ppermute | solution.py:767
  479.7 23.7 %collective-permute-start.20 = (bf16[576,1024]{1,0:T(8,128)(2,1)}, bf16[576,1024]{1,0:T(8,128)(2,1)}, u32[]{:S(2)}, u32[]{:S(2)}) collective-permute-start(bf16[576,1024]{1,0:T(8,128)(2,1)} %unpack_rows.4.refs_7_), channel_id=1, source_target_pairs={{12,8},{13,9},{14,10},{15,11},{28,24},{29,25},{30,26},{31,27}} | collective-permute-start | bytes 3538952 | tf_op jit(solution)/shard_map/ppermute | solution.py:768
  497.9 32.7 %all-to-all-start.12 = ((bf16[4,288,1024]{2,1,0:T(8,128)(2,1)}), bf16[4,288,1024]{2,1,0:T(8,128)(2,1)S(1)}, u32[]{:S(2)}, u32[]{:S(2)}) async-start(bf16[4,288,1024]{2,1,0:T(8,128)(2,1)} %bitcast.231), calls=%async_computation.12 | async-start | bytes 4718592 | tf_op jit(solution)/shard_map/all_to_all | solution.py:805
  513.1 28.1 %collective-permute-start.21 = (bf16[576,1024]{1,0:T(8,128)(2,1)}, bf16[576,1024]{1,0:T(8,128)(2,1)}, u32[]{:S(2)}, u32[]{:S(2)}) collective-permute-start(bf16[576,1024]{1,0:T(8,128)(2,1)} %get-tuple-element.109), channel_id=1, source_target_pairs={{0,4},{4,8},{1,5},{5,9},{2,6},{6,10},{3,7},{7,11},{16,20},{20,24},... | collective-permute-start | bytes 3538952 | tf_op jit(solution)/shard_map/ppermute | solution.py:767
  518.6 22.7 %collective-permute-start.22 = (bf16[576,1024]{1,0:T(8,128)(2,1)}, bf16[576,1024]{1,0:T(8,128)(2,1)}, u32[]{:S(2)}, u32[]{:S(2)}) collective-permute-start(bf16[576,1024]{1,0:T(8,128)(2,1)} %get-tuple-element.110), channel_id=1, source_target_pairs={{8,4},{12,8},{9,5},{13,9},{10,6},{14,10},{11,7},{15,11},{24,20},{2... | collective-permute-start | bytes 3538952 | tf_op jit(solution)/shard_map/ppermute | solution.py:768
  532.0 30.5 %all-to-all-start.11 = ((bf16[4,288,1024]{2,1,0:T(8,128)(2,1)}), bf16[4,288,1024]{2,1,0:T(8,128)(2,1)}, u32[]{:S(2)}, u32[]{:S(2)}) async-start(bf16[4,288,1024]{2,1,0:T(8,128)(2,1)} %bitcast.230), calls=%async_computation.11 | async-start | bytes 4718592 | tf_op jit(solution)/shard_map/all_to_all | solution.py:805
  536.5 146.6 %reduce-scatter.10.cloned.1.call-start = ((), (), s32[]{:S(2)}) async-start(), calls=%async_computation.23 | async-start | bytes 5242880
  551.0 31.1 %collective-permute-start.23 = (bf16[576,1024]{1,0:T(8,128)(2,1)}, bf16[576,1024]{1,0:T(8,128)(2,1)}, u32[]{:S(2)}, u32[]{:S(2)}) collective-permute-start(bf16[576,1024]{1,0:T(8,128)(2,1)} %get-tuple-element.107), channel_id=1, source_target_pairs={{0,4},{4,8},{8,12},{1,5},{5,9},{9,13},{2,6},{6,10},{10,14},{3,7},{... | collective-permute-start | bytes 3538952 | tf_op jit(solution)/shard_map/ppermute | solution.py:767
  560.6 26.7 %collective-permute-start.24 = (bf16[576,1024]{1,0:T(8,128)(2,1)}, bf16[576,1024]{1,0:T(8,128)(2,1)}, u32[]{:S(2)}, u32[]{:S(2)}) collective-permute-start(bf16[576,1024]{1,0:T(8,128)(2,1)} %get-tuple-element.108), channel_id=1, source_target_pairs={{4,0},{8,4},{12,8},{5,1},{9,5},{13,9},{6,2},{10,6},{14,10},{7,3},{... | collective-permute-start | bytes 3538952 | tf_op jit(solution)/shard_map/ppermute | solution.py:768
  689.0 77.9 %reduce-scatter.12.cloned.1.call-start = ((), (), s32[]{:S(2)}) async-start(), calls=%async_computation.24 | async-start | bytes 6553600
  705.4 33.4 %all-to-all-start.14 = ((bf16[4,128,1024]{2,1,0:T(8,128)(2,1)}), bf16[4,128,1024]{2,1,0:T(8,128)(2,1)S(1)}, u32[]{:S(2)}, u32[]{:S(2)}) async-start(bf16[4,128,1024]{2,1,0:T(8,128)(2,1)} %bitcast.221), calls=%async_computation.14 | async-start | bytes 2097152 | tf_op jit(solution)/shard_map/all_to_all | solution.py:805
  767.0 36.2 %all-to-all-start.15 = ((bf16[4,32,5120]{2,1,0:T(8,128)(2,1)}), bf16[4,32,5120]{2,1,0:T(8,128)(2,1)}, u32[]{:S(2)}, u32[]{:S(2)}) async-start(bf16[4,32,5120]{2,1,0:T(8,128)(2,1)} %bitcast.236), calls=%async_computation.16 | async-start | bytes 2621440 | tf_op jit(solution)/shard_map/all_to_all | solution.py:805
  771.7 122.7 %reduce-scatter.8.cloned.1.call-start = ((), (), s32[]{:S(2)}) async-start(), calls=%async_computation.22 | async-start | bytes 5898240 | tf_op jit(solution)/shard_map/reduce_scatter | solution.py:1147
  805.3 25.0 %collective-permute-start.32 = (bf16[32,5120]{1,0:T(8,128)(2,1)}, bf16[32,5120]{1,0:T(8,128)(2,1)}, u32[]{:S(2)}, u32[]{:S(2)}) collective-permute-start(bf16[32,5120]{1,0:T(8,128)(2,1)} %fusion.61.refs_1_), channel_id=1, source_target_pairs={{0,8},{4,12},{8,0},{12,4},{1,9},{5,13},{9,1},{13,5},{2,10},{6,14},... | collective-permute-start | bytes 983048 | tf_op jit(solution)/shard_map/ppermute | solution.py:837
  807.4 22.9 %collective-permute-start.33 = (bf16[32,5120]{1,0:T(8,128)(2,1)}, bf16[32,5120]{1,0:T(8,128)(2,1)}, u32[]{:S(2)}, u32[]{:S(2)}) collective-permute-start(bf16[32,5120]{1,0:T(8,128)(2,1)} %fusion.61.refs_1_), channel_id=1, source_target_pairs={{0,12},{4,0},{8,4},{12,8},{1,13},{5,1},{9,5},{13,9},{2,14},{6,2},{... | collective-permute-start | bytes 983048 | tf_op jit(solution)/shard_map/ppermute | solution.py:837
  815.2 28.5 %collective-permute-start.28 = (bf16[128,896]{1,0:T(8,128)(2,1)}, bf16[128,896]{1,0:T(8,128)(2,1)}, u32[]{:S(2)}, u32[]{:S(2)}) collective-permute-start(bf16[128,896]{1,0:T(8,128)(2,1)} %get-tuple-element.130), channel_id=1, source_target_pairs={{0,1},{1,0},{2,3},{3,2},{4,5},{5,4},{6,7},{7,6},{8,9},{9,8},{10,11... | collective-permute-start | bytes 688136 | tf_op jit(solution)/shard_map/ppermute | solution.py:773
  816.5 27.2 %collective-permute-start.29 = (bf16[128,896]{1,0:T(8,128)(2,1)}, bf16[128,896]{1,0:T(8,128)(2,1)}, u32[]{:S(2)}, u32[]{:S(2)}) collective-permute-start(bf16[128,896]{1,0:T(8,128)(2,1)} %get-tuple-element.129), channel_id=1, source_target_pairs={{0,2},{1,3},{2,0},{3,1},{4,6},{5,7},{6,4},{7,5},{8,10},{9,11},{10,... | collective-permute-start | bytes 688136 | tf_op jit(solution)/shard_map/ppermute | solution.py:773
  818.1 28.0 %collective-permute-start.30 = (bf16[128,896]{1,0:T(8,128)(2,1)}, bf16[128,896]{1,0:T(8,128)(2,1)}, u32[]{:S(2)}, u32[]{:S(2)}) collective-permute-start(bf16[128,896]{1,0:T(8,128)(2,1)} %get-tuple-element.128), channel_id=1, source_target_pairs={{0,3},{1,2},{2,1},{3,0},{4,7},{5,6},{6,5},{7,4},{8,11},{9,10},{10,... | collective-permute-start | bytes 688136 | tf_op jit(solution)/shard_map/ppermute | solution.py:773
  835.8 37.7 %collective-permute-start.38 = (bf16[4,32,5120]{2,1,0:T(8,128)(2,1)}, bf16[4,32,5120]{2,1,0:T(8,128)(2,1)}, u32[]{:S(2)}, u32[]{:S(2)}) collective-permute-start(bf16[4,32,5120]{2,1,0:T(8,128)(2,1)} %gather_fusion.5), channel_id=1, source_target_pairs={{0,16},{16,0},{1,17},{17,1},{2,18},{18,2},{3,19},{19,3},{4,20},{20... | collective-permute-start | bytes 3932168 | tf_op jit(solution)/shard_map/ppermute | solution.py:788
  837.1 32.1 %collective-permute-start.39 = (bf16[128,1024]{1,0:T(8,128)(2,1)}, bf16[128,1024]{1,0:T(8,128)(2,1)}, u32[]{:S(2)}, u32[]{:S(2)}) collective-permute-start(bf16[128,1024]{1,0:T(8,128)(2,1)} %run_after.33), channel_id=1, source_target_pairs={{0,4},{4,8},{8,12},{12,0},{1,5},{5,9},{9,13},{13,1},{2,6},{6,10},{... | collective-permute-start | bytes 786440 | tf_op jit(solution)/shard_map/ppermute | solution.py:837
  843.7 25.5 %collective-permute-start.40 = (bf16[128,1024]{1,0:T(8,128)(2,1)}, bf16[128,1024]{1,0:T(8,128)(2,1)}, u32[]{:S(2)}, u32[]{:S(2)}) collective-permute-start(bf16[128,1024]{1,0:T(8,128)(2,1)} %run_after.33), channel_id=1, source_target_pairs={{0,8},{4,12},{8,0},{12,4},{1,9},{5,13},{9,1},{13,5},{2,10},{6,14},... | collective-permute-start | bytes 786440 | tf_op jit(solution)/shard_map/ppermute | solution.py:837
  843.7 25.6 %collective-permute-start.41 = (bf16[128,1024]{1,0:T(8,128)(2,1)}, bf16[128,1024]{1,0:T(8,128)(2,1)}, u32[]{:S(2)}, u32[]{:S(2)}) collective-permute-start(bf16[128,1024]{1,0:T(8,128)(2,1)} %run_after.33), channel_id=1, source_target_pairs={{0,12},{4,0},{8,4},{12,8},{1,13},{5,1},{9,5},{13,9},{2,14},{6,2},{... | collective-permute-start | bytes 786440 | tf_op jit(solution)/shard_map/ppermute | solution.py:837
  865.4 25.0 %all-to-all-start.16 = ((bf16[4,32,3200]{2,1,0:T(8,128)(2,1)}), bf16[4,32,3200]{2,1,0:T(8,128)(2,1)S(1)}, u32[]{:S(2)}, u32[]{:S(2)}) async-start(bf16[4,32,3200]{2,1,0:T(8,128)(2,1)} %bitcast.234), calls=%async_computation.17 | async-start | bytes 1638400 | tf_op jit(solution)/shard_map/all_to_all | solution.py:805
  (96 other events, 911.7 us)
Sparse Core Ops, SparseCore 0:
  85.8 33.1 all-gather.2
  121.4 85.6 all-gather.4
  632.5 50.6 reduce-scatter.9
  705.5 61.4 reduce-scatter.11
  778.1 65.0 reduce-scatter.7
